TPU v7x, 32 devices: a whole 2x2x4 slice. The times are simulated.
32 devices in a mesh: seq: 8 (over z, x), head: 4 (over y, core).
Axes of the slice: x: 2, y: 2, z: 4, core: 2. Of those that a mesh axis runs over, the one named last changes fastest.
Arguments:
- inputs: bfloat16 [6, 2, 1024, 768], P(None, None, 'seq', 'head'), may hold values from -15 to 15
- doc_lengths: int32 [6, 8], replicated, may hold values from 0 to 1024, as said below
- attn_gain: float32 [768], P('head'), may hold values from 0.5 to 1.5
- attn_bias: float32 [768], P('head'), may hold values from -2 to 2
- w_qkv: bfloat16 [768, 3, 768], P(None, None, 'head'), may hold values from -0.21875 to 0.21875
- w_out: bfloat16 [768, 768], P('head'), may hold values from -1.75 to 1.75
- ffn_gain: float32 [768], P('head'), may hold values from 0.5 to 1.5
- ffn_bias: float32 [768], P('head'), may hold values from -2 to 2
- w_up: bfloat16 [768, 3072], P(None, 'head'), may hold values from -0.21875 to 0.21875
- w_down: bfloat16 [3072, 768], P('head'), may hold values from -0.109375 to 0.109375
- cotangent: bfloat16 [6, 2, 1024, 768], P(None, None, 'seq', 'head'), may hold values from -6 to 6
Outputs:
- outputs: bfloat16 [6, 2, 1024, 768], P(None, None, 'seq', 'head')
- input_grad: float32 [6, 2, 1024, 768], P(None, None, 'seq', 'head')
- qkv_grad: float32 [768, 3, 768], P(None, None, 'head')
- out_grad: float32 [768, 768], P('head')
- up_grad: float32 [768, 3072], P(None, 'head')
- down_grad: float32 [3072, 768], P('head')
- attn_gain_grad: float32 [768], P('head')
- attn_bias_grad: float32 [768], P('head')
- ffn_gain_grad: float32 [768], P('head')
- ffn_bias_grad: float32 [768], P('head')
Inputs may be any that keep to these rules, and one draw needn't show every extreme that they name: `doc_lengths`: each row sums to at most 1024. In one row, which one varies, the first entry is 1024 and the others are 0; in the other rows every entry is at least 64 and at most 128.
All inputs are finite; a program needn't handle non-finite values.
Results may differ from a plain program's by a relative error of at most 0.013.
Values may be sent and summed in bfloat16 or wider, within the bound.
A program may use at most 512 MiB of HBM per device.

v0:
```python
import jax
import jax.numpy as jnp
from jax import lax
from jax.sharding import PartitionSpec as P

D = 768
HEAD_DIM = 64
BLOCK = 16


norm_eps = 1e-05
masked_score = -1e30
rotary_base = 10000.0


def passed_along(block, axis, distance):
    devices = range(lax.axis_size(axis))
    route = [(i - distance, i) for i in devices if i - distance in devices]
    return lax.ppermute(block, axis, route)


def from_behind(x, axis, by):
    devices = lax.axis_size(axis)
    return lax.ppermute(x, axis, [(i, (i + by) % devices) for i in range(devices)])


def segment_ids(doc_lengths, positions):
    doc_ends = jnp.cumsum(doc_lengths, axis=1)
    return jnp.sum((doc_ends[:, :, None] <= positions[None, None, :]).astype(jnp.int32), axis=1)


def rotate(values, positions, sign):
    half_dim = values.shape[-1] // 2
    freqs = rotary_base ** (-jnp.arange(half_dim, dtype=jnp.float32) / half_dim)
    angles = positions.astype(jnp.float32)[:, None, None] * freqs
    cosine = jnp.cos(angles)
    sine = sign * jnp.sin(angles)
    first_half = values[..., :half_dim]
    second_half = values[..., half_dim:]
    return jnp.concatenate(
        [first_half * cosine - second_half * sine, second_half * cosine + first_half * sine],
        axis=-1,
    )


def row_pair(first_sum, second_sum):
    return lax.psum((first_sum, second_sum), "head")


def normalize(share, gain, bias):
    row_total, row_square = row_pair(jnp.sum(share, axis=-1), jnp.sum(share * share, axis=-1))
    mean_value = row_total / D
    inv_std = lax.rsqrt(row_square / D - mean_value * mean_value + norm_eps)
    centered = (share - mean_value[..., None]) * inv_std[..., None]
    scaled = (centered * gain + bias).astype(jnp.bfloat16)
    gathered = lax.all_gather(scaled, "head", axis=3, tiled=True)
    return (gathered, centered, inv_std)


def norm_backward(partial_value, gain, centered, inv_std):
    share = lax.psum_scatter(partial_value, "head", scatter_dimension=3, tiled=True)
    scaled = share * gain
    first_mean, second_mean = row_pair(
        jnp.sum(scaled, axis=-1), jnp.sum(scaled * centered, axis=-1)
    )
    grad_in = inv_std[..., None] * (
        scaled - first_mean[..., None] / D - centered * (second_mean[..., None] / D)
    )
    gain_grad = jnp.sum(share * centered, axis=(0, 1, 2))
    bias_grad = jnp.sum(share, axis=(0, 1, 2))
    return (grad_in, gain_grad, bias_grad)


def branch_total(partial_value):
    return lax.psum_scatter(partial_value, "head", scatter_dimension=3, tiled=True)


def gradient_rows(share):
    return lax.all_gather(share, "head", axis=3, tiled=True)


def mask_rule(query_pos, query_seg, key_pos, key_seg):
    query_block = (query_pos // BLOCK)[:, None]
    key_block = (key_pos // BLOCK)[None, :]
    order = jnp.stack([key_block < query_block, key_block <= query_block])
    same_doc = query_seg[:, :, None] == key_seg[:, None, :]
    return jnp.logical_and(order[None, :, None], same_doc[:, None, None])


def absorb(state_now, scores, allowed, value_piece):
    run_max, run_sum, run_acc = state_now
    masked = jnp.where(allowed, scores, masked_score)
    new_max = jnp.maximum(run_max, jnp.max(masked, axis=-1))
    weights_now = jnp.where(allowed, jnp.exp(masked - new_max[..., None]), 0.0)
    factor = jnp.exp(run_max - new_max)
    new_sum = run_sum * factor + jnp.sum(weights_now, axis=-1)
    added = jnp.einsum(
        "schlk,skhd->schld",
        weights_now,
        value_piece.astype(jnp.float32),
        precision=lax.Precision.HIGHEST,
    )
    return (new_max, new_sum, run_acc * factor[..., None] + added)


def body(
    inputs,
    doc_lengths,
    attn_gain,
    attn_bias,
    w_qkv,
    w_out,
    ffn_gain,
    ffn_bias,
    w_up,
    w_down,
    cotangent,
):
    seqs_here, _, local_len, _ = inputs.shape
    head_local = w_qkv.shape[2] // HEAD_DIM
    first_pos = lax.axis_index("seq") * local_len
    positions = first_pos + jnp.arange(local_len, dtype=jnp.int32)
    segments = segment_ids(doc_lengths, positions)
    inputs_wide = inputs.astype(jnp.float32)
    normed_one, centered_one, inv_one = normalize(inputs_wide, attn_gain, attn_bias)
    projected = jnp.einsum("scld,dtk->scltk", normed_one, w_qkv, preferred_element_type=jnp.float32)
    split_rows = projected.reshape(seqs_here, 2, local_len, 3, head_local, HEAD_DIM)
    queries = (rotate(split_rows[:, :, :, 0], positions, 1.0) * HEAD_DIM ** (-0.5)).astype(
        jnp.bfloat16
    )
    key_rows = rotate(split_rows[:, :, :, 1], positions, 1.0).astype(jnp.bfloat16)
    value_rows = split_rows[:, :, :, 2].astype(jnp.bfloat16)
    clean_keys = key_rows[:, 1].reshape(seqs_here, local_len, head_local * HEAD_DIM)
    clean_values = value_rows[:, 1].reshape(seqs_here, local_len, head_local * HEAD_DIM)
    block_ids = positions // BLOCK
    own_allowed = jnp.logical_and(
        (block_ids[:, None] == block_ids[None, :])[None],
        segments[:, :, None] == segments[:, None, :],
    )[:, None, None]
    noisy_scores = jnp.einsum(
        "sclhd,skhd->schlk", queries[:, :1], key_rows[:, 0], preferred_element_type=jnp.float32
    )
    half_shape = (seqs_here, 1, head_local, local_len)
    empty_state = (
        jnp.full(half_shape, masked_score, jnp.float32),
        jnp.zeros(half_shape, jnp.float32),
        jnp.zeros(half_shape + (HEAD_DIM,), jnp.float32),
    )
    noisy_state = absorb(empty_state, noisy_scores, own_allowed, value_rows[:, 0])
    start_state = jax.tree.map(
        lambda first, second: jnp.concatenate([first, second], axis=1), noisy_state, empty_state
    )
    piece_keys = lax.all_gather(clean_keys, "seq", axis=1, tiled=True)
    piece_values = lax.all_gather(clean_values, "seq", axis=1, tiled=True)
    piece_len = piece_keys.shape[1]
    key_pos = jnp.arange(piece_len, dtype=jnp.int32)
    key_seg = segment_ids(doc_lengths, key_pos)
    key_heads = piece_keys.reshape(seqs_here, piece_len, head_local, HEAD_DIM)
    value_heads = piece_values.reshape(seqs_here, piece_len, head_local, HEAD_DIM)
    scores = jnp.einsum("sclhd,skhd->schlk", queries, key_heads, preferred_element_type=jnp.float32)
    final_max, final_sum, final_acc = absorb(
        start_state, scores, mask_rule(positions, segments, key_pos, key_seg), value_heads
    )
    attended = final_acc / final_sum[..., None]
    log_total = final_max + jnp.log(final_sum)
    attended_low = attended.astype(jnp.bfloat16)
    out_heads = w_out.reshape(head_local, HEAD_DIM, w_out.shape[1])
    attn_share = branch_total(
        jnp.einsum("schld,hdm->sclm", attended_low, out_heads, preferred_element_type=jnp.float32)
    )
    hidden_res = inputs_wide + attn_share
    normed_two, centered_two, inv_two = normalize(hidden_res, ffn_gain, ffn_bias)
    up_value = jnp.einsum("scld,df->sclf", normed_two, w_up, preferred_element_type=jnp.float32)
    activated, gelu_back = jax.vjp(lambda inner: jax.nn.gelu(inner, approximate=True), up_value)
    act_low = activated.astype(jnp.bfloat16)
    ffn_share = branch_total(
        jnp.einsum("sclf,fm->sclm", act_low, w_down, preferred_element_type=jnp.float32)
    )
    outputs = (hidden_res + ffn_share).astype(jnp.bfloat16)
    grad_out = cotangent.astype(jnp.float32)
    grad_full = gradient_rows(cotangent)
    down_grad = jnp.einsum("sclf,sclm->fm", act_low, grad_full, preferred_element_type=jnp.float32)
    act_grad = jnp.einsum("sclm,fm->sclf", grad_full, w_down, preferred_element_type=jnp.float32)
    up_pre_grad = gelu_back(act_grad)[0].astype(jnp.bfloat16)
    up_grad = jnp.einsum(
        "scld,sclf->df", normed_two, up_pre_grad, preferred_element_type=jnp.float32
    )
    normed_two_grad = jnp.einsum(
        "sclf,df->scld", up_pre_grad, w_up, preferred_element_type=jnp.float32
    )
    back_two, ffn_gain_grad, ffn_bias_grad = norm_backward(
        normed_two_grad, ffn_gain, centered_two, inv_two
    )
    resid_grad = grad_out + back_two
    resid_full = gradient_rows(resid_grad.astype(jnp.bfloat16))
    out_grad = jnp.einsum(
        "schld,sclm->hdm", attended_low, resid_full, preferred_element_type=jnp.float32
    ).reshape(w_out.shape)
    attended_grad = jnp.einsum(
        "sclm,hdm->schld", resid_full, out_heads, preferred_element_type=jnp.float32
    ).astype(jnp.bfloat16)
    grad_wide = attended_grad.astype(jnp.float32)
    row_delta = jnp.sum(grad_wide * attended, axis=-1)
    noisy_probs = jnp.where(own_allowed, jnp.exp(noisy_scores - log_total[:, :1, :, :, None]), 0.0)
    noisy_prob_grad = jnp.einsum(
        "schld,skhd->schlk",
        attended_grad[:, :1],
        value_rows[:, 0],
        preferred_element_type=jnp.float32,
    )
    noisy_score_grad = (noisy_probs * (noisy_prob_grad - row_delta[:, :1, :, :, None])).astype(
        jnp.bfloat16
    )
    noisy_query_grad = jnp.einsum(
        "schlk,skhd->schld", noisy_score_grad, key_rows[:, 0], preferred_element_type=jnp.float32
    )
    noisy_key_grad = jnp.einsum(
        "schlk,sclhd->skhd", noisy_score_grad, queries[:, :1], preferred_element_type=jnp.float32
    )
    noisy_value_grad = jnp.einsum(
        "schlk,schld->skhd", noisy_probs, grad_wide[:, :1], precision=lax.Precision.HIGHEST
    )
    query_start = jnp.concatenate([noisy_query_grad, jnp.zeros_like(noisy_query_grad)], axis=1)
    flat_zero = jnp.zeros((seqs_here, local_len, head_local * HEAD_DIM), jnp.float32)

    def piece_grads(piece_keys, piece_values, first_row, query_total):
        key_pos = first_row + jnp.arange(local_len, dtype=jnp.int32)
        key_seg = segment_ids(doc_lengths, key_pos)
        key_heads = piece_keys.reshape(seqs_here, local_len, head_local, HEAD_DIM)
        value_heads = piece_values.reshape(seqs_here, local_len, head_local, HEAD_DIM)
        scores = jnp.einsum(
            "sclhd,skhd->schlk", queries, key_heads, preferred_element_type=jnp.float32
        )
        allowed = mask_rule(positions, segments, key_pos, key_seg)
        weights_now = jnp.where(allowed, jnp.exp(scores - log_total[..., None]), 0.0)
        prob_grad = jnp.einsum(
            "schld,skhd->schlk", attended_grad, value_heads, preferred_element_type=jnp.float32
        )
        score_grad = (weights_now * (prob_grad - row_delta[..., None])).astype(jnp.bfloat16)
        query_out = query_total + jnp.einsum(
            "schlk,skhd->schld", score_grad, key_heads, preferred_element_type=jnp.float32
        )
        key_part = jnp.einsum(
            "schlk,sclhd->skhd", score_grad, queries, preferred_element_type=jnp.float32
        )
        value_part = jnp.einsum(
            "schlk,schld->skhd", weights_now, grad_wide, precision=lax.Precision.HIGHEST
        )
        return (key_part.reshape(flat_zero.shape), value_part.reshape(flat_zero.shape), query_out)

    def cycle_body(cycle_step, carried):
        piece_keys, piece_values, key_acc, value_acc, query_acc = carried
        source = (lax.axis_index("seq") - cycle_step) % lax.axis_size("seq")
        first_row = source * local_len
        key_part, value_part, query_acc = piece_grads(
            piece_keys, piece_values, first_row, query_acc
        )
        key_acc = key_acc + key_part
        value_acc = value_acc + value_part
        piece_keys, piece_values = passed_along((piece_keys, piece_values), "seq", 1)
        key_acc, value_acc = (
            from_behind(key_acc.astype(jnp.bfloat16), "seq", 1).astype(key_acc.dtype),
            from_behind(value_acc.astype(jnp.bfloat16), "seq", 1).astype(value_acc.dtype),
        )
        return (piece_keys, piece_values, key_acc, value_acc, query_acc)

    cycle_start = (clean_keys, clean_values, flat_zero, flat_zero, query_start)
    _, _, clean_key_grad, clean_value_grad, query_acc = lax.fori_loop(
        0, lax.axis_size("seq"), cycle_body, cycle_start
    )
    head_shape = (seqs_here, local_len, head_local, HEAD_DIM)
    query_total = rotate(jnp.transpose(query_acc, (0, 1, 3, 2, 4)), positions, -1.0) * HEAD_DIM ** (
        -0.5
    )
    key_total = rotate(
        jnp.stack([noisy_key_grad, clean_key_grad.reshape(head_shape)], axis=1), positions, -1.0
    )
    value_total = jnp.stack([noisy_value_grad, clean_value_grad.reshape(head_shape)], axis=1)
    qkv_pre_grad = (
        jnp.stack([query_total, key_total, value_total], axis=3)
        .reshape(seqs_here, 2, local_len, 3, head_local * HEAD_DIM)
        .astype(jnp.bfloat16)
    )
    qkv_grad = jnp.einsum(
        "scld,scltk->dtk", normed_one, qkv_pre_grad, preferred_element_type=jnp.float32
    )
    normed_one_grad = jnp.einsum(
        "scltk,dtk->scld", qkv_pre_grad, w_qkv, preferred_element_type=jnp.float32
    )
    back_one, attn_gain_grad, attn_bias_grad = norm_backward(
        normed_one_grad, attn_gain, centered_one, inv_one
    )
    input_grad = resid_grad + back_one
    (
        qkv_grad,
        out_grad,
        up_grad,
        down_grad,
        attn_gain_grad,
        attn_bias_grad,
        ffn_gain_grad,
        ffn_bias_grad,
    ) = lax.psum(
        (
            qkv_grad,
            out_grad,
            up_grad,
            down_grad,
            attn_gain_grad,
            attn_bias_grad,
            ffn_gain_grad,
            ffn_bias_grad,
        ),
        "seq",
    )
    return (
        outputs,
        input_grad,
        qkv_grad,
        out_grad,
        up_grad,
        down_grad,
        attn_gain_grad,
        attn_bias_grad,
        ffn_gain_grad,
        ffn_bias_grad,
    )


def solution(mesh):
    in_specs = (
        P(None, None, "seq", "head"),
        P(),
        P("head"),
        P("head"),
        P(None, None, "head"),
        P("head", None),
        P("head"),
        P("head"),
        P(None, "head"),
        P("head", None),
        P(None, None, "seq", "head"),
    )
    out_specs = (
        P(None, None, "seq", "head"),
        P(None, None, "seq", "head"),
        P(None, None, "head"),
        P("head", None),
        P(None, "head"),
        P("head", None),
        P("head"),
        P("head"),
        P("head"),
        P("head"),
    )
    return jax.shard_map(body, mesh=mesh, in_specs=in_specs, out_specs=out_specs, check_vma=False)
```

profile of v0, /device:TPU:0, one launch (start us, length us, event | category | flops | bytes accessed | tf_op | source)
XLA Modules:
  0.0 1016.8 jit_solution(15802060531693274674)
XLA Ops:
  8.6 12.6 %all-reduce.9 = (f32[6,2,128]{2,1,0:T(2,128)S(1)}, f32[6,2,128]{2,1,0:T(2,128)S(1)}) all-reduce(f32[6,2,128]{2,1,0:T(2,128)S(1)} %get-tuple-element.590, f32[6,2,128]{2,1,0:T(2,128)S(1)} %get-tuple-element.589), channel_id=1, replica_groups=mesh['seq'=8,'head'=4] {'head'}, use_global_device_ids=true, to_apply=%region_5.6 | all-reduce | flops 3072 | bytes 24576 | tf_op jit(solution)/shard_map/psum | solution.py:47
  25.0 23.7 %all-gather.7.cloned.1.call-done = bf16[6,2,128,768]{2,3,1,0:T(8,128)(2,1)} async-done(((bf16[6,2,128,192]{2,3,1,0:T(8,128)(2,1)}), bf16[6,2,128,768]{2,3,1,0:T(8,128)(2,1)}) %all-gather.7.cloned.1.call-update) | async-done | bytes 2359312 | tf_op jit(solution)/shard_map/all_gather | solution.py:56
  48.7 3.2 fusion.32
  69.2 41.5 %all-gather.9.cloned.1.call-done = bf16[6,1024,192]{1,2,0:T(8,128)(2,1)} async-done(((bf16[6,128,192]{1,2,0:T(8,128)(2,1)}), bf16[6,1024,192]{1,2,0:T(8,128)(2,1)}) %all-gather.9.cloned.1.call-update) | async-done | bytes 2359312 | tf_op jit(solution)/shard_map/all_gather | solution.py:153
  110.7 11.3 %fusion.22 = (f32[6,2,3,128]{3,1,2,0:T(2,128)S(1)}, f32[6,3,1024,2,128]{4,2,3,1,0:T(8,128)}) fusion(pred[6,2,128,1024]{2,3,1,0:T(8,128)(4,1)S(1)} %broadcast_and_fusion.1, bf16[6,1024,3,64,1]{1,3,4,2,0:T(8,128)(2,1)} %bitcast.320, bf16[6,2,128,3,64]{2,4,3,0,1:T(8,128)(2,1)S(1)} %fusion.89), kind=kOutput, calls=%fused_computation.42 | convolution fusion | flops 613412352 | bytes 23414784 | tf_op jit(solution)/shard_map/sclhd,skhd->schlk/dot_general | solution.py:160
  122.0 16.4 %fusion.135 = (f32[6,2,3,128]{3,1,2,0:T(2,128)S(1)}, f32[6,2,3,128,1024]{3,4,1,2,0:T(8,128)}) fusion(f32[6,2,3,128]{3,1,2,0:T(2,128)S(1)} %pad_maximum_fusion.3, f32[6,3,1024,2,128]{4,2,3,1,0:T(8,128)} %get-tuple-element.673, pred[6,2,128,1024]{2,3,1,0:T(8,128)(4,1)S(1)} %broadcast_and_fusion.1), kind=kLoop, calls=%fused_computation.226 | loop fusion | flops 18869760 | bytes 39358464 | tf_op jit(solution)/shard_map/reduce_sum | solution.py:96
  139.0 25.6 %all-gather.11.cloned.1.call-done = bf16[6,1024,192]{1,2,0:T(8,128)(2,1)} async-done(((bf16[6,128,192]{1,2,0:T(8,128)(2,1)}), bf16[6,1024,192]{1,2,0:T(8,128)(2,1)}) %all-gather.11.cloned.1.call-update) | async-done | bytes 2359312 | tf_op jit(solution)/shard_map/all_gather | solution.py:154
  164.7 12.6 %fusion.137 = (bf16[6,2,3,128,64]{3,4,2,0,1:T(8,128)(2,1)S(1)}, f32[6,2,3,128,64]{3,4,2,0,1:T(8,128)}) fusion(f32[6,2,3,128]{3,2,0,1:T(4,128)S(1)} %copy.100, bf16[6,1024,3,64,1]{1,3,2,0,4:T(8,128)(2,1)} %bitcast.324, f32[6,2,3,128,1024]{3,4,1,2,0:T(8,128)} %get-tuple-element.640, f32[6,2,3,128]{3,2,0,1:T(4,128)S(1)} %copy.98, ...), kind=kOutput, calls=%fused_computation.228 | convolution fusion | flops 3625058304 | bytes 23629824 | tf_op jit(solution)/shard_map/schlk,skhd->schld/dot_general | solution.py:97
  178.1 3.0 convolution_bitcast_fusion.2
  181.2 46.1 %reduce-scatter.5.cloned.1.call-done = f32[6,2,128,192]{2,3,1,0:T(8,128)} async-done(((f32[6,2,128,768]{2,3,1,0:T(8,128)}), f32[6,2,128,192]{2,3,1,0:T(8,128)}) %reduce-scatter.5.cloned.1.call-update) | async-done | bytes 1179664 | tf_op jit(solution)/shard_map/reduce_scatter | solution.py:75
  229.4 10.2 all-reduce.8
  242.7 24.7 %all-gather.13.cloned.1.call-done = bf16[6,2,128,768]{2,3,1,0:T(8,128)(2,1)} async-done(((bf16[6,2,128,192]{2,3,1,0:T(8,128)(2,1)}), bf16[6,2,128,768]{2,3,1,0:T(8,128)(2,1)}) %all-gather.13.cloned.1.call-update) | async-done | bytes 2359312 | tf_op jit(solution)/shard_map/all_gather | solution.py:56
  267.4 7.5 multiply_convert_fusion
  274.9 18.1 %all-gather.15.cloned.1.call-done = bf16[6,2,128,768]{2,3,1,0:T(8,128)(2,1)} async-done(((bf16[6,2,128,192]{2,3,1,0:T(8,128)(2,1)}), bf16[6,2,128,768]{2,3,1,0:T(8,128)(2,1)}) %all-gather.15.cloned.1.call-update) | async-done | bytes 2359312 | tf_op jit(solution)/shard_map/all_gather | solution.py:79
  293.0 8.2 fusion.29
  302.6 3.7 fusion.92
  306.3 47.9 %reduce-scatter.9.cloned.1.call-done = f32[6,2,128,192]{2,3,1,0:T(8,128)} async-done(((f32[6,2,128,768]{2,3,1,0:T(8,128)}), f32[6,2,128,192]{2,3,1,0:T(8,128)}) %reduce-scatter.9.cloned.1.call-update) | async-done | bytes 1179664 | tf_op jit(solution)/shard_map/reduce_scatter | solution.py:61
  354.3 2.5 multiply_reduce_fusion
  356.8 11.3 %all-reduce.7 = (f32[6,2,128]{2,1,0:T(2,128)}, f32[6,2,128]{2,1,0:T(2,128)}) all-reduce(f32[6,2,128]{2,1,0:T(2,128)} %get-tuple-element.580, f32[6,2,128]{2,1,0:T(2,128)} %get-tuple-element.584), channel_id=1, replica_groups=mesh['seq'=8,'head'=4] {'head'}, use_global_device_ids=true, to_apply=%region_21.22 | all-reduce | flops 3072 | bytes 24576 | tf_op jit(solution)/shard_map/psum | solution.py:47
  372.8 24.7 %all-gather.17.cloned.1.call-done = bf16[6,2,128,768]{2,3,1,0:T(8,128)(2,1)} async-done(((bf16[6,2,128,192]{2,3,1,0:T(8,128)(2,1)}), bf16[6,2,128,768]{2,3,1,0:T(8,128)(2,1)}) %all-gather.17.cloned.1.call-update) | async-done | bytes 2359312 | tf_op jit(solution)/shard_map/all_gather | solution.py:79
  397.5 2.3 multiply_reduce_fusion.1
  407.8 249.7 %while.27 = (s32[]{:T(128)}, bf16[6,128,192]{1,2,0:T(8,128)(2,1)}, bf16[6,128,192]{1,2,0:T(8,128)(2,1)}, f32[6,128,192]{1,2,0:T(8,128)}, f32[6,128,192]{1,2,0:T(...) while((s32[]{:T(128)}, bf16[6,128,192]{1,2,0:T(8,128)(2,1)}, ...), condition=%wide.region_25.26_spmd.clone.clone.clone, body=%wide.region_23.25_spmd.clone.clone.clone.sunk | while | flops 760960384 | bytes 41536376 | solution.py:268
  408.8 4.1 collective-permute-start
  414.6 3.4 collective-permute-start.1
  423.6 3.1 fusion.200
  429.3 6.4 collective-permute-done.2
  437.5 3.1 collective-permute-done.3
  442.5 2.2 collective-permute-start
  446.4 4.3 collective-permute-start.1
  455.5 3.1 fusion.200
  459.4 2.2 collective-permute-start.3
  462.0 6.4 collective-permute-done.2
  470.3 2.2 collective-permute-done.3
  478.1 4.6 collective-permute-start.1
  487.5 3.1 fusion.200
  494.0 5.9 collective-permute-done.2
  509.1 4.6 collective-permute-start.1
  518.5 3.1 fusion.200
  525.0 5.9 collective-permute-done.2
  540.2 4.6 collective-permute-start.1
  549.6 3.1 fusion.200
  556.0 5.9 collective-permute-done.2
  571.2 4.6 collective-permute-start.1
  580.6 3.1 fusion.200
  586.3 7.1 collective-permute-done.2
  602.1 4.0 collective-permute-start.1
  610.9 3.1 fusion.200
  616.6 6.9 collective-permute-done.2
  632.1 4.2 collective-permute-start.1
  641.2 3.1 fusion.200
  646.9 6.7 collective-permute-done.2
  661.6 4.2 convolution_bitcast_fusion.1
  667.0 5.8 fusion.97
  672.9 6.1 fusion.44
  679.0 3.4 fusion.49
  684.2 2.8 fusion.54
  687.0 23.0 %reduce-scatter.11.cloned.1.call-done = f32[6,2,128,192]{2,3,1,0:T(8,128)} async-done(((f32[6,2,128,768]{2,3,1,0:T(8,128)}), f32[6,2,128,192]{2,3,1,0:T(8,128)}) %reduce-scatter.11.cloned.1.call-update) | async-done | bytes 1179664 | tf_op jit(solution)/shard_map/reduce_scatter | solution.py:61
  710.1 2.4 fusion.87
  712.5 22.0 %all-reduce.4 = (f32[192]{0:T(256)}, f32[192]{0:T(256)}, f32[192]{0:T(256)}, f32[192]{0:T(256)}) all-reduce(f32[192]{0:T(256)} %get-tuple-element.581, f32[192]{0:T(256)} %get-tuple-element.586, f32[192]{0:T(256)} %get-tuple-element.579, f32[192]{0:T(256)} %get-tuple-element.585), channel_id=1, replica_groups=mesh['seq'=8,'head'=4] {'seq'}, use_global_device_ids=true, to_apply=%region_36.37 | all-reduce | flops 768 | bytes 6144 | tf_op jit(solution)/shard_map/psum | solution.py:303
  734.5 12.3 %all-reduce.6 = (f32[6,2,128]{2,1,0:T(2,128)}, f32[6,2,128]{2,1,0:T(2,128)}) all-reduce(f32[6,2,128]{2,1,0:T(2,128)} %get-tuple-element.582, f32[6,2,128]{2,1,0:T(2,128)} %get-tuple-element.583), channel_id=1, replica_groups=mesh['seq'=8,'head'=4] {'head'}, use_global_device_ids=true, to_apply=%region_30.31 | all-reduce | flops 3072 | bytes 24576 | tf_op jit(solution)/shard_map/psum | solution.py:47
  749.4 11.4 %reduce-scatter.7.cloned.1.call-done = f32[6,2,128,192]{2,3,1,0:T(8,128)} async-done(((f32[6,2,128,768]{2,3,1,0:T(8,128)}), f32[6,2,128,192]{2,3,1,0:T(8,128)}) %reduce-scatter.7.cloned.1.call-update) | async-done | bytes 1179664 | tf_op jit(solution)/shard_map/reduce_scatter | solution.py:75
  760.8 3.9 fusion.86
  764.6 237.0 %all-reduce.12.cloned.1.call-done = (f32[768,3,192]{0,2,1:T(8,128)}, f32[192,768]{1,0:T(8,128)}, f32[768,768]{1,0:T(8,128)}, f32[768,768]{1,0:T(8,128)}) async-done(((f32[768,3,192]{0,2,1:T(8,128)}, f32[192,768]{1,0:T(8,128)}, f32[768,768]{1,0:T(8,128)}, f32[768,768]{1,0:T(8,128)}), (f32[768,3,192]{0,2,1:T(8,128)}, f32[192,768]{1,0:T(8,128)}, f32[768,768]{1,0:T(8,128)}, ...) | async-done | bytes 7077904 | tf_op jit(solution)/shard_map/psum | solution.py:303
  1001.7 2.9 copy.247
  (466 shorter events, 182.8 us)
Async XLA Ops:
  7.2 260.2 %copy-start = (bf16[768,768]{1,0:T(8,128)(2,1)S(1)}, bf16[768,768]{1,0:T(8,128)(2,1)}, u32[]{:S(2)}) copy-start(bf16[768,768]{1,0:T(8,128)(2,1)} %param.21) | copy-start | bytes 3538948
  7.2 41.5 %copy-start.54 = (bf16[768,3,192]{0,2,1:T(8,128)(2,1)S(1)}, bf16[768,3,192]{0,2,1:T(8,128)(2,1)}, u32[]{:S(2)}) copy-start(bf16[768,3,192]{0,2,1:T(8,128)(2,1)} %param.17) | copy-start | bytes 2654212
  7.2 41.4 %all-gather.7.cloned.1.call-start = ((), (), s32[]{:S(2)}) async-start(), calls=%async_computation.4 | async-start | bytes 2949120 | tf_op jit(solution)/shard_map/all_gather | solution.py:56
  24.1 86.6 %all-gather.9.cloned.1.call-start = ((), (), s32[]{:S(2)}) async-start(), calls=%async_computation.5 | async-start | bytes 2654208 | tf_op jit(solution)/shard_map/all_gather | solution.py:153
  25.0 29.0 %copy-start.42 = (f32[128,32]{0,1:T(8,128)}, f32[128,32]{0,1:T(8,128)S(1)}, u32[]{:S(2)}) copy-start(f32[128,32]{0,1:T(8,128)S(1)} %get-tuple-element.671) | copy-start | bytes 49156
  56.8 107.9 %all-gather.11.cloned.1.call-start = ((), (), s32[]{:S(2)}) async-start(), calls=%async_computation.6 | async-start | bytes 2654208 | tf_op jit(solution)/shard_map/all_gather | solution.py:154
  62.5 164.8 %reduce-scatter.5.cloned.1.call-start = ((), (), s32[]{:S(2)}) async-start(), calls=%async_computation.7 | async-start | bytes 5898240 | tf_op jit(solution)/shard_map/reduce_scatter | solution.py:75
  63.1 3.2 copy-start.29
  164.7 13.4 %copy-start.37 = (bf16[192,768]{1,0:T(8,128)(2,1)S(1)}, bf16[192,768]{1,0:T(8,128)(2,1)}, u32[]{:S(2)}) copy-start(bf16[192,768]{1,0:T(8,128)(2,1)} %param.18) | copy-start | bytes 884740
  181.1 46.2 %copy-start.9 = (bf16[6,2,128,192]{2,3,1,0:T(8,128)(2,1)S(1)}, bf16[6,2,128,192]{2,3,1,0:T(8,128)(2,1)}, u32[]{:S(2)}) copy-start(bf16[6,2,128,192]{2,3,1,0:T(8,128)(2,1)} %param.13) | copy-start | bytes 1769476
  181.1 86.3 %all-gather.13.cloned.1.call-start = ((), (), s32[]{:S(2)}) async-start(), calls=%async_computation.8 | async-start | bytes 2949120 | tf_op jit(solution)/shard_map/all_gather | solution.py:56
  229.4 140.1 %copy-start.3 = (f32[6,2,128,192]{2,3,1,0:T(8,128)}, f32[6,2,128,192]{2,3,1,0:T(8,128)S(1)}, u32[]{:S(2)}) copy-start(f32[6,2,128,192]{2,3,1,0:T(8,128)S(1)} %get-tuple-element.638) | copy-start | bytes 3538948
  241.5 51.4 %all-gather.15.cloned.1.call-start = ((), (), s32[]{:S(2)}) async-start(), calls=%async_computation.10 | async-start | bytes 2949120 | tf_op jit(solution)/shard_map/all_gather | solution.py:79
  242.1 112.1 %reduce-scatter.9.cloned.1.call-start = ((), (), s32[]{:S(2)}) async-start(), calls=%async_computation.11 | async-start | bytes 5898240 | tf_op jit(solution)/shard_map/reduce_scatter | solution.py:61
  306.3 63.8 %copy-start.15 = (bf16[6,2,128,192]{2,3,1,0:T(8,128)(2,1)S(1)}, bf16[6,2,128,192]{2,3,1,0:T(8,128)(2,1)}, u32[]{:S(2)}) copy-start(bf16[6,2,128,192]{2,3,1,0:T(8,128)(2,1)} %param.23) | copy-start | bytes 1769476
  306.3 91.2 %all-gather.17.cloned.1.call-start = ((), (), s32[]{:S(2)}) async-start(), calls=%async_computation.12 | async-start | bytes 2949120 | tf_op jit(solution)/shard_map/all_gather | solution.py:79
  354.3 15.8 %copy-start.13 = (f32[6,2,128,192]{2,3,1,0:T(8,128)S(1)}, f32[6,2,128,192]{2,3,1,0:T(8,128)}, u32[]{:S(2)}) copy-start(f32[6,2,128,192]{2,3,1,0:T(8,128)} %reduce-scatter.9.cloned.1.call-done) | copy-start | bytes 3538948
  372.1 25.4 %copy-start.34 = (f32[6,2,3,128,64]{3,4,2,0,1:T(8,128)S(1)}, f32[6,2,3,128,64]{3,4,2,0,1:T(8,128)}, u32[]{:S(2)}) copy-start(f32[6,2,3,128,64]{3,4,2,0,1:T(8,128)} %get-tuple-element.677) | copy-start | bytes 3538948
  372.1 25.4 %copy-start.38 = (bf16[192,768]{1,0:T(8,128)(2,1)S(1)}, bf16[192,768]{1,0:T(8,128)(2,1)}, u32[]{:S(2)}) copy-start(bf16[192,768]{1,0:T(8,128)(2,1)} %param.18) | copy-start | bytes 884740
  372.1 337.9 %reduce-scatter.11.cloned.1.call-start = ((), (), s32[]{:S(2)}) async-start(), calls=%async_computation.13 | async-start | bytes 5898240 | tf_op jit(solution)/shard_map/reduce_scatter | solution.py:61
  408.8 32.7 %collective-permute-start = (bf16[6,128,192]{1,2,0:T(8,128)(2,1)S(1)}, bf16[6,128,192]{1,2,0:T(8,128)(2,1)}, u32[]{:S(2)}, u32[]{:S(2)}) collective-permute-start(bf16[6,128,192]{1,2,0:T(8,128)(2,1)S(1)} %copy.232), channel_id=1, source_target_pairs={{0,4},{4,8},{8,12},{12,16},{16,20},{20,24},{24,28},{1,5},{5,9},{9,... | collective-permute-start | bytes 884744 | tf_op jit(solution)/shard_map/while/body/eval_jaxpr/ppermute | solution.py:19
  414.6 26.9 %collective-permute-start.1 = (bf16[6,128,192]{1,2,0:T(8,128)(2,1)}, bf16[6,128,192]{1,2,0:T(8,128)(2,1)}, u32[]{:S(2)}, u32[]{:S(2)}) collective-permute-start(bf16[6,128,192]{1,2,0:T(8,128)(2,1)} %copy.233), channel_id=1, source_target_pairs={{0,4},{4,8},{8,12},{12,16},{16,20},{20,24},{24,28},{1,5},{5,9},{9,... | collective-permute-start | bytes 884744 | tf_op jit(solution)/shard_map/while/body/eval_jaxpr/ppermute | solution.py:19
  422.8 12.9 %collective-permute-start.2 = (bf16[6,128,192]{1,2,0:T(8,128)(2,1)}, bf16[6,128,192]{1,2,0:T(8,128)(2,1)}, u32[]{:S(2)}, u32[]{:S(2)}) collective-permute-start(bf16[6,128,192]{1,2,0:T(8,128)(2,1)} %fusion.199), channel_id=1, source_target_pairs={{0,4},{4,8},{8,12},{12,16},{16,20},{20,24},{24,28},{28,0},{1,5},{5... | collective-permute-start | bytes 884744 | tf_op jit(solution)/shard_map/while/body/eval_jaxpr/ppermute | solution.py:24
  427.5 13.2 %collective-permute-start.3 = (bf16[6,128,192]{1,2,0:T(8,128)(2,1)}, bf16[6,128,192]{1,2,0:T(8,128)(2,1)S(1)}, u32[]{:S(2)}, u32[]{:S(2)}) collective-permute-start(bf16[6,128,192]{1,2,0:T(8,128)(2,1)} %fusion.201), channel_id=1, source_target_pairs={{0,4},{4,8},{8,12},{12,16},{16,20},{20,24},{24,28},{28,0},{1,5},{5... | collective-permute-start | bytes 884744 | tf_op jit(solution)/shard_map/while/body/eval_jaxpr/ppermute | solution.py:24
  442.5 30.9 %collective-permute-start = (bf16[6,128,192]{1,2,0:T(8,128)(2,1)S(1)}, bf16[6,128,192]{1,2,0:T(8,128)(2,1)}, u32[]{:S(2)}, u32[]{:S(2)}) collective-permute-start(bf16[6,128,192]{1,2,0:T(8,128)(2,1)S(1)} %copy.232), channel_id=1, source_target_pairs={{0,4},{4,8},{8,12},{12,16},{16,20},{20,24},{24,28},{1,5},{5,9},{9,... | collective-permute-start | bytes 884744 | tf_op jit(solution)/shard_map/while/body/eval_jaxpr/ppermute | solution.py:19
  446.4 27.0 %collective-permute-start.1 = (bf16[6,128,192]{1,2,0:T(8,128)(2,1)}, bf16[6,128,192]{1,2,0:T(8,128)(2,1)}, u32[]{:S(2)}, u32[]{:S(2)}) collective-permute-start(bf16[6,128,192]{1,2,0:T(8,128)(2,1)} %copy.233), channel_id=1, source_target_pairs={{0,4},{4,8},{8,12},{12,16},{16,20},{20,24},{24,28},{1,5},{5,9},{9,... | collective-permute-start | bytes 884744 | tf_op jit(solution)/shard_map/while/body/eval_jaxpr/ppermute | solution.py:19
  455.5 13.0 %collective-permute-start.2 = (bf16[6,128,192]{1,2,0:T(8,128)(2,1)}, bf16[6,128,192]{1,2,0:T(8,128)(2,1)}, u32[]{:S(2)}, u32[]{:S(2)}) collective-permute-start(bf16[6,128,192]{1,2,0:T(8,128)(2,1)} %fusion.199), channel_id=1, source_target_pairs={{0,4},{4,8},{8,12},{12,16},{16,20},{20,24},{24,28},{28,0},{1,5},{5... | collective-permute-start | bytes 884744 | tf_op jit(solution)/shard_map/while/body/eval_jaxpr/ppermute | solution.py:24
  459.4 13.1 %collective-permute-start.3 = (bf16[6,128,192]{1,2,0:T(8,128)(2,1)}, bf16[6,128,192]{1,2,0:T(8,128)(2,1)S(1)}, u32[]{:S(2)}, u32[]{:S(2)}) collective-permute-start(bf16[6,128,192]{1,2,0:T(8,128)(2,1)} %fusion.201), channel_id=1, source_target_pairs={{0,4},{4,8},{8,12},{12,16},{16,20},{20,24},{24,28},{28,0},{1,5},{5... | collective-permute-start | bytes 884744 | tf_op jit(solution)/shard_map/while/body/eval_jaxpr/ppermute | solution.py:24
  474.4 30.1 %collective-permute-start = (bf16[6,128,192]{1,2,0:T(8,128)(2,1)S(1)}, bf16[6,128,192]{1,2,0:T(8,128)(2,1)}, u32[]{:S(2)}, u32[]{:S(2)}) collective-permute-start(bf16[6,128,192]{1,2,0:T(8,128)(2,1)S(1)} %copy.232), channel_id=1, source_target_pairs={{0,4},{4,8},{8,12},{12,16},{16,20},{20,24},{24,28},{1,5},{5,9},{9,... | collective-permute-start | bytes 884744 | tf_op jit(solution)/shard_map/while/body/eval_jaxpr/ppermute | solution.py:19
  478.1 26.4 %collective-permute-start.1 = (bf16[6,128,192]{1,2,0:T(8,128)(2,1)}, bf16[6,128,192]{1,2,0:T(8,128)(2,1)}, u32[]{:S(2)}, u32[]{:S(2)}) collective-permute-start(bf16[6,128,192]{1,2,0:T(8,128)(2,1)} %copy.233), channel_id=1, source_target_pairs={{0,4},{4,8},{8,12},{12,16},{16,20},{20,24},{24,28},{1,5},{5,9},{9,... | collective-permute-start | bytes 884744 | tf_op jit(solution)/shard_map/while/body/eval_jaxpr/ppermute | solution.py:19
  487.4 12.4 %collective-permute-start.2 = (bf16[6,128,192]{1,2,0:T(8,128)(2,1)}, bf16[6,128,192]{1,2,0:T(8,128)(2,1)}, u32[]{:S(2)}, u32[]{:S(2)}) collective-permute-start(bf16[6,128,192]{1,2,0:T(8,128)(2,1)} %fusion.199), channel_id=1, source_target_pairs={{0,4},{4,8},{8,12},{12,16},{16,20},{20,24},{24,28},{28,0},{1,5},{5... | collective-permute-start | bytes 884744 | tf_op jit(solution)/shard_map/while/body/eval_jaxpr/ppermute | solution.py:24
  491.3 12.3 %collective-permute-start.3 = (bf16[6,128,192]{1,2,0:T(8,128)(2,1)}, bf16[6,128,192]{1,2,0:T(8,128)(2,1)S(1)}, u32[]{:S(2)}, u32[]{:S(2)}) collective-permute-start(bf16[6,128,192]{1,2,0:T(8,128)(2,1)} %fusion.201), channel_id=1, source_target_pairs={{0,4},{4,8},{8,12},{12,16},{16,20},{20,24},{24,28},{28,0},{1,5},{5... | collective-permute-start | bytes 884744 | tf_op jit(solution)/shard_map/while/body/eval_jaxpr/ppermute | solution.py:24
  505.5 30.1 %collective-permute-start = (bf16[6,128,192]{1,2,0:T(8,128)(2,1)S(1)}, bf16[6,128,192]{1,2,0:T(8,128)(2,1)}, u32[]{:S(2)}, u32[]{:S(2)}) collective-permute-start(bf16[6,128,192]{1,2,0:T(8,128)(2,1)S(1)} %copy.232), channel_id=1, source_target_pairs={{0,4},{4,8},{8,12},{12,16},{16,20},{20,24},{24,28},{1,5},{5,9},{9,... | collective-permute-start | bytes 884744 | tf_op jit(solution)/shard_map/while/body/eval_jaxpr/ppermute | solution.py:19
  509.1 26.4 %collective-permute-start.1 = (bf16[6,128,192]{1,2,0:T(8,128)(2,1)}, bf16[6,128,192]{1,2,0:T(8,128)(2,1)}, u32[]{:S(2)}, u32[]{:S(2)}) collective-permute-start(bf16[6,128,192]{1,2,0:T(8,128)(2,1)} %copy.233), channel_id=1, source_target_pairs={{0,4},{4,8},{8,12},{12,16},{16,20},{20,24},{24,28},{1,5},{5,9},{9,... | collective-permute-start | bytes 884744 | tf_op jit(solution)/shard_map/while/body/eval_jaxpr/ppermute | solution.py:19
  518.5 12.4 %collective-permute-start.2 = (bf16[6,128,192]{1,2,0:T(8,128)(2,1)}, bf16[6,128,192]{1,2,0:T(8,128)(2,1)}, u32[]{:S(2)}, u32[]{:S(2)}) collective-permute-start(bf16[6,128,192]{1,2,0:T(8,128)(2,1)} %fusion.199), channel_id=1, source_target_pairs={{0,4},{4,8},{8,12},{12,16},{16,20},{20,24},{24,28},{28,0},{1,5},{5... | collective-permute-start | bytes 884744 | tf_op jit(solution)/shard_map/while/body/eval_jaxpr/ppermute | solution.py:24
  522.4 12.3 %collective-permute-start.3 = (bf16[6,128,192]{1,2,0:T(8,128)(2,1)}, bf16[6,128,192]{1,2,0:T(8,128)(2,1)S(1)}, u32[]{:S(2)}, u32[]{:S(2)}) collective-permute-start(bf16[6,128,192]{1,2,0:T(8,128)(2,1)} %fusion.201), channel_id=1, source_target_pairs={{0,4},{4,8},{8,12},{12,16},{16,20},{20,24},{24,28},{28,0},{1,5},{5... | collective-permute-start | bytes 884744 | tf_op jit(solution)/shard_map/while/body/eval_jaxpr/ppermute | solution.py:24
  536.5 30.0 %collective-permute-start = (bf16[6,128,192]{1,2,0:T(8,128)(2,1)S(1)}, bf16[6,128,192]{1,2,0:T(8,128)(2,1)}, u32[]{:S(2)}, u32[]{:S(2)}) collective-permute-start(bf16[6,128,192]{1,2,0:T(8,128)(2,1)S(1)} %copy.232), channel_id=1, source_target_pairs={{0,4},{4,8},{8,12},{12,16},{16,20},{20,24},{24,28},{1,5},{5,9},{9,... | collective-permute-start | bytes 884744 | tf_op jit(solution)/shard_map/while/body/eval_jaxpr/ppermute | solution.py:19
  540.2 26.3 %collective-permute-start.1 = (bf16[6,128,192]{1,2,0:T(8,128)(2,1)}, bf16[6,128,192]{1,2,0:T(8,128)(2,1)}, u32[]{:S(2)}, u32[]{:S(2)}) collective-permute-start(bf16[6,128,192]{1,2,0:T(8,128)(2,1)} %copy.233), channel_id=1, source_target_pairs={{0,4},{4,8},{8,12},{12,16},{16,20},{20,24},{24,28},{1,5},{5,9},{9,... | collective-permute-start | bytes 884744 | tf_op jit(solution)/shard_map/while/body/eval_jaxpr/ppermute | solution.py:19
  549.6 12.3 %collective-permute-start.2 = (bf16[6,128,192]{1,2,0:T(8,128)(2,1)}, bf16[6,128,192]{1,2,0:T(8,128)(2,1)}, u32[]{:S(2)}, u32[]{:S(2)}) collective-permute-start(bf16[6,128,192]{1,2,0:T(8,128)(2,1)} %fusion.199), channel_id=1, source_target_pairs={{0,4},{4,8},{8,12},{12,16},{16,20},{20,24},{24,28},{28,0},{1,5},{5... | collective-permute-start | bytes 884744 | tf_op jit(solution)/shard_map/while/body/eval_jaxpr/ppermute | solution.py:24
  553.5 12.2 %collective-permute-start.3 = (bf16[6,128,192]{1,2,0:T(8,128)(2,1)}, bf16[6,128,192]{1,2,0:T(8,128)(2,1)S(1)}, u32[]{:S(2)}, u32[]{:S(2)}) collective-permute-start(bf16[6,128,192]{1,2,0:T(8,128)(2,1)} %fusion.201), channel_id=1, source_target_pairs={{0,4},{4,8},{8,12},{12,16},{16,20},{20,24},{24,28},{28,0},{1,5},{5... | collective-permute-start | bytes 884744 | tf_op jit(solution)/shard_map/while/body/eval_jaxpr/ppermute | solution.py:24
  567.5 29.9 %collective-permute-start = (bf16[6,128,192]{1,2,0:T(8,128)(2,1)S(1)}, bf16[6,128,192]{1,2,0:T(8,128)(2,1)}, u32[]{:S(2)}, u32[]{:S(2)}) collective-permute-start(bf16[6,128,192]{1,2,0:T(8,128)(2,1)S(1)} %copy.232), channel_id=1, source_target_pairs={{0,4},{4,8},{8,12},{12,16},{16,20},{20,24},{24,28},{1,5},{5,9},{9,... | collective-permute-start | bytes 884744 | tf_op jit(solution)/shard_map/while/body/eval_jaxpr/ppermute | solution.py:19
  571.2 26.2 %collective-permute-start.1 = (bf16[6,128,192]{1,2,0:T(8,128)(2,1)}, bf16[6,128,192]{1,2,0:T(8,128)(2,1)}, u32[]{:S(2)}, u32[]{:S(2)}) collective-permute-start(bf16[6,128,192]{1,2,0:T(8,128)(2,1)} %copy.233), channel_id=1, source_target_pairs={{0,4},{4,8},{8,12},{12,16},{16,20},{20,24},{24,28},{1,5},{5,9},{9,... | collective-permute-start | bytes 884744 | tf_op jit(solution)/shard_map/while/body/eval_jaxpr/ppermute | solution.py:19
  580.6 12.9 %collective-permute-start.2 = (bf16[6,128,192]{1,2,0:T(8,128)(2,1)}, bf16[6,128,192]{1,2,0:T(8,128)(2,1)}, u32[]{:S(2)}, u32[]{:S(2)}) collective-permute-start(bf16[6,128,192]{1,2,0:T(8,128)(2,1)} %fusion.199), channel_id=1, source_target_pairs={{0,4},{4,8},{8,12},{12,16},{16,20},{20,24},{24,28},{28,0},{1,5},{5... | collective-permute-start | bytes 884744 | tf_op jit(solution)/shard_map/while/body/eval_jaxpr/ppermute | solution.py:24
  584.5 12.1 %collective-permute-start.3 = (bf16[6,128,192]{1,2,0:T(8,128)(2,1)}, bf16[6,128,192]{1,2,0:T(8,128)(2,1)S(1)}, u32[]{:S(2)}, u32[]{:S(2)}) collective-permute-start(bf16[6,128,192]{1,2,0:T(8,128)(2,1)} %fusion.201), channel_id=1, source_target_pairs={{0,4},{4,8},{8,12},{12,16},{16,20},{20,24},{24,28},{28,0},{1,5},{5... | collective-permute-start | bytes 884744 | tf_op jit(solution)/shard_map/while/body/eval_jaxpr/ppermute | solution.py:24
  598.4 29.1 %collective-permute-start = (bf16[6,128,192]{1,2,0:T(8,128)(2,1)S(1)}, bf16[6,128,192]{1,2,0:T(8,128)(2,1)}, u32[]{:S(2)}, u32[]{:S(2)}) collective-permute-start(bf16[6,128,192]{1,2,0:T(8,128)(2,1)S(1)} %copy.232), channel_id=1, source_target_pairs={{0,4},{4,8},{8,12},{12,16},{16,20},{20,24},{24,28},{1,5},{5,9},{9,... | collective-permute-start | bytes 884744 | tf_op jit(solution)/shard_map/while/body/eval_jaxpr/ppermute | solution.py:19
  602.1 25.4 %collective-permute-start.1 = (bf16[6,128,192]{1,2,0:T(8,128)(2,1)}, bf16[6,128,192]{1,2,0:T(8,128)(2,1)}, u32[]{:S(2)}, u32[]{:S(2)}) collective-permute-start(bf16[6,128,192]{1,2,0:T(8,128)(2,1)} %copy.233), channel_id=1, source_target_pairs={{0,4},{4,8},{8,12},{12,16},{16,20},{20,24},{24,28},{1,5},{5,9},{9,... | collective-permute-start | bytes 884744 | tf_op jit(solution)/shard_map/while/body/eval_jaxpr/ppermute | solution.py:19
  610.9 12.7 %collective-permute-start.2 = (bf16[6,128,192]{1,2,0:T(8,128)(2,1)}, bf16[6,128,192]{1,2,0:T(8,128)(2,1)}, u32[]{:S(2)}, u32[]{:S(2)}) collective-permute-start(bf16[6,128,192]{1,2,0:T(8,128)(2,1)} %fusion.199), channel_id=1, source_target_pairs={{0,4},{4,8},{8,12},{12,16},{16,20},{20,24},{24,28},{28,0},{1,5},{5... | collective-permute-start | bytes 884744 | tf_op jit(solution)/shard_map/while/body/eval_jaxpr/ppermute | solution.py:24
  614.8 11.8 %collective-permute-start.3 = (bf16[6,128,192]{1,2,0:T(8,128)(2,1)}, bf16[6,128,192]{1,2,0:T(8,128)(2,1)S(1)}, u32[]{:S(2)}, u32[]{:S(2)}) collective-permute-start(bf16[6,128,192]{1,2,0:T(8,128)(2,1)} %fusion.201), channel_id=1, source_target_pairs={{0,4},{4,8},{8,12},{12,16},{16,20},{20,24},{24,28},{28,0},{1,5},{5... | collective-permute-start | bytes 884744 | tf_op jit(solution)/shard_map/while/body/eval_jaxpr/ppermute | solution.py:24
  628.4 29.1 %collective-permute-start = (bf16[6,128,192]{1,2,0:T(8,128)(2,1)S(1)}, bf16[6,128,192]{1,2,0:T(8,128)(2,1)}, u32[]{:S(2)}, u32[]{:S(2)}) collective-permute-start(bf16[6,128,192]{1,2,0:T(8,128)(2,1)S(1)} %copy.232), channel_id=1, source_target_pairs={{0,4},{4,8},{8,12},{12,16},{16,20},{20,24},{24,28},{1,5},{5,9},{9,... | collective-permute-start | bytes 884744 | tf_op jit(solution)/shard_map/while/body/eval_jaxpr/ppermute | solution.py:19
  632.1 25.4 %collective-permute-start.1 = (bf16[6,128,192]{1,2,0:T(8,128)(2,1)}, bf16[6,128,192]{1,2,0:T(8,128)(2,1)}, u32[]{:S(2)}, u32[]{:S(2)}) collective-permute-start(bf16[6,128,192]{1,2,0:T(8,128)(2,1)} %copy.233), channel_id=1, source_target_pairs={{0,4},{4,8},{8,12},{12,16},{16,20},{20,24},{24,28},{1,5},{5,9},{9,... | collective-permute-start | bytes 884744 | tf_op jit(solution)/shard_map/while/body/eval_jaxpr/ppermute | solution.py:19
  641.2 12.5 %collective-permute-start.2 = (bf16[6,128,192]{1,2,0:T(8,128)(2,1)}, bf16[6,128,192]{1,2,0:T(8,128)(2,1)}, u32[]{:S(2)}, u32[]{:S(2)}) collective-permute-start(bf16[6,128,192]{1,2,0:T(8,128)(2,1)} %fusion.199), channel_id=1, source_target_pairs={{0,4},{4,8},{8,12},{12,16},{16,20},{20,24},{24,28},{28,0},{1,5},{5... | collective-permute-start | bytes 884744 | tf_op jit(solution)/shard_map/while/body/eval_jaxpr/ppermute | solution.py:24
  645.1 11.6 %collective-permute-start.3 = (bf16[6,128,192]{1,2,0:T(8,128)(2,1)}, bf16[6,128,192]{1,2,0:T(8,128)(2,1)S(1)}, u32[]{:S(2)}, u32[]{:S(2)}) collective-permute-start(bf16[6,128,192]{1,2,0:T(8,128)(2,1)} %fusion.201), channel_id=1, source_target_pairs={{0,4},{4,8},{8,12},{12,16},{16,20},{20,24},{24,28},{28,0},{1,5},{5... | collective-permute-start | bytes 884744 | tf_op jit(solution)/shard_map/while/body/eval_jaxpr/ppermute | solution.py:24
  665.8 95.0 %reduce-scatter.7.cloned.1.call-start = ((), (), s32[]{:S(2)}) async-start(), calls=%async_computation.9 | async-start | bytes 5898240 | tf_op jit(solution)/shard_map/reduce_scatter | solution.py:75
  672.8 328.8 %all-reduce.12.cloned.1.call-start = ((), (), s32[]{:S(2)}) async-start(), calls=%async_computation.14 | async-start | bytes 14155776 | tf_op jit(solution)/shard_map/psum | solution.py:303
  672.9 6.1 copy-start.51
  672.9 6.1 copy-start.56
  679.0 3.5 copy-start.22
  679.0 3.5 copy-start.52
  687.0 23.1 %copy-start.10 = (bf16[6,2,128,192]{2,3,1,0:T(8,128)(2,1)S(1)}, bf16[6,2,128,192]{2,3,1,0:T(8,128)(2,1)}, u32[]{:S(2)}) copy-start(bf16[6,2,128,192]{2,3,1,0:T(8,128)(2,1)} %param.13) | copy-start | bytes 1769476
  687.0 73.8 %copy-start.14 = (f32[6,2,128,192]{2,3,1,0:T(8,128)S(1)}, f32[6,2,128,192]{2,3,1,0:T(8,128)}, u32[]{:S(2)}) copy-start(f32[6,2,128,192]{2,3,1,0:T(8,128)} %reduce-scatter.9.cloned.1.call-done) | copy-start | bytes 3538948
  687.0 73.8 %copy-start.4 = (f32[6,2,128,192]{2,3,1,0:T(8,128)S(1)}, f32[6,2,128,192]{2,3,1,0:T(8,128)}, u32[]{:S(2)}) copy-start(f32[6,2,128,192]{2,3,1,0:T(8,128)} %copy-done.3) | copy-start | bytes 3538948
  687.0 73.8 %copy-start.16 = (bf16[6,2,128,192]{2,3,1,0:T(8,128)(2,1)S(1)}, bf16[6,2,128,192]{2,3,1,0:T(8,128)(2,1)}, u32[]{:S(2)}) copy-start(bf16[6,2,128,192]{2,3,1,0:T(8,128)(2,1)} %param.23) | copy-start | bytes 1769476
  687.0 73.7 %copy-start.41 = (f32[6,2,128]{2,1,0:T(2,128)S(1)}, f32[6,2,128]{2,1,0:T(2,128)}, u32[]{:S(2)}) copy-start(f32[6,2,128]{2,1,0:T(2,128)} %copy-done.40) | copy-start | bytes 18436
  1001.7 3.8 copy-start.27
  (79 other events, 111.8 us)
Sparse Core Ops, SparseCore 0:
  24.2 24.3 all-gather.6
  56.9 53.7 all-gather.8
  112.7 51.9 all-gather.10
  181.2 46.0 reduce-scatter.4
  241.7 25.6 all-gather.12
  268.9 24.0 all-gather.14
  306.4 47.8 reduce-scatter.8
  372.2 25.1 all-gather.16
  665.9 44.1 reduce-scatter.10
  712.6 48.1 reduce-scatter.6
  765.8 235.8 all-reduce.11
where the time goes:
time: 1020 us
  waiting for transfers between devices  591 us (58%)
  matrix products  134 us (13%)
  other arithmetic  86.3 us (8%)
  starting transfers between devices  69.7 us (7%)
  blocking collectives  68.4 us (7%)
  local copies, waits for them, and re-layouts  52.2 us (5%)
  between operations  14.7 us (1%)
    psum x1, waiting for transfers between devices, body(): lax.psum((qkv_grad, out_grad, up_grad, down_grad, attn_gain_grad, attn_bi...  237 us
    reduce_scatter x2, waiting for transfers between devices, norm_backward(): lax.psum_scatter(partial_value, 'head', scatter_dimension=3, tiled=True)  71 us
    ppermute x16, waiting for transfers between devices, from_behind(): lax.ppermute(x, axis, [(i, (i + by) % devices) for i in range(devices)])  66.3 us
    reduce_scatter x2, waiting for transfers between devices, branch_total(): lax.psum_scatter(partial_value, 'head', scatter_dimension=3, tiled=True)  57.5 us
    ppermute x16, starting transfers between devices, passed_along(): return lax.ppermute(block, axis, route)  52.6 us
    all_gather x2, waiting for transfers between devices, normalize(): gathered = lax.all_gather(scaled, 'head', axis=3, tiled=True)  48.4 us
    psum x4, blocking collectives, row_pair(): return lax.psum((first_sum, second_sum), 'head')  46.4 us
    all_gather x2, waiting for transfers between devices, gradient_rows(): return lax.all_gather(share, 'head', axis=3, tiled=True)  42.8 us
  transfers between devices with their start and end apart: 43, of which 27 were waited for; matrix products, arithmetic and copies ran while one was open for 17% of the time, Pallas kernels for 0%

commit v1 on v0

--- a/solution.py
+++ b/solution.py
@@ -1,6 +1,10 @@
+import functools
+
 import jax
 import jax.numpy as jnp
 from jax import lax
+from jax.experimental import pallas as pl
+from jax.experimental.pallas import tpu as pltpu
 from jax.sharding import PartitionSpec as P
 
 D = 768
@@ -11,6 +15,13 @@
 norm_eps = 1e-05
 masked_score = -1e30
 rotary_base = 10000.0
+
+MESH = pl.DeviceIdType.MESH
+VMEM = pltpu.VMEM
+F32 = jnp.float32
+BF16 = jnp.bfloat16
+ROWS_LIMIT = 16 << 20
+VMEM_LIMIT = 60 << 20
 
 
 def passed_along(block, axis, distance):
@@ -103,7 +114,7 @@
     return (new_max, new_sum, run_acc * factor[..., None] + added)
 
 
-def body(
+def gathered_body(
     inputs,
     doc_lengths,
     attn_gain,
@@ -327,6 +338,824 @@
     )
 
 
+def dot(a, b, ca, cb):
+    return lax.dot_general(a, b, (((ca,), (cb,)), ((), ())), preferred_element_type=F32)
+
+
+def remote(src, dst, send, recv, device):
+    return pltpu.make_async_remote_copy(
+        src_ref=src, dst_ref=dst, send_sem=send, recv_sem=recv, device_id=device, device_id_type=MESH
+    )
+
+
+class Place:
+    def __init__(self, n):
+        self.n = n
+        self.me = lax.axis_index("seq")
+        self.head = lax.axis_index("head")
+        self.core = lax.rem(self.head, 2)
+        self.y = lax.div(self.head, 2)
+        self.sib = (self.me, self.y * 2 + 1 - self.core)
+        self.yp = (self.me, (1 - self.y) * 2 + self.core)
+        self.diag = (self.me, (1 - self.y) * 2 + 1 - self.core)
+        self.half = n // 2
+        self.band = max(1, n // 8)
+
+    def lowest(self, slot, i):
+        near = i - self.band
+        short = jnp.where(i >= self.half, jnp.minimum(near, self.half), near)
+        return jnp.where(slot == 0, 0, jnp.maximum(short, 0))
+
+    def greet(self, near, everyone):
+        bar = pltpu.get_barrier_semaphore()
+        for d in near:
+            pl.semaphore_signal(bar, inc=1, device_id=d, device_id_type=MESH)
+        count = len(near)
+        if everyone:
+            for d in range(1, self.n):
+                there = lax.rem(self.me + d, self.n)
+                pl.semaphore_signal(bar, inc=1, device_id=(there, self.head), device_id_type=MESH)
+            count += self.n - 1
+        pl.semaphore_wait(bar, count)
+
+
+def each(count, step):
+    def run(i, carry):
+        step(i)
+        return carry
+
+    lax.fori_loop(0, count, run, 0)
+
+
+def row_stats(x):
+    mean = jnp.sum(x, axis=1, keepdims=True) / D
+    var = jnp.sum(x * x, axis=1, keepdims=True) / D - mean * mean
+    return mean, lax.rsqrt(var + norm_eps)
+
+
+def whole_rows(ref, s):
+    return jnp.concatenate([ref[s, 0], ref[s, 1]], axis=1)
+
+
+def turn(v, cosine, sine):
+    parts = []
+    for h in range(v.shape[0] // HEAD_DIM):
+        a = v[h * 64 : h * 64 + 32]
+        b = v[h * 64 + 32 : h * 64 + 64]
+        parts += [a * cosine - b * sine, b * cosine + a * sine]
+    return jnp.concatenate(parts, axis=0)
+
+
+def masks(me, length, start, end):
+    shape = (length, 2 * length)
+    key = lax.broadcasted_iota(jnp.int32, shape, 0)
+    row = lax.broadcasted_iota(jnp.int32, shape, 1)
+    noisy = row < length
+    at = jnp.where(noisy, row, row - length)
+    key_block = key >> 4
+    row_block = at >> 4
+    pos = key + me * length
+    same = jnp.logical_and(pos >= start, pos < end)
+    clean = jnp.logical_and(same, key_block < row_block + jnp.where(noisy, 0, 1))
+    own = jnp.logical_and(same, key_block == row_block)[:, :length]
+    return clean, own
+
+
+def front(n, perm, x_in, c_in, gb_in, w_t, wo_in, cos, sin, bounds,
+          xg, cg, ag, wog, gbf, n1, qt, kvn, kvo, kvb, att, lse,
+          own, land, gland, acc, mrow, lrow,
+          ss, sr, ys, yr, fs, fr, gs, gr, ws, wr, ks, kr):
+    at = Place(n)
+    slots, _, length, feat = x_in.shape
+    rows = 2 * length
+    hl = feat // HEAD_DIM
+    core, y, me = at.core, at.y, at.me
+    fulls = (xg, cg, ag)
+
+    def sib_copy(k, s):
+        return remote(own.at[k, s], land.at[k, s], ss.at[k, s], sr.at[k, s], at.sib)
+
+    def build(k, s):
+        a, b = own[k, s], land[k, s]
+
+        @pl.when(core == 0)
+        def _():
+            fulls[k][s, y] = jnp.concatenate([a, b], axis=1)
+
+        @pl.when(core == 1)
+        def _():
+            fulls[k][s, y] = jnp.concatenate([b, a], axis=1)
+
+    def y_copy(k, s):
+        part = fulls[k].at[s, y, pl.ds(length * core, length)]
+        return remote(part, part, ys.at[k, s], yr.at[k, s], at.yp)
+
+    def f_copy(k, s):
+        part = fulls[k].at[s, 1 - y, pl.ds(length * core, length)]
+        return remote(part, part, fs.at[k, s], fr.at[k, s], at.sib)
+
+    def kv_copy(s, i):
+        return remote(kvo.at[s], kvb.at[s, me], ks.at[s, i], kr.at[s, me], (i, at.head))
+
+    at.greet([at.sib, at.yp, at.diag], True)
+
+    def stage(s):
+        own[0, s] = x_in[perm[s]].reshape(rows, feat)
+        sib_copy(0, s).start()
+
+    each(slots, stage)
+    gland[at.head] = gb_in[...]
+    g_copies = [
+        remote(gb_in, gland.at[at.head], gs.at[k], gr.at[k], d)
+        for k, d in enumerate((at.sib, at.yp, at.diag))
+    ]
+    for copy in g_copies:
+        copy.start()
+
+    def stage_cot(s):
+        own[1, s] = c_in[perm[s]].reshape(rows, feat)
+        sib_copy(1, s).start()
+
+    def first_y(s):
+        sib_copy(0, s).wait_recv()
+        build(0, s)
+        y_copy(0, s).start()
+
+    each(slots, first_y)
+    each(slots, stage_cot)
+    for copy in g_copies:
+        copy.wait()
+    gbf[...] = jnp.concatenate([gland[i] for i in range(4)], axis=1)
+
+    def project(s):
+        x = whole_rows(xg, s).astype(F32)
+        mean, inv = row_stats(x)
+        normed = ((x - mean) * inv * gbf[0:1] + gbf[1:2]).astype(BF16)
+        n1[s] = normed
+        pt = dot(w_t[...], normed, 1, 1)
+        qk = turn(pt[: 2 * feat], cos[...], sin[...])
+        qt[s] = (qk[:feat] * HEAD_DIM**-0.5).astype(BF16)
+        kv = jnp.concatenate([qk[feat:], pt[2 * feat :]], axis=0).astype(BF16)
+        kvn[s] = kv[:, :length]
+        kvo[s] = kv[:, length:]
+        for d in range(1, n):
+            i = me + d
+
+            @pl.when(jnp.logical_and(i < n, at.lowest(s, i) <= me))
+            def _():
+                kv_copy(s, i).start()
+
+    def arrive(t):
+        @pl.when(t < slots)
+        def _():
+            y_copy(0, t).wait_recv()
+            f_copy(0, t).start()
+
+        @pl.when(t >= 1)
+        def _():
+            f_copy(0, t - 1).wait_recv()
+            project(t - 1)
+
+    each(slots + 1, arrive)
+
+    def first_y_cot(s):
+        sib_copy(1, s).wait_recv()
+        build(1, s)
+        y_copy(1, s).start()
+
+    each(slots, first_y_cot)
+
+    def wo_block(who):
+        return wog.at[pl.ds(pl.multiple_of(feat * who, 16), feat)]
+
+    wog[pl.ds(pl.multiple_of(feat * at.head, 16), feat)] = wo_in[...]
+    wo_sib = remote(wo_in, wo_block(at.head), ws.at[0], wr.at[0], at.sib)
+    wo_y = remote(wo_in, wo_block(at.head), ws.at[1], wr.at[1], at.yp)
+    wo_f = remote(wo_block(at.yp[1]), wo_block(at.yp[1]), ws.at[2], wr.at[2], at.sib)
+    wo_sib.start()
+    wo_y.start()
+
+    def absorb(s, h, keys, values, lanes, allowed, first):
+        hd = slice(h * HEAD_DIM, (h + 1) * HEAD_DIM)
+        sc = dot(keys[hd], qt[s, hd, lanes], 0, 0)
+        sc = jnp.where(allowed, sc, masked_score)
+        top = jnp.max(sc, axis=0, keepdims=True)
+        if first:
+            new = top
+        else:
+            old = mrow[h : h + 1, lanes]
+            new = jnp.maximum(old, top)
+            scale = jnp.exp(old - new)
+        p = jnp.exp(sc - new)
+        total = jnp.sum(p, axis=0, keepdims=True)
+        add = dot(values[hd], p.astype(BF16), 1, 0)
+        mrow[h : h + 1, lanes] = new
+        if first:
+            lrow[h : h + 1, lanes] = total
+            acc[hd, lanes] = add
+        else:
+            lrow[h : h + 1, lanes] = lrow[h : h + 1, lanes] * scale + total
+            acc[hd, lanes] = acc[hd, lanes] * scale + add
+
+    every = slice(0, rows)
+
+    def attend(s):
+        start, end = bounds[s, 0:1], bounds[s, 1:2]
+        clean, noisy = masks(me, length, start, end)
+        kc, kn = kvo[s], kvn[s]
+        for h in range(hl):
+            absorb(s, h, kc[:feat], kc[feat:], every, clean, True)
+            absorb(s, h, kn[:feat], kn[feat:], slice(0, length), noisy, False)
+
+        def one(j, carry):
+            remote(kvo.at[s], kvb.at[s, j], ks.at[s, j], kr.at[s, j], at.sib).wait_recv()
+            kv = kvb[s, j]
+            pos = lax.broadcasted_iota(jnp.int32, (length, rows), 0) + j * length
+            allowed = pos >= start
+            for h in range(hl):
+                absorb(s, h, kv[:feat], kv[feat:], every, allowed, False)
+            return carry
+
+        lax.fori_loop(at.lowest(s, me), me, one, 0)
+        for h in range(hl):
+            hd = slice(h * HEAD_DIM, (h + 1) * HEAD_DIM)
+            att[s, hd] = acc[hd] / lrow[h : h + 1]
+        lse[s] = mrow[...] + jnp.log(lrow[...])
+        own[2, s] = att[s].T.astype(BF16)
+        sib_copy(2, s).start()
+
+    mrow[...] = jnp.zeros_like(mrow)
+    lrow[...] = jnp.ones_like(lrow)
+
+    def second(t):
+        @pl.when(t < slots)
+        def _():
+            attend(t)
+            y_copy(1, t).wait_recv()
+            f_copy(1, t).start()
+
+        @pl.when(t >= 1)
+        def _():
+            sib_copy(2, t - 1).wait_recv()
+            build(2, t - 1)
+            y_copy(2, t - 1).start()
+
+    each(slots + 1, second)
+    wo_y.wait_recv()
+    wo_f.start()
+
+    def last(s):
+        y_copy(2, s).wait_recv()
+        f_copy(2, s).start()
+
+    each(slots, last)
+
+    def finish(s):
+        for k in range(3):
+            sib_copy(k, s).wait_send()
+            y_copy(k, s).wait_send()
+            f_copy(k, s).wait_send()
+        f_copy(1, s).wait_recv()
+        f_copy(2, s).wait_recv()
+        for d in range(1, n):
+            i = me + d
+
+            @pl.when(jnp.logical_and(i < n, at.lowest(s, i) <= me))
+            def _():
+                kv_copy(s, i).wait_send()
+
+    each(slots, finish)
+    wo_sib.wait()
+    wo_y.wait_send()
+    wo_f.wait()
+
+
+def middle(n, perm, xg, ag, cg, wog, gbf, wu, wd,
+           out, rl, rf, up_g, dn_g, gsum,
+           hid, n2, act, upre, ep, er, es, ey, ef, fp, fc, fh, fy, ob, osd,
+           e1s, e1r, e2s, e2r, e3s, e3r, f1s, f1r, f2s, f2r, f3s, f3r):
+    at = Place(n)
+    slots, _, rows, half = xg.shape
+    length = rows // 2
+    feat = half // 2
+    core, y = at.core, at.y
+    mine = pl.ds(length * core, length)
+    other = pl.ds(length * (1 - core), length)
+    at.greet([at.sib, at.yp], False)
+
+    def e_core(s):
+        return remote(ep.at[s, other], er.at[s], e1s.at[s], e1r.at[s], at.sib)
+
+    def e_y(s):
+        return remote(es.at[s], ey.at[s], e2s.at[s], e2r.at[s], at.yp)
+
+    def e_back(s):
+        return remote(ef.at[s, mine], ef.at[s, mine], e3s.at[s], e3r.at[s], at.sib)
+
+    def f_core(s):
+        return remote(fp.at[s, other], fc.at[s], f1s.at[s], f1r.at[s], at.sib)
+
+    def f_y(s):
+        return remote(fh.at[s, 1 - y], fy.at[s], f2s.at[s], f2r.at[s], at.yp)
+
+    def f_back(s):
+        return remote(osd.at[s], ob.at[s, core], f3s.at[s], f3r.at[s], at.sib)
+
+    def forward(s):
+        x = whole_rows(xg, s).astype(F32)
+        branch = dot(ag[s, 0], wog[:half], 1, 0) + dot(ag[s, 1], wog[half:], 1, 0)
+        h = x + branch
+        hid[s, 0] = h[:, :half]
+        hid[s, 1] = h[:, half:]
+        mean, inv = row_stats(h)
+        normed = ((h - mean) * inv * gbf[2:3] + gbf[3:4]).astype(BF16)
+        n2[s] = normed
+        up = dot(normed, wu[...], 1, 0)
+        cube = 0.7978845608028654 * (up + 0.044715 * up * up * up)
+        t = jnp.tanh(cube)
+        act[s] = (0.5 * up * (1.0 + t)).astype(BF16)
+        slope = 0.5 * (1.0 + t) + 0.5 * up * (1.0 - t * t) * (
+            0.7978845608028654 * (1.0 + 3 * 0.044715 * up * up)
+        )
+        da = dot(whole_rows(cg, s), wd[...], 1, 1)
+        pre = (da * slope).astype(BF16)
+        upre[s] = pre
+        ep[s] = dot(pre, wu[...], 1, 1).astype(BF16)
+        e_core(s).start()
+
+    def loop_one(t):
+        @pl.when(t < slots)
+        def _():
+            forward(t)
+
+        @pl.when(t >= 1)
+        def _():
+            s = t - 1
+            e_core(s).wait_recv()
+            es[s] = (ep[s, mine].astype(F32) + er[s].astype(F32)).astype(BF16)
+            e_y(s).start()
+
+    each(slots + 1, loop_one)
+    dn_g[...] = jnp.zeros_like(dn_g)
+    up_g[...] = jnp.zeros_like(up_g)
+    gsum[...] = jnp.zeros_like(gsum)
+
+    def loop_two(t):
+        @pl.when(t < slots)
+        def _():
+            fp[t] = dot(act[t], wd[...], 1, 0).astype(BF16)
+            f_core(t).start()
+            dn_g[...] += dot(act[t], whole_rows(cg, t), 0, 0)
+            up_g[...] += dot(n2[t], upre[t], 0, 0)
+            e_y(t).wait_recv()
+            ef[t, mine] = (es[t].astype(F32) + ey[t].astype(F32)).astype(BF16)
+            e_back(t).start()
+
+        @pl.when(t >= 1)
+        def _():
+            s = t - 1
+            f_core(s).wait_recv()
+            both = fp[s, mine].astype(F32) + fc[s].astype(F32)
+            fh[s, 0] = both[:, :half].astype(BF16)
+            fh[s, 1] = both[:, half:].astype(BF16)
+            f_y(s).start()
+
+    each(slots + 1, loop_two)
+
+    def loop_three(s):
+        e_back(s).wait_recv()
+        e = ef[s].astype(F32)
+        h = whole_rows(hid, s)
+        mean, inv = row_stats(h)
+        xh = (h - mean) * inv
+        gsum[0:1] += jnp.sum(e * xh, axis=0, keepdims=True)
+        gsum[1:2] += jnp.sum(e, axis=0, keepdims=True)
+        g = e * gbf[2:3]
+        first = jnp.sum(g, axis=1, keepdims=True) / D
+        second = jnp.sum(g * xh, axis=1, keepdims=True) / D
+        resid = whole_rows(cg, s).astype(F32) + inv * (g - first - xh * second)
+        rl[s] = resid.astype(BF16)
+
+        for yy in range(2):
+            for cc in range(2):
+
+                @pl.when(jnp.logical_and(y == yy, core == cc))
+                def _():
+                    rf[s] = resid[cc * length : (cc + 1) * length, yy * half : (yy + 1) * half]
+
+    each(slots, loop_three)
+
+    def loop_four(s):
+        f_y(s).wait_recv()
+        total = hid[s, y, mine] + (fh[s, y].astype(F32) + fy[s].astype(F32))
+        lo = total[:, :feat].astype(BF16)
+        hi = total[:, feat:].astype(BF16)
+
+        @pl.when(core == 0)
+        def _():
+            ob[s, 0] = lo
+            osd[s] = hi
+
+        @pl.when(core == 1)
+        def _():
+            ob[s, 1] = hi
+            osd[s] = lo
+
+        f_back(s).start()
+
+    each(slots, loop_four)
+
+    def finish(s):
+        e_core(s).wait_send()
+        e_y(s).wait_send()
+        e_back(s).wait_send()
+        f_core(s).wait_send()
+        f_y(s).wait_send()
+        f_back(s).wait()
+
+    each(slots, finish)
+
+    def place(s):
+        out[s] = ob[perm[s]]
+
+    each(slots, place)
+
+
+def back(n, perm, xg, n1, gbf, w_t, wo, rl, rf, att, lse, qt, kvn, kvo, kvb, cos, sin, bounds,
+         ig, qg, og, gsum,
+         do, dq, drow, dkv, dst, dla, qp, ep, er, st, sr_, es, ss_, ey, sy, ib, isd,
+         ks, kr, a1s, a1r, b1s, b1r, a2s, a2r, b2s, b2r, a3s, a3r):
+    at = Place(n)
+    slots, _, rows, half = xg.shape
+    length = rows // 2
+    feat = half // 2
+    hl = feat // HEAD_DIM
+    core, y, me = at.core, at.y, at.me
+    mine = pl.ds(length * core, length)
+    other = pl.ds(length * (1 - core), length)
+    at.greet([at.sib, at.yp], True)
+    every = slice(0, rows)
+
+    def kv_copy(s, j):
+        return remote(dst.at[s, j], dla.at[s, me], ks.at[s, j], kr.at[s, me], (j, at.head))
+
+    def e_core(s):
+        return remote(ep.at[s, other], er.at[s], a1s.at[s], a1r.at[s], at.sib)
+
+    def s_core(s):
+        return remote(st.at[s, 1 - core], sr_.at[s], b1s.at[s], b1r.at[s], at.sib)
+
+    def e_y(s):
+        return remote(es.at[s, 1 - y], ey.at[s], a2s.at[s], a2r.at[s], at.yp)
+
+    def s_y(s):
+        return remote(ss_.at[s], sy.at[s], b2s.at[s], b2r.at[s], at.yp)
+
+    def i_back(s):
+        return remote(isd.at[s], ib.at[s, core], a3s.at[s], a3r.at[s], at.sib)
+
+    og[...] = jnp.zeros_like(og)
+    qg[...] = jnp.zeros_like(qg)
+    gsum[...] = jnp.zeros_like(gsum)
+    drow[...] = jnp.zeros_like(drow)
+
+    def head_grads(s, h, keys, values, lanes, allowed):
+        hd = slice(h * HEAD_DIM, (h + 1) * HEAD_DIM)
+        q = qt[s, hd, lanes]
+        d_out = do[hd, lanes]
+        sc = dot(keys[hd], q, 0, 0)
+        p = jnp.exp(jnp.where(allowed, sc, masked_score) - lse[s, h : h + 1, lanes])
+        dp = dot(values[hd], d_out, 0, 0)
+        ds = (p * (dp - drow[h : h + 1, lanes])).astype(BF16)
+        dq_add = dot(keys[hd], ds, 1, 0)
+        dk = dot(q, ds, 1, 1)
+        dv = dot(d_out, p.astype(BF16), 1, 1)
+        return dq_add, dk, dv
+
+    def attend_back(s):
+        low_rows = rl[s]
+        d_out = dot(wo[...], low_rows, 1, 1).astype(BF16)
+        do[...] = d_out
+        a = att[s]
+        og[...] += dot(a.astype(BF16), low_rows, 1, 0)
+        prod = d_out.astype(F32) * a
+        for h in range(hl):
+            drow[h : h + 1] = jnp.sum(prod[h * HEAD_DIM : (h + 1) * HEAD_DIM], axis=0, keepdims=True)
+        start, end = bounds[s, 0:1], bounds[s, 1:2]
+        clean, noisy = masks(me, length, start, end)
+        kc, kn = kvo[s], kvn[s]
+        first = slice(0, length)
+        noisy_k = []
+        for h in range(hl):
+            hd = slice(h * HEAD_DIM, (h + 1) * HEAD_DIM)
+            vd = slice(feat + h * HEAD_DIM, feat + (h + 1) * HEAD_DIM)
+            dqa, dk, dv = head_grads(s, h, kc[:feat], kc[feat:], every, clean)
+            dq[hd] = dqa
+            dkv[s, hd] = dk
+            dkv[s, vd] = dv
+            dqa, dk, dv = head_grads(s, h, kn[:feat], kn[feat:], first, noisy)
+            dq[hd, first] += dqa
+            noisy_k.append(dk)
+            qp[s, 2 * feat + h * HEAD_DIM : 2 * feat + (h + 1) * HEAD_DIM, first] = dv.astype(BF16)
+        qp[s, feat : 2 * feat, first] = turn(
+            jnp.concatenate(noisy_k, axis=0), cos[:, :length], -sin[:, :length]
+        ).astype(BF16)
+
+        def one(j, carry):
+            kv = kvb[s, j]
+            pos = lax.broadcasted_iota(jnp.int32, (length, rows), 0) + j * length
+            allowed = pos >= start
+            for h in range(hl):
+                hd = slice(h * HEAD_DIM, (h + 1) * HEAD_DIM)
+                vd = slice(feat + h * HEAD_DIM, feat + (h + 1) * HEAD_DIM)
+                dqa, dk, dv = head_grads(s, h, kv[:feat], kv[feat:], every, allowed)
+                dq[hd] += dqa
+                dst[s, j, hd] = dk.astype(BF16)
+                dst[s, j, vd] = dv.astype(BF16)
+            kv_copy(s, j).start()
+            return carry
+
+        lax.fori_loop(at.lowest(s, me), me, one, 0)
+        qp[s, :feat] = (turn(dq[...], cos[...], -sin[...]) * HEAD_DIM**-0.5).astype(BF16)
+
+    each(slots, attend_back)
+
+    def project_back(s):
+        for d in range(1, n):
+            i = me + d
+
+            @pl.when(jnp.logical_and(i < n, at.lowest(s, i) <= me))
+            def _():
+                remote(dst.at[s, i], dla.at[s, i], ks.at[s, i], kr.at[s, i], at.sib).wait_recv()
+                dkv[s] += dla[s, i].astype(F32)
+
+        late = slice(length, rows)
+        total = dkv[s]
+        qp[s, feat : 2 * feat, late] = turn(total[:feat], cos[:, late], -sin[:, late]).astype(BF16)
+        qp[s, 2 * feat :, late] = total[feat:].astype(BF16)
+        pre = qp[s]
+        qg[...] += dot(pre, n1[s], 1, 0)
+        e = dot(pre, w_t[...], 0, 0)
+        x = whole_rows(xg, s).astype(F32)
+        mean, inv = row_stats(x)
+        xh = (x - mean) * inv
+        gsum[0:1] += jnp.sum(e * xh, axis=0, keepdims=True)
+        gsum[1:2] += jnp.sum(e, axis=0, keepdims=True)
+        ep[s] = e.astype(BF16)
+        g = e * gbf[0:1]
+        one_sum = jnp.sum(g, axis=1, keepdims=True)
+        two_sum = jnp.sum(g * xh, axis=1, keepdims=True)
+        lane = lax.broadcasted_iota(jnp.int32, (rows, 128), 1)
+        packed = jnp.where(lane == 0, one_sum, jnp.where(lane == 1, two_sum, 0.0)).T
+        st[s, 0] = packed[:8, :length]
+        st[s, 1] = packed[:8, length:]
+        e_core(s).start()
+        s_core(s).start()
+
+    def send_on(s):
+        e_core(s).wait_recv()
+        s_core(s).wait_recv()
+        both = ep[s, mine].astype(F32) + er[s].astype(F32)
+        es[s, 0] = both[:, :half].astype(BF16)
+        es[s, 1] = both[:, half:].astype(BF16)
+        ss_[s] = st[s, core] + sr_[s]
+        e_y(s).start()
+        s_y(s).start()
+
+    def loop_two(t):
+        @pl.when(t < slots)
+        def _():
+            project_back(t)
+
+        @pl.when(t >= 1)
+        def _():
+            send_on(t - 1)
+
+    each(slots + 1, loop_two)
+
+    def input_part(s):
+        e_y(s).wait_recv()
+        s_y(s).wait_recv()
+        e = es[s, y].astype(F32) + ey[s].astype(F32)
+        sums = ss_[s] + sy[s]
+        cols = jnp.concatenate([sums, jnp.zeros((120, length), F32)], axis=0).T
+        first, second = cols[:, 0:1] / D, cols[:, 1:2] / D
+        x = jnp.concatenate([xg[s, 0, mine], xg[s, 1, mine]], axis=1).astype(F32)
+        mean, inv = row_stats(x)
+        xh = (xg[s, y, mine].astype(F32) - mean) * inv
+        gain = jnp.where(y == 0, gbf[0:1, :half], gbf[0:1, half:])
+        grad = rf[s] + inv * (e * gain - first - xh * second)
+        lo, hi = grad[:, :feat], grad[:, feat:]
+
+        @pl.when(core == 0)
+        def _():
+            ib[s, 0] = lo
+            isd[s] = hi
+
+        @pl.when(core == 1)
+        def _():
+            ib[s, 1] = hi
+            isd[s] = lo
+
+        i_back(s).start()
+
+    each(slots, input_part)
+
+    def finish(s):
+        e_core(s).wait_send()
+        s_core(s).wait_send()
+        e_y(s).wait_send()
+        s_y(s).wait_send()
+        i_back(s).wait()
+
+        def sent(j, carry):
+            kv_copy(s, j).wait_send()
+            return carry
+
+        lax.fori_loop(at.lowest(s, me), me, sent, 0)
+
+    each(slots, finish)
+
+    def place(s):
+        ig[s] = ib[perm[s]]
+
+    each(slots, place)
+
+
+def call(kernel, ident, n, operands, outs, scratch, flops):
+    specs = [
+        pl.BlockSpec(memory_space=pltpu.SMEM if o.ndim == 1 else VMEM) for o in operands
+    ]
+    return pl.pallas_call(
+        functools.partial(kernel, n),
+        out_shape=[jax.ShapeDtypeStruct(s, t) for s, t in outs],
+        in_specs=specs,
+        out_specs=[pl.BlockSpec(memory_space=VMEM)] * len(outs),
+        scratch_shapes=scratch,
+        compiler_params=pltpu.CompilerParams(
+            collective_id=ident, has_side_effects=True, vmem_limit_bytes=VMEM_LIMIT
+        ),
+        cost_estimate=pl.CostEstimate(flops=flops, bytes_accessed=20 << 20, transcendentals=0),
+        name=kernel.__name__,
+    )(*operands)
+
+
+def body(
+    inputs,
+    doc_lengths,
+    attn_gain,
+    attn_bias,
+    w_qkv,
+    w_out,
+    ffn_gain,
+    ffn_bias,
+    w_up,
+    w_down,
+    cotangent,
+):
+    n = lax.axis_size("seq")
+    slots, _, length, feat = inputs.shape
+    rows, half, hl = 2 * length, 2 * feat, feat // HEAD_DIM
+    held = slots * n * half * length * 2
+    if held > ROWS_LIMIT:
+        return gathered_body(
+            inputs, doc_lengths, attn_gain, attn_bias, w_qkv, w_out, ffn_gain, ffn_bias, w_up, w_down, cotangent
+        )
+    sem = pltpu.SemaphoreType.DMA
+    me = lax.axis_index("seq")
+    long = jnp.argmax(doc_lengths[:, 0]).astype(jnp.int32)
+    ids = jnp.arange(slots, dtype=jnp.int32)
+    perm = jnp.where(ids == 0, long, jnp.where(ids == long, 0, ids))
+    ends = jnp.cumsum(doc_lengths, axis=1)[perm]
+    positions = me * length + jnp.arange(length, dtype=jnp.int32)
+    past = ends[:, :, None] <= positions[None, None, :]
+    first_key = jnp.max(jnp.where(past, ends[:, :, None], 0), axis=1)
+    last_key = jnp.min(jnp.where(past, 2**30, ends[:, :, None]), axis=1)
+    bounds = jnp.zeros((slots, 8, rows), jnp.int32)
+    bounds = bounds.at[:, 0].set(jnp.tile(first_key, (1, 2))).at[:, 1].set(jnp.tile(last_key, (1, 2)))
+    half_dim = HEAD_DIM // 2
+    freqs = rotary_base ** (-jnp.arange(half_dim, dtype=F32) / half_dim)
+    angles = freqs[:, None] * positions.astype(F32)[None, :]
+    cos = jnp.tile(jnp.cos(angles), (1, 2))
+    sin = jnp.tile(jnp.sin(angles), (1, 2))
+    w_t = w_qkv.reshape(D, 3 * feat).T
+    gains = jnp.concatenate(
+        [jnp.stack([attn_gain, attn_bias, ffn_gain, ffn_bias]), jnp.zeros((4, feat), F32)], axis=0
+    )
+    fulls = [((slots, 2, rows, half), BF16)] * 3
+    kinds = (3, slots)
+    xg, cg, ag, wog, gbf, n1, qt, kvn, kvo, kvb, att, lse = call(
+        front,
+        0,
+        n,
+        (perm, inputs, cotangent, gains, w_t, w_out, cos, sin, bounds),
+        fulls
+        + [
+            ((D, D), BF16),
+            ((8, D), F32),
+            ((slots, rows, D), BF16),
+            ((slots, feat, rows), BF16),
+            ((slots, half, length), BF16),
+            ((slots, half, length), BF16),
+            ((slots, n, half, length), BF16),
+            ((slots, feat, rows), F32),
+            ((slots, 8, rows), F32),
+        ],
+        [
+            VMEM((3, slots, rows, feat), BF16),
+            VMEM((3, slots, rows, feat), BF16),
+            VMEM((4, 8, feat), F32),
+            VMEM((feat, rows), F32),
+            VMEM((8, rows), F32),
+            VMEM((8, rows), F32),
+            *[sem(kinds)] * 6,
+            *[sem((3,))] * 4,
+            *[sem((slots, n))] * 2,
+        ],
+        3 * 10**9,
+    )
+    wide = VMEM((slots, rows, D), BF16)
+    part = VMEM((slots, length, D), BF16)
+    outputs, rl, rf, up_grad, down_grad, gsum2 = call(
+        middle,
+        1,
+        n,
+        (perm, xg, ag, cg, wog, gbf, w_up, w_down),
+        [
+            ((slots, 2, length, feat), BF16),
+            ((slots, rows, D), BF16),
+            ((slots, length, half), F32),
+            (w_up.shape, F32),
+            (w_down.shape, F32),
+            ((8, D), F32),
+        ],
+        [
+            VMEM((slots, 2, rows, half), F32),
+            *[wide] * 4,
+            *[part] * 3,
+            *[wide] * 2,
+            part,
+            VMEM((slots, 2, length, half), BF16),
+            VMEM((slots, length, half), BF16),
+            VMEM((slots, 2, length, feat), BF16),
+            VMEM((slots, length, feat), BF16),
+            *[sem((slots,))] * 12,
+        ],
+        15 * 10**9,
+    )
+    stat = VMEM((slots, 8, length), F32)
+    input_grad, qkv_grad, out_grad, gsum1 = call(
+        back,
+        2,
+        n,
+        (perm, xg, n1, gbf, w_t, w_out, rl, rf, att, lse, qt, kvn, kvo, kvb, cos, sin, bounds),
+        [
+            ((slots, 2, length, feat), F32),
+            ((3 * feat, D), F32),
+            ((feat, D), F32),
+            ((8, D), F32),
+        ],
+        [
+            VMEM((feat, rows), BF16),
+            VMEM((feat, rows), F32),
+            VMEM((8, rows), F32),
+            VMEM((slots, half, length), F32),
+            VMEM((slots, n, half, length), BF16),
+            VMEM((slots, n, half, length), BF16),
+            VMEM((slots, 3 * feat, rows), BF16),
+            wide,
+            part,
+            VMEM((slots, 2, 8, length), F32),
+            stat,
+            VMEM((slots, 2, length, half), BF16),
+            stat,
+            VMEM((slots, length, half), BF16),
+            stat,
+            VMEM((slots, 2, length, feat), F32),
+            VMEM((slots, length, feat), F32),
+            *[sem((slots, n))] * 2,
+            *[sem((slots,))] * 10,
+        ],
+        10 * 10**9,
+    )
+    gains_sum = lax.psum(jnp.concatenate([gsum1[:2], gsum2[:2] * 0.25], axis=0), ("seq", "head"))
+    gains_own = lax.dynamic_slice(gains_sum, (0, lax.axis_index("head") * feat), (4, feat))
+    up_low, down_low = lax.psum((up_grad.astype(BF16), down_grad.astype(BF16)), "seq")
+    qkv_low, out_low = lax.psum((qkv_grad.astype(BF16), out_grad.astype(BF16)), "seq")
+    return (
+        outputs,
+        input_grad,
+        qkv_low.astype(F32).T.reshape(w_qkv.shape),
+        out_low.astype(F32),
+        up_low.astype(F32),
+        down_low.astype(F32),
+        gains_own[0],
+        gains_own[1],
+        gains_own[2],
+        gains_own[3],
+    )
+
+
 def solution(mesh):
     in_specs = (
         P(None, None, "seq", "head"),

time: 1020 us -> 366 us (0.36)
  waiting for transfers between devices: 591 us -> 92.2 us
  Pallas kernels: 0 us -> 175 us
  matrix products: 134 us -> 0 us
  starting transfers between devices: 69.7 us -> 0.04 us
  other arithmetic: 86.3 us -> 16.7 us
  local copies, waits for them, and re-layouts: 52.2 us -> 12.3 us
  blocking collectives: 68.4 us -> 55.1 us
    pallas_call x0 -> x3, Pallas kernels: none -> 175 us  [call(): pl.pallas_call(functools.partial(kernel, n), out_shape=[jax.ShapeDtypeStr...]
    all_gather x6 -> x0, waiting for transfers between devices: 158 us -> none  [the longest x2 48.4 us: normalize(): gathered = lax.all_gather(scaled, 'head', axis=3, tiled=True)]
    psum x1, waiting for transfers between devices: 237 us -> 92.2 us  [body(): lax.psum((qkv_grad.astype(BF16), out_grad.astype(BF16)), 'seq')]
    dot_general x60 -> x0, matrix products: 134 us -> none  [the longest x8 24.7 us: piece_grads(): jnp.einsum('schlk,schld->skhd', weights_now, grad_wide, precision=lax.Pre...]
    reduce_scatter x4 -> x0, waiting for transfers between devices: 128 us -> none  [the longest x2 71 us: norm_backward(): lax.psum_scatter(partial_value, 'head', scatter_dimension=3, tiled=True)]
    ppermute x32 -> x0, starting transfers between devices: 68 us -> none  [the longest x16 52.6 us: passed_along(): return lax.ppermute(block, axis, route)]
    ppermute x32 -> x0, waiting for transfers between devices: 66.3 us -> none  [the longest x16 66.3 us: from_behind(): lax.ppermute(x, axis, [(i, (i + by) % devices) for i in range(devices)])]
    convert_element_type x37 -> x7, other arithmetic: 41.5 us -> 11 us  [the longest x1 2.94 us: body(): up_low.astype(F32)]
  transfers between devices with their start and end apart: 43 -> 1, of which waited for: 27 -> 1; matrix products, arithmetic and copies ran while one was open for 17% -> 1% of each run, Pallas kernels for 0% -> 0%
where the time goes in v1:
time: 366 us
  Pallas kernels  175 us (48%)
  waiting for transfers between devices  92.2 us (25%)
  blocking collectives  55.1 us (15%)
  other arithmetic  16.7 us (5%)
  between operations  14.3 us (4%)
  local copies, waits for them, and re-layouts  12.3 us (3%)
    pallas_call x3, Pallas kernels, call(): pl.pallas_call(functools.partial(kernel, n), out_shape=[jax.ShapeDtypeStr...  175 us
    psum x1, waiting for transfers between devices, body(): lax.psum((qkv_grad.astype(BF16), out_grad.astype(BF16)), 'seq')  92.2 us
    psum x1, blocking collectives, body(): lax.psum(jnp.concatenate([gsum1[:2], gsum2[:2] * 0.25], axis=0), ('seq',...  55.1 us
    unnamed x34, local copies, waits for them, and re-layouts  8.7 us
  transfers between devices with their start and end apart: 1, of which 1 were waited for; matrix products, arithmetic and copies ran while one was open for 1% of the time, Pallas kernels for 0%

profile of v1, /device:TPU:0, one launch (start us, length us, event | category | flops | bytes accessed | tf_op | source)
XLA Modules:
  0.0 365.7 jit_solution(4314245574759618085)
XLA Ops:
  7.2 0.0 copy-start.7
  7.2 0.0 copy-start.10
  7.2 0.0 copy-start.11
  7.2 0.0 copy-start.12
  7.2 0.0 copy-start.13
  7.2 0.0 all-reduce.4.cloned.1.call-start
  7.3 0.9 slice_reduce_fusion
  8.2 0.7 iota_reduce_fusion
  8.8 0.7 fusion.2
  9.5 1.2 compare_select_fusion.6.perm
  10.6 0.8 reduce_window_sum.11
  11.5 0.6 gather_fusion
  12.0 0.1 fusion.1
  12.2 0.1 multiply_sine_fusion
  12.3 0.6 copy.33
  13.0 0.6 copy.34
  13.6 2.2 copy.25.x_in
  15.8 0.0 copy-done.7
  15.8 1.2 copy.26.c_in
  17.0 0.0 copy-start.9
  17.0 0.0 copy-done.10
  17.0 0.0 copy-done.11
  17.1 0.0 copy-done.12
  17.1 0.0 copy-done.13
  17.1 0.6 concatenate.10.gb_in
  17.7 0.0 copy-done.9
  17.7 68.1 %front.1 = (bf16[6,2,256,384]{3,2,1,0:T(8,128)(2,1)}, bf16[6,2,256,384]{3,2,1,0:T(8,128)(2,1)}, bf16[6,2,256,384]{3,2,1,0:T(8,128)(2,1)}, bf16[768,768]{1,0:T(8,...) custom-call(s32[6]{0:T(128)} %compare_select_fusion.6.perm, ...), custom_call_target="tpu_custom_call" | custom-call | flops 3000000000 | bytes 20971520 | tf_op jit(solution)/shard_map/front/pallas_call | solution.py:989
  85.8 54.5 %middle.1 = (bf16[6,2,128,192]{3,2,1,0:T(8,128)(2,1)}, bf16[6,256,768]{2,1,0:T(8,128)(2,1)}, f32[6,128,384]{2,1,0:T(8,128)}, f32[768,768]{1,0:T(8,128)}, f32[768,768]{1,0:T(8,128)}, /*index=5*/f32[8,768]{1,0:T(8,128)}) custom-call(s32[6]{0:T(128)} %compare_select_fusion.6.perm, bf16[6,2,256,384]{3,2,1,0:T(8,128)(2,1)} %get-tuple-element.58.xg, ...), custom_call_target="tpu_custom_call" | custom-call | flops 15000000512 | bytes 20971520 | tf_op jit(solution)/shard_map/middle/pallas_call | solution.py:989
  140.3 52.5 %back.1 = (f32[6,2,128,192]{3,2,1,0:T(8,128)}, f32[576,768]{1,0:T(8,128)}, f32[192,768]{1,0:T(8,128)}, f32[8,768]{1,0:T(8,128)}) custom-call(s32[6]{0:T(128)} %compare_select_fusion.6.perm, bf16[6,2,256,384]{3,2,1,0:T(8,128)(2,1)} %get-tuple-element.58.xg, bf16[6,256,768]{2,1,0:T(8,128)(2,1)} %get-tuple-element.64.n1, f32[8,768]{1,0:T(8,128)} %get-tuple-element.62.gbf, ...), custom_call_target="tpu_custom_call" | custom-call | flops 10000000000 | bytes 20971520 | tf_op jit(solution)/shard_map/back/pallas_call | solution.py:989
  192.8 0.0 copy-start.6
  192.8 0.0 copy-start.1
  192.8 2.6 convert_element_type.30
  195.5 0.0 copy-done.6
  195.5 0.7 convert_element_type.31
  196.2 0.0 copy-done.1
  196.2 0.0 copy-start
  196.2 1.1 convert_element_type.33
  197.4 1.0 copy-done
  198.3 1.1 convert_element_type.35
  199.4 0.0 copy-start.2
  199.4 0.0 all-reduce.4.cloned.1.call-update
  199.5 0.0 copy-start.5
  199.5 0.9 slice.61
  200.4 0.5 copy-done.2
  200.9 1.5 copy.28
  202.3 0.0 copy-done.5
  202.4 1.1 copy.27
  203.4 0.7 slice_multiply_fusion
  204.2 55.1 %psum.39 = f32[4,768]{1,0:T(4,128)S(1)} all-reduce(f32[4,768]{1,0:T(4,128)S(1)} %pad_maximum_fusion), channel_id=1, replica_groups=mesh['seq'=8,'head'=4] {'seq','head'}, use_global_device_ids=true, to_apply=%region_8.9 | all-reduce | flops 3072 | bytes 24576 | tf_op jit(solution)/shard_map/psum | solution.py:1141
  259.3 0.7 fusion.4
  259.9 92.2 %all-reduce.4.cloned.1.call-done = (bf16[768,3,192]{0,2,1:T(8,128)(2,1)}, bf16[192,768]{1,0:T(8,128)(2,1)}, bf16[768,768]{1,0:T(8,128)(2,1)}, bf16[768,768]{1,0:T(8,128)(2,1)}) async-done(((bf16[768,3,192]{0,2,1:T(8,128)(2,1)}, bf16[192,768]{1,0:T(8,128)(2,1)}, bf16[768,768]{1,0:T(8,128)(2,1)}, bf16[768,768]{1,0:T(8,128)(2,1)}), (bf16[768,3,192]{0,2,1:T(8,128)(2,1)}, bf16[192,768]{1,0:T(8,128)(2,1)}, ...) | async-done | bytes 3538960 | tf_op jit(solution)/shard_map/psum | solution.py:1144
  352.1 0.0 copy-start.3
  352.1 2.9 convert_element_type.34
  355.1 0.0 copy-done.3
  355.1 0.0 copy-start.4
  355.1 1.6 convert_element_type.36
  356.7 0.0 copy-start.8
  356.7 0.0 copy-done.4
  356.7 1.4 reshape.210
  358.0 0.0 copy-done.8
  358.0 0.9 convert_element_type.32
  (11 shorter events, 0.1 us)
Async XLA Ops:
  7.2 8.6 %copy-start.7 = (bf16[6,2,128,192]{2,3,1,0:T(8,128)(2,1)S(1)}, bf16[6,2,128,192]{2,3,1,0:T(8,128)(2,1)}, u32[]{:S(2)}) copy-start(bf16[6,2,128,192]{2,3,1,0:T(8,128)(2,1)} %param.25) | copy-start | bytes 1769476
  7.2 9.9 %copy-start.10 = (f32[192]{0:T(256)S(1)}, f32[192]{0:T(256)}, u32[]{:S(2)}) copy-start(f32[192]{0:T(256)} %param.17) | copy-start | bytes 2308
  7.2 9.9 %copy-start.11 = (f32[192]{0:T(256)S(1)}, f32[192]{0:T(256)}, u32[]{:S(2)}) copy-start(f32[192]{0:T(256)} %param.18) | copy-start | bytes 2308
  7.2 9.9 %copy-start.12 = (f32[192]{0:T(256)S(1)}, f32[192]{0:T(256)}, u32[]{:S(2)}) copy-start(f32[192]{0:T(256)} %param.21) | copy-start | bytes 2308
  7.2 9.9 %copy-start.13 = (f32[192]{0:T(256)S(1)}, f32[192]{0:T(256)}, u32[]{:S(2)}) copy-start(f32[192]{0:T(256)} %param.22) | copy-start | bytes 2308
  7.2 344.9 %all-reduce.4.cloned.1.call-start = ((), (), s32[]{:S(2)}) async-start(), calls=%async_computation | async-start | bytes 7077888 | tf_op jit(solution)/shard_map/psum | solution.py:1144
  17.0 0.7 copy-start.9
  192.8 2.6 copy-start.6
  192.8 3.4 copy-start.1
  196.2 2.1 copy-start
  199.4 1.4 copy-start.2
  199.5 2.9 copy-start.5
  352.1 2.9 copy-start.3
  355.1 1.6 copy-start.4
  356.7 1.4 copy-start.8
Sparse Core Ops, SparseCore 0:
  199.6 152.5 all-reduce.3

commit v2 on v1

--- a/solution.py
+++ b/solution.py
@@ -421,6 +421,78 @@
     return clean, own
 
 
+class Sum:
+    def __init__(self, at, src, res, gx, part, gz, xs, xr, zs, zr, cs, cr, fs, fr):
+        self.m = at.n // 2
+        self.lo = lax.rem(at.me, 2)
+        self.hi = lax.div(at.me, 2)
+        self.head = at.head
+        self.pair = (at.me + 1 - 2 * self.lo, at.head)
+        self.src, self.res, self.gx, self.part, self.gz = src, res, gx, part, gz
+        self.xs, self.xr, self.zs, self.zr = xs, xr, zs, zr
+        self.cs, self.cr, self.fs, self.fr = cs, cr, fs, fr
+
+    def at_z(self, k):
+        return (2 * k + self.lo, self.head)
+
+    def x(self, k):
+        return remote(self.src.at[1 - self.lo, k], self.gx.at[k], self.xs.at[k], self.xr.at[k], self.pair)
+
+    def z(self, k):
+        return remote(self.part.at[k], self.gz.at[self.hi], self.zs.at[k], self.zr.at[self.hi], self.at_z(k))
+
+    def z_in(self, k):
+        return remote(self.part.at[k], self.gz.at[k], self.zs.at[k], self.zr.at[k], self.at_z(k))
+
+    def c(self, k):
+        own = self.res.at[self.lo, self.hi]
+        return remote(own, own, self.cs.at[k], self.cr.at[self.hi], self.at_z(k))
+
+    def c_in(self, k):
+        part = self.res.at[self.lo, k]
+        return remote(part, part, self.cs.at[k], self.cr.at[k], self.at_z(k))
+
+    def f(self, k):
+        part = self.res.at[self.lo, k]
+        return remote(part, part, self.fs.at[k], self.fr.at[k], self.pair)
+
+    def others(self):
+        return [lax.rem(self.hi + d, self.m) for d in range(1, self.m)]
+
+    def begin(self):
+        each(self.m, lambda k: self.x(k).start())
+
+    def pass_on(self, k):
+        self.x(k).wait_recv()
+        self.part[k] = (self.src[self.lo, k].astype(F32) + self.gx[k].astype(F32)).astype(BF16)
+
+        @pl.when(k != self.hi)
+        def _():
+            self.z(k).start()
+
+    def reduce(self):
+        total = self.part[self.hi].astype(F32)
+        for k in self.others():
+            self.z_in(k).wait_recv()
+            total += self.gz[k].astype(F32)
+        self.res[self.lo, self.hi] = total.astype(BF16)
+        for k in self.others():
+            self.c(k).start()
+        self.f(self.hi).start()
+
+    def forward(self, d):
+        k = lax.rem(self.hi + d, self.m)
+        self.c_in(k).wait_recv()
+        self.f(k).start()
+
+    def finish(self):
+        each(self.m, lambda k: self.x(k).wait_send())
+        for k in self.others():
+            self.z(k).wait_send()
+            self.c(k).wait_send()
+        each(self.m, lambda k: self.f(k).wait())
+
+
 def front(n, perm, x_in, c_in, gb_in, w_t, wo_in, cos, sin, bounds,
           xg, cg, ag, wog, gbf, n1, qt, kvn, kvo, kvb, att, lse,
           own, land, gland, acc, mrow, lrow,
@@ -535,45 +607,55 @@
     wo_sib.start()
     wo_y.start()
 
-    def absorb(s, h, keys, values, lanes, allowed, first):
-        hd = slice(h * HEAD_DIM, (h + 1) * HEAD_DIM)
-        sc = dot(keys[hd], qt[s, hd, lanes], 0, 0)
-        sc = jnp.where(allowed, sc, masked_score)
-        top = jnp.max(sc, axis=0, keepdims=True)
-        if first:
-            new = top
-        else:
-            old = mrow[h : h + 1, lanes]
-            new = jnp.maximum(old, top)
-            scale = jnp.exp(old - new)
-        p = jnp.exp(sc - new)
-        total = jnp.sum(p, axis=0, keepdims=True)
-        add = dot(values[hd], p.astype(BF16), 1, 0)
-        mrow[h : h + 1, lanes] = new
-        if first:
-            lrow[h : h + 1, lanes] = total
-            acc[hd, lanes] = add
-        else:
-            lrow[h : h + 1, lanes] = lrow[h : h + 1, lanes] * scale + total
-            acc[hd, lanes] = acc[hd, lanes] * scale + add
-
-    every = slice(0, rows)
+    heads = [slice(h * HEAD_DIM, (h + 1) * HEAD_DIM) for h in range(hl)]
+    first_half = slice(0, length)
 
     def attend(s):
         start, end = bounds[s, 0:1], bounds[s, 1:2]
         clean, noisy = masks(me, length, start, end)
         kc, kn = kvo[s], kvn[s]
+        q = [qt[s, hd] for hd in heads]
+        sc = [dot(kc[hd], q[h], 0, 0) for h, hd in enumerate(heads)]
+        sn = [dot(kn[hd], q[h][:, :length], 0, 0) for h, hd in enumerate(heads)]
+        sc = [jnp.where(clean, v, masked_score) for v in sc]
+        sn = [jnp.where(noisy, v, masked_score) for v in sn]
+        top = []
         for h in range(hl):
-            absorb(s, h, kc[:feat], kc[feat:], every, clean, True)
-            absorb(s, h, kn[:feat], kn[feat:], slice(0, length), noisy, False)
+            tc = jnp.max(sc[h], axis=0, keepdims=True)
+            tn = jnp.max(sn[h], axis=0, keepdims=True)
+            top.append(
+                jnp.concatenate([jnp.maximum(tc[:, :length], tn), tc[:, length:]], axis=1)
+            )
+        pc = [jnp.exp(sc[h] - top[h]) for h in range(hl)]
+        pn = [jnp.exp(sn[h] - top[h][:, :length]) for h in range(hl)]
+        oc = [dot(kc[feat:][hd], pc[h].astype(BF16), 1, 0) for h, hd in enumerate(heads)]
+        on = [dot(kn[feat:][hd], pn[h].astype(BF16), 1, 0) for h, hd in enumerate(heads)]
+        for h, hd in enumerate(heads):
+            tc = jnp.sum(pc[h], axis=0, keepdims=True)
+            tn = jnp.sum(pn[h], axis=0, keepdims=True)
+            mrow[h : h + 1] = top[h]
+            lrow[h : h + 1] = jnp.concatenate([tc[:, :length] + tn, tc[:, length:]], axis=1)
+            acc[hd, first_half] = oc[h][:, :length] + on[h]
+            acc[hd, slice(length, rows)] = oc[h][:, length:]
 
         def one(j, carry):
             remote(kvo.at[s], kvb.at[s, j], ks.at[s, j], kr.at[s, j], at.sib).wait_recv()
             kv = kvb[s, j]
+            q = [qt[s, hd] for hd in heads]
+            old = [mrow[h : h + 1] for h in range(hl)]
+            total = [lrow[h : h + 1] for h in range(hl)]
             pos = lax.broadcasted_iota(jnp.int32, (length, rows), 0) + j * length
             allowed = pos >= start
-            for h in range(hl):
-                absorb(s, h, kv[:feat], kv[feat:], every, allowed, False)
+            sc = [dot(kv[hd], q[h], 0, 0) for h, hd in enumerate(heads)]
+            sc = [jnp.where(allowed, v, masked_score) for v in sc]
+            new = [jnp.maximum(old[h], jnp.max(sc[h], axis=0, keepdims=True)) for h in range(hl)]
+            p = [jnp.exp(sc[h] - new[h]) for h in range(hl)]
+            add = [dot(kv[feat:][hd], p[h].astype(BF16), 1, 0) for h, hd in enumerate(heads)]
+            scale = [jnp.exp(old[h] - new[h]) for h in range(hl)]
+            for h, hd in enumerate(heads):
+                mrow[h : h + 1] = new[h]
+                lrow[h : h + 1] = total[h] * scale[h] + jnp.sum(p[h], axis=0, keepdims=True)
+                acc[hd] = acc[hd] * scale[h] + add[h]
             return carry
 
         lax.fori_loop(at.lowest(s, me), me, one, 0)
@@ -631,8 +713,8 @@
 
 
 def middle(n, perm, xg, ag, cg, wog, gbf, wu, wd,
-           out, rl, rf, up_g, dn_g, gsum,
-           hid, n2, act, upre, ep, er, es, ey, ef, fp, fc, fh, fy, ob, osd,
+           out, rl, rf, gl, gsum,
+           up_g, dn_g, hid, n2, act, upre, ep, er, es, ey, ef, fp, fc, fh, fy, ob, osd,
            e1s, e1r, e2s, e2r, e3s, e3r, f1s, f1r, f2s, f2r, f3s, f3r):
     at = Place(n)
     slots, _, rows, half = xg.shape
@@ -722,14 +804,17 @@
 
     each(slots + 1, loop_two)
 
+    gl[0] = up_g[...].astype(BF16).reshape(gl.shape[1:])
+    gl[1] = dn_g[...].astype(BF16).reshape(gl.shape[1:])
+
     def loop_three(s):
         e_back(s).wait_recv()
         e = ef[s].astype(F32)
         h = whole_rows(hid, s)
         mean, inv = row_stats(h)
         xh = (h - mean) * inv
-        gsum[0:1] += jnp.sum(e * xh, axis=0, keepdims=True)
-        gsum[1:2] += jnp.sum(e, axis=0, keepdims=True)
+        gsum[2:3] += jnp.sum(e * xh, axis=0, keepdims=True)
+        gsum[3:4] += jnp.sum(e, axis=0, keepdims=True)
         g = e * gbf[2:3]
         first = jnp.sum(g, axis=1, keepdims=True) / D
         second = jnp.sum(g * xh, axis=1, keepdims=True) / D
@@ -781,19 +866,25 @@
     each(slots, place)
 
 
-def back(n, perm, xg, n1, gbf, w_t, wo, rl, rf, att, lse, qt, kvn, kvo, kvb, cos, sin, bounds,
-         ig, qg, og, gsum,
-         do, dq, drow, dkv, dst, dla, qp, ep, er, st, sr_, es, ss_, ey, sy, ib, isd,
-         ks, kr, a1s, a1r, b1s, b1r, a2s, a2r, b2s, b2r, a3s, a3r):
+def back(n, perm, xg, n1, gbf, w_t, wo, rl, rf, att, lse, qt, kvn, kvo, kvb, cos, sin, bounds, gl, gs_two,
+         ig, res1, res2, res3, gains,
+         og, qq, qkv, gsum, do, dq, drow, dkv, dst, dla, qp, ep, er, st, sr_, es, ss_, ey, sy, ib, isd,
+         src2, src3, gx1, pt1, gz1, gx2, pt2, gz2, gx3, pt3, gz3, gh, gq, gf,
+         ks, kr, a1s, a1r, b1s, b1r, a2s, a2r, b2s, b2r, a3s, a3r, hs, hr, qs, qr, *sums):
     at = Place(n)
     slots, _, rows, half = xg.shape
+    sum1 = Sum(at, gl, res1, gx1, pt1, gz1, *sums[0:8])
+    sum2 = Sum(at, src2, res2, gx2, pt2, gz2, *sums[8:16])
+    sum3 = Sum(at, src3, res3, gx3, pt3, gz3, *sums[16:24])
+    m = n // 2
     length = rows // 2
     feat = half // 2
     hl = feat // HEAD_DIM
     core, y, me = at.core, at.y, at.me
     mine = pl.ds(length * core, length)
     other = pl.ds(length * (1 - core), length)
-    at.greet([at.sib, at.yp], True)
+    at.greet([at.sib, at.yp, at.diag], True)
+    sum1.begin()
     every = slice(0, rows)
 
     def kv_copy(s, j):
@@ -815,22 +906,28 @@
         return remote(isd.at[s], ib.at[s, core], a3s.at[s], a3r.at[s], at.sib)
 
     og[...] = jnp.zeros_like(og)
-    qg[...] = jnp.zeros_like(qg)
+    qq[...] = jnp.zeros_like(qq)
+    qkv[...] = jnp.zeros_like(qkv)
     gsum[...] = jnp.zeros_like(gsum)
     drow[...] = jnp.zeros_like(drow)
 
-    def head_grads(s, h, keys, values, lanes, allowed):
-        hd = slice(h * HEAD_DIM, (h + 1) * HEAD_DIM)
-        q = qt[s, hd, lanes]
-        d_out = do[hd, lanes]
-        sc = dot(keys[hd], q, 0, 0)
-        p = jnp.exp(jnp.where(allowed, sc, masked_score) - lse[s, h : h + 1, lanes])
-        dp = dot(values[hd], d_out, 0, 0)
-        ds = (p * (dp - drow[h : h + 1, lanes])).astype(BF16)
-        dq_add = dot(keys[hd], ds, 1, 0)
-        dk = dot(q, ds, 1, 1)
-        dv = dot(d_out, p.astype(BF16), 1, 1)
-        return dq_add, dk, dv
+    heads = [slice(h * HEAD_DIM, (h + 1) * HEAD_DIM) for h in range(hl)]
+
+    def head_grads(s, kv, lanes, allowed):
+        q = [qt[s, hd, lanes] for hd in heads]
+        d_out = [do[hd, lanes] for hd in heads]
+        sc = [dot(kv[hd], q[h], 0, 0) for h, hd in enumerate(heads)]
+        dp = [dot(kv[feat:][hd], d_out[h], 0, 0) for h, hd in enumerate(heads)]
+        p = [
+            jnp.exp(jnp.where(allowed, sc[h], masked_score) - lse[s, h : h + 1, lanes])
+            for h in range(hl)
+        ]
+        ds = [(p[h] * (dp[h] - drow[h : h + 1, lanes])).astype(BF16) for h in range(hl)]
+        dv = [dot(d_out[h], p[h].astype(BF16), 1, 1) for h in range(hl)]
+        dk = [dot(q[h], ds[h], 1, 1) for h in range(hl)]
+        dq_add = [dot(kv[hd], ds[h], 1, 0) for h, hd in enumerate(heads)]
+        together = [jnp.concatenate(v, axis=0) for v in (dq_add, dk, dv)]
+        return together
 
     def attend_back(s):
         low_rows = rl[s]
@@ -845,40 +942,42 @@
         clean, noisy = masks(me, length, start, end)
         kc, kn = kvo[s], kvn[s]
         first = slice(0, length)
-        noisy_k = []
-        for h in range(hl):
-            hd = slice(h * HEAD_DIM, (h + 1) * HEAD_DIM)
-            vd = slice(feat + h * HEAD_DIM, feat + (h + 1) * HEAD_DIM)
-            dqa, dk, dv = head_grads(s, h, kc[:feat], kc[feat:], every, clean)
-            dq[hd] = dqa
-            dkv[s, hd] = dk
-            dkv[s, vd] = dv
-            dqa, dk, dv = head_grads(s, h, kn[:feat], kn[feat:], first, noisy)
-            dq[hd, first] += dqa
-            noisy_k.append(dk)
-            qp[s, 2 * feat + h * HEAD_DIM : 2 * feat + (h + 1) * HEAD_DIM, first] = dv.astype(BF16)
-        qp[s, feat : 2 * feat, first] = turn(
-            jnp.concatenate(noisy_k, axis=0), cos[:, :length], -sin[:, :length]
-        ).astype(BF16)
+        dqa, dk, dv = head_grads(s, kc, every, clean)
+        dqn, dkn, dvn = head_grads(s, kn, first, noisy)
+        dq[...] = dqa
+        dq[:, first] += dqn
+        dkv[s, :feat] = dk
+        dkv[s, feat:] = dv
+        qp[s, 2 * feat :, first] = dvn.astype(BF16)
+        qp[s, feat : 2 * feat, first] = turn(dkn, cos[:, :length], -sin[:, :length]).astype(BF16)
 
         def one(j, carry):
             kv = kvb[s, j]
             pos = lax.broadcasted_iota(jnp.int32, (length, rows), 0) + j * length
             allowed = pos >= start
-            for h in range(hl):
-                hd = slice(h * HEAD_DIM, (h + 1) * HEAD_DIM)
-                vd = slice(feat + h * HEAD_DIM, feat + (h + 1) * HEAD_DIM)
-                dqa, dk, dv = head_grads(s, h, kv[:feat], kv[feat:], every, allowed)
-                dq[hd] += dqa
-                dst[s, j, hd] = dk.astype(BF16)
-                dst[s, j, vd] = dv.astype(BF16)
+            dqa, dk, dv = head_grads(s, kv, every, allowed)
+            dq[...] += dqa
+            dst[s, j, :feat] = dk.astype(BF16)
+            dst[s, j, feat:] = dv.astype(BF16)
             kv_copy(s, j).start()
             return carry
 
         lax.fori_loop(at.lowest(s, me), me, one, 0)
         qp[s, :feat] = (turn(dq[...], cos[...], -sin[...]) * HEAD_DIM**-0.5).astype(BF16)
-
-    each(slots, attend_back)
+        qq[...] += dot(qp[s, :feat], n1[s], 1, 0)
+
+    def loop_one(t):
+        attend_back(t)
+
+        @pl.when(jnp.logical_and(t >= 1, t <= m))
+        def _():
+            sum1.pass_on(t - 1)
+
+    each(slots, loop_one)
+    src2[0] = og[...].astype(BF16).reshape(src2.shape[1:])
+    src2[1] = qq[...].astype(BF16).reshape(src2.shape[1:])
+    sum2.begin()
+    sum1.reduce()
 
     def project_back(s):
         for d in range(1, n):
@@ -894,7 +993,7 @@
         qp[s, feat : 2 * feat, late] = turn(total[:feat], cos[:, late], -sin[:, late]).astype(BF16)
         qp[s, 2 * feat :, late] = total[feat:].astype(BF16)
         pre = qp[s]
-        qg[...] += dot(pre, n1[s], 1, 0)
+        qkv[...] += dot(pre[feat:], n1[s], 1, 0)
         e = dot(pre, w_t[...], 0, 0)
         x = whole_rows(xg, s).astype(F32)
         mean, inv = row_stats(x)
@@ -931,7 +1030,34 @@
         def _():
             send_on(t - 1)
 
+        @pl.when(jnp.logical_and(t >= 1, t < m))
+        def _():
+            sum1.forward(t)
+
+        @pl.when(jnp.logical_and(t >= 1, t <= m))
+        def _():
+            sum2.pass_on(t - 1)
+
+        @pl.when(t == m + 1)
+        def _():
+            sum2.reduce()
+
     each(slots + 1, loop_two)
+    grads = qkv[...].astype(BF16)
+    src3[0] = grads[:feat].reshape(src3.shape[1:])
+    src3[1] = grads[feat:].reshape(src3.shape[1:])
+    sum3.begin()
+    h_copies = [
+        remote(gsum, gh.at[k], hs.at[k], hr.at[k], d) for k, d in enumerate((at.sib, at.yp, at.diag))
+    ]
+    for copy in h_copies:
+        copy.start()
+
+    def share(i):
+        return remote(gf, gq.at[me], qs.at[i], qr.at[me], (i, at.head))
+
+    def share_in(i):
+        return remote(gf, gq.at[i], qs.at[i], qr.at[i], (i, at.head))
 
     def input_part(s):
         e_y(s).wait_recv()
@@ -959,7 +1085,41 @@
 
         i_back(s).start()
 
-    each(slots, input_part)
+    def loop_three(t):
+        input_part(t)
+
+        @pl.when(t < m - 1)
+        def _():
+            sum2.forward(t + 1)
+
+        @pl.when(t >= slots - m)
+        def _():
+            sum3.pass_on(t - (slots - m))
+
+        @pl.when(t == 0)
+        def _():
+            for copy in h_copies:
+                copy.wait()
+            total = gsum[...] + gh[0] + gh[1] + gh[2]
+            row = lax.broadcasted_iota(jnp.int32, total.shape, 0)
+            total = jnp.where(row < 2, total, gs_two[...])
+            for h in range(4):
+
+                @pl.when(at.head == h)
+                def _():
+                    gf[...] = total[:, h * feat : (h + 1) * feat]
+
+            gq[me] = gf[...]
+            for d in range(1, n):
+                share(lax.rem(me + d, n)).start()
+
+    each(slots, loop_three)
+    sum3.reduce()
+    for d in range(1, n):
+        share_in(lax.rem(me + d, n)).wait_recv()
+    gains[...] = jnp.sum(gq[...], axis=0)
+    for d in range(1, m):
+        sum3.forward(d)
 
     def finish(s):
         e_core(s).wait_send()
@@ -975,6 +1135,11 @@
         lax.fori_loop(at.lowest(s, me), me, sent, 0)
 
     each(slots, finish)
+
+    for part in (sum1, sum2, sum3):
+        part.finish()
+    for d in range(1, n):
+        share(lax.rem(me + d, n)).wait_send()
 
     def place(s):
         ig[s] = ib[perm[s]]
@@ -1076,7 +1241,8 @@
     )
     wide = VMEM((slots, rows, D), BF16)
     part = VMEM((slots, length, D), BF16)
-    outputs, rl, rf, up_grad, down_grad, gsum2 = call(
+    m = n // 2
+    outputs, rl, rf, gl, gsum2 = call(
         middle,
         1,
         n,
@@ -1085,11 +1251,12 @@
             ((slots, 2, length, feat), BF16),
             ((slots, rows, D), BF16),
             ((slots, length, half), F32),
-            (w_up.shape, F32),
-            (w_down.shape, F32),
+            ((2, m, D // m, D), BF16),
             ((8, D), F32),
         ],
         [
+            VMEM(w_up.shape, F32),
+            VMEM(w_down.shape, F32),
             VMEM((slots, 2, rows, half), F32),
             *[wide] * 4,
             *[part] * 3,
@@ -1104,18 +1271,25 @@
         15 * 10**9,
     )
     stat = VMEM((slots, 8, length), F32)
-    input_grad, qkv_grad, out_grad, gsum1 = call(
+    quarter = [VMEM((m, D // m, D), BF16)] * 3
+    small = (m, feat // m, D)
+    input_grad, res1, res2, res3, gain_grads = call(
         back,
         2,
         n,
-        (perm, xg, n1, gbf, w_t, w_out, rl, rf, att, lse, qt, kvn, kvo, kvb, cos, sin, bounds),
+        (perm, xg, n1, gbf, w_t, w_out, rl, rf, att, lse, qt, kvn, kvo, kvb, cos, sin, bounds, gl, gsum2),
         [
             ((slots, 2, length, feat), F32),
-            ((3 * feat, D), F32),
-            ((feat, D), F32),
-            ((8, D), F32),
+            ((2, m, D // m, D), BF16),
+            ((2, *small), BF16),
+            ((2, *small), BF16),
+            ((8, feat), F32),
         ],
         [
+            VMEM((feat, D), F32),
+            VMEM((feat, D), F32),
+            VMEM((half, D), F32),
+            VMEM((8, D), F32),
             VMEM((feat, rows), BF16),
             VMEM((feat, rows), F32),
             VMEM((8, rows), F32),
@@ -1133,26 +1307,34 @@
             stat,
             VMEM((slots, 2, length, feat), F32),
             VMEM((slots, length, feat), F32),
+            *[VMEM((2, *small), BF16)] * 2,
+            *quarter,
+            *[VMEM(small, BF16)] * 6,
+            VMEM((3, 8, D), F32),
+            VMEM((n, 8, feat), F32),
+            VMEM((8, feat), F32),
             *[sem((slots, n))] * 2,
             *[sem((slots,))] * 10,
+            *[sem((3,))] * 2,
+            *[sem((n,))] * 2,
+            *[sem((m,))] * 24,
         ],
         10 * 10**9,
     )
-    gains_sum = lax.psum(jnp.concatenate([gsum1[:2], gsum2[:2] * 0.25], axis=0), ("seq", "head"))
-    gains_own = lax.dynamic_slice(gains_sum, (0, lax.axis_index("head") * feat), (4, feat))
-    up_low, down_low = lax.psum((up_grad.astype(BF16), down_grad.astype(BF16)), "seq")
-    qkv_low, out_low = lax.psum((qkv_grad.astype(BF16), out_grad.astype(BF16)), "seq")
+    up_grad, down_grad = res1.reshape(2, D, D).astype(F32)
+    out_grad, q_grad = res2.reshape(2, feat, D).astype(F32)
+    qkv_grad = jnp.concatenate([q_grad[None], res3.reshape(2, feat, D).astype(F32)], axis=0)
     return (
         outputs,
         input_grad,
-        qkv_low.astype(F32).T.reshape(w_qkv.shape),
-        out_low.astype(F32),
-        up_low.astype(F32),
-        down_low.astype(F32),
-        gains_own[0],
-        gains_own[1],
-        gains_own[2],
-        gains_own[3],
+        jnp.transpose(qkv_grad, (2, 0, 1)),
+        out_grad,
+        up_grad,
+        down_grad,
+        gain_grads[0],
+        gain_grads[1],
+        gain_grads[2],
+        gain_grads[3],
     )
 
 

time: 366 us -> 286 us (0.78)
  waiting for transfers between devices: 92.2 us -> 0 us
  Pallas kernels: 175 us -> 263 us
  blocking collectives: 55.1 us -> 0 us
  between operations: 14.3 us -> 0.81 us
  other arithmetic: 16.7 us -> 5 us
  local copies, waits for them, and re-layouts: 12.3 us -> 16.6 us
    psum x1 -> x0, waiting for transfers between devices: 92.2 us -> none  [body(): lax.psum((qkv_grad.astype(BF16), out_grad.astype(BF16)), 'seq')]
    pallas_call x3, Pallas kernels: 175 us -> 263 us  [call(): pl.pallas_call(functools.partial(kernel, n), out_shape=[jax.ShapeDtypeStr...]
    psum x1 -> x0, blocking collectives: 55.1 us -> none  [body(): lax.psum(jnp.concatenate([gsum1[:2], gsum2[:2] * 0.25], axis=0), ('seq',...]
    convert_element_type x7 -> x1, other arithmetic: 11 us -> 0.12 us  [body(): res3.reshape(2, feat, D).astype(F32)]
    unnamed x34 -> x20, local copies, waits for them, and re-layouts: 8.7 us -> 9.69 us
  transfers between devices with their start and end apart: 1 -> 0, of which waited for: 1 -> 0; matrix products, arithmetic and copies ran while one was open for 1% -> 0% of each run, Pallas kernels for 0% -> 0%
where the time goes in v2:
time: 286 us
  Pallas kernels  263 us (92%)
  local copies, waits for them, and re-layouts  16.6 us (6%)
  other arithmetic  5 us (2%)
    pallas_call x3, Pallas kernels, call(): pl.pallas_call(functools.partial(kernel, n), out_shape=[jax.ShapeDtypeStr...  263 us
    unnamed x20, local copies, waits for them, and re-layouts  9.69 us

profile of v2, /device:TPU:0, one launch (start us, length us, event | category | flops | bytes accessed | tf_op | source)
XLA Modules:
  0.0 285.9 jit_solution(4388408231004866606)
XLA Ops:
  0.6 0.0 copy-start.4
  0.7 0.9 slice_reduce_fusion
  1.5 0.7 iota_reduce_fusion
  2.2 1.2 compare_select_fusion.6.perm
  3.4 0.7 fusion.2
  4.0 0.8 reduce_window_sum.11
  4.9 0.6 gather_fusion
  5.4 0.1 fusion.1
  5.5 1.3 concatenate.10.gb_in
  6.9 0.1 multiply_sine_fusion
  7.1 0.6 copy.33
  7.7 0.6 copy.34
  8.4 0.0 copy-start.5
  8.4 2.2 copy.25.x_in
  10.6 0.0 copy-done.4
  10.6 1.2 copy.26.c_in
  11.8 0.0 copy-done.5
  11.8 67.9 %front.1 = (bf16[6,2,256,384]{3,2,1,0:T(8,128)(2,1)}, bf16[6,2,256,384]{3,2,1,0:T(8,128)(2,1)}, bf16[6,2,256,384]{3,2,1,0:T(8,128)(2,1)}, bf16[768,768]{1,0:T(8,...) custom-call(s32[6]{0:T(128)} %compare_select_fusion.6.perm, ...), custom_call_target="tpu_custom_call" | custom-call | flops 3000000000 | bytes 20971520 | tf_op jit(solution)/shard_map/front/pallas_call | solution.py:1154
  79.7 53.7 %middle.1 = (bf16[6,2,128,192]{3,2,1,0:T(8,128)(2,1)}, bf16[6,256,768]{2,1,0:T(8,128)(2,1)}, f32[6,128,384]{2,1,0:T(8,128)}, bf16[2,4,192,768]{3,2,1,0:T(8,128)(2,1)}, f32[8,768]{1,0:T(8,128)}) custom-call(s32[6]{0:T(128)} %compare_select_fusion.6.perm, bf16[6,2,256,384]{3,2,1,0:T(8,128)(2,1)} %get-tuple-element.58.xg, ...), custom_call_target="tpu_custom_call" | custom-call | flops 15000000512 | bytes 20971520 | tf_op jit(solution)/shard_map/middle/pallas_call | solution.py:1154
  133.4 0.0 copy-start.2
  133.4 141.9 %back.1 = (f32[6,2,128,192]{3,2,1,0:T(8,128)}, bf16[2,4,192,768]{3,2,1,0:T(8,128)(2,1)}, bf16[2,4,48,768]{3,2,1,0:T(8,128)(2,1)}, bf16[2,4,48,768]{3,2,1,0:T(8,128)(2,1)}, f32[8,192]{1,0:T(8,128)}) custom-call(s32[6]{0:T(128)} %compare_select_fusion.6.perm, bf16[6,2,256,384]{3,2,1,0:T(8,128)(2,1)} %get-tuple-element.58.xg, ...), custom_call_target="tpu_custom_call" | custom-call | flops 10000000000 | bytes 20971520 | tf_op jit(solution)/shard_map/back/pallas_call | solution.py:1154
  275.3 0.0 copy-done.2
  275.3 0.0 copy-start.6
  275.3 0.0 copy-start.3
  275.3 1.1 copy.27
  276.4 0.0 copy-start.1
  276.4 3.0 %copy.28 = f32[6,2,128,192]{2,3,1,0:T(8,128)} copy(f32[6,2,128,192]{3,2,1,0:T(8,128)} %get-tuple-element.91) | data formatting | bytes 2359296
  279.4 0.0 copy-done.6
  279.4 0.6 fusion.6
  279.9 0.0 copy-done.3
  279.9 0.1 bitcast_convert_fusion
  280.1 0.0 copy-done.1
  280.1 0.9 fusion.5
  281.0 0.0 copy-start
  281.0 1.3 maximum_bitcast_fusion
  282.3 1.0 copy-done
  283.3 2.6 fusion.4
  (10 shorter events, 0.1 us)
Async XLA Ops:
  0.6 10.0 %copy-start.4 = (bf16[6,2,128,192]{2,3,1,0:T(8,128)(2,1)S(1)}, bf16[6,2,128,192]{2,3,1,0:T(8,128)(2,1)}, u32[]{:S(2)}) copy-start(bf16[6,2,128,192]{2,3,1,0:T(8,128)(2,1)} %param.25) | copy-start | bytes 1769476
  8.4 3.4 %copy-start.5 = (s32[6,8,256]{2,1,0:T(8,128)}, s32[6,8,256]{2,1,0:T(8,128)S(1)}, u32[]{:S(2)}) copy-start(s32[6,8,256]{2,1,0:T(8,128)S(1)} %scatter.9.bounds) | copy-start | bytes 147460
  133.4 141.9 %copy-start.2 = (bf16[6,2,128,192]{3,2,1,0:T(8,128)(2,1)S(1)}, bf16[6,2,128,192]{3,2,1,0:T(8,128)(2,1)}, u32[]{:S(2)}) copy-start(bf16[6,2,128,192]{3,2,1,0:T(8,128)(2,1)} %get-tuple-element.90) | copy-start | bytes 1769476
  275.3 4.1 %copy-start.6 = (f32[8,192]{1,0:T(8,128)S(1)}, f32[8,192]{1,0:T(8,128)}, u32[]{:S(2)}) copy-start(f32[8,192]{1,0:T(8,128)} %get-tuple-element.79) | copy-start | bytes 18436
  275.3 4.6 %copy-start.3 = (bf16[2,4,48,768]{3,2,1,0:T(8,128)(2,1)S(1)}, bf16[2,4,48,768]{3,2,1,0:T(8,128)(2,1)}, u32[]{:S(2)}) copy-start(bf16[2,4,48,768]{3,2,1,0:T(8,128)(2,1)} %get-tuple-element.77) | copy-start | bytes 1769476
  276.4 3.7 %copy-start.1 = (bf16[2,4,48,768]{3,2,1,0:T(8,128)(2,1)S(1)}, bf16[2,4,48,768]{3,2,1,0:T(8,128)(2,1)}, u32[]{:S(2)}) copy-start(bf16[2,4,48,768]{3,2,1,0:T(8,128)(2,1)} %get-tuple-element.76) | copy-start | bytes 1769476
  281.0 2.3 copy-start

commit v3 on v0

--- a/solution.py
+++ b/solution.py
@@ -1,6 +1,11 @@
+import functools
+import types
+
 import jax
 import jax.numpy as jnp
 from jax import lax
+from jax.experimental import pallas as pl
+from jax.experimental.pallas import tpu as pltpu
 from jax.sharding import PartitionSpec as P
 
 D = 768
@@ -11,6 +16,13 @@
 norm_eps = 1e-05
 masked_score = -1e30
 rotary_base = 10000.0
+
+MESH = pl.DeviceIdType.MESH
+VMEM = pltpu.VMEM
+F32 = jnp.float32
+BF16 = jnp.bfloat16
+ROWS_LIMIT = 16 << 20
+VMEM_LIMIT = 63 << 20
 
 
 def passed_along(block, axis, distance):
@@ -103,7 +115,7 @@
     return (new_max, new_sum, run_acc * factor[..., None] + added)
 
 
-def body(
+def gathered_body(
     inputs,
     doc_lengths,
     attn_gain,
@@ -327,6 +339,948 @@
     )
 
 
+def dot(a, b, ca, cb):
+    return lax.dot_general(a, b, (((ca,), (cb,)), ((), ())), preferred_element_type=F32)
+
+
+def remote(src, dst, send, recv, device):
+    return pltpu.make_async_remote_copy(
+        src_ref=src, dst_ref=dst, send_sem=send, recv_sem=recv, device_id=device, device_id_type=MESH
+    )
+
+
+class Place:
+    def __init__(self, n):
+        self.n = n
+        self.me = lax.axis_index("seq")
+        self.head = lax.axis_index("head")
+        self.core = lax.rem(self.head, 2)
+        self.y = lax.div(self.head, 2)
+        self.sib = (self.me, self.y * 2 + 1 - self.core)
+        self.yp = (self.me, (1 - self.y) * 2 + self.core)
+        self.diag = (self.me, (1 - self.y) * 2 + 1 - self.core)
+        self.half = n // 2
+        self.band = max(1, n // 8)
+
+    def lowest(self, slot, i):
+        near = i - self.band
+        short = jnp.where(i >= self.half, jnp.minimum(near, self.half), near)
+        return jnp.where(slot == 0, 0, jnp.maximum(short, 0))
+
+    def spot(self, slot, block, other):
+        window = self.half + self.band
+        near = self.half + lax.rem(other, self.band)
+        late = jnp.where(block >= self.half, other - self.half, near)
+        return jnp.where(slot == 0, other, self.n + (slot - 1) * window + late)
+
+    def spots(self, slots):
+        return self.n + (slots - 1) * (self.half + self.band)
+
+    def greet(self, near, everyone):
+        bar = pltpu.get_barrier_semaphore()
+        for d in near:
+            pl.semaphore_signal(bar, inc=1, device_id=d, device_id_type=MESH)
+        count = len(near)
+        if everyone:
+            for d in range(1, self.n):
+                there = lax.rem(self.me + d, self.n)
+                pl.semaphore_signal(bar, inc=1, device_id=(there, self.head), device_id_type=MESH)
+            count += self.n - 1
+        pl.semaphore_wait(bar, count)
+
+
+def each(count, step):
+    def run(i, carry):
+        step(i)
+        return carry
+
+    lax.fori_loop(0, count, run, 0)
+
+
+def row_stats(x):
+    mean = jnp.sum(x, axis=1, keepdims=True) / D
+    var = jnp.sum(x * x, axis=1, keepdims=True) / D - mean * mean
+    return mean, lax.rsqrt(var + norm_eps)
+
+
+def whole_rows(ref, s):
+    return jnp.concatenate([ref[s, 0], ref[s, 1]], axis=1)
+
+
+def turn(v, cosine, sine):
+    parts = []
+    for h in range(v.shape[0] // HEAD_DIM):
+        a = v[h * 64 : h * 64 + 32]
+        b = v[h * 64 + 32 : h * 64 + 64]
+        parts += [a * cosine - b * sine, b * cosine + a * sine]
+    return jnp.concatenate(parts, axis=0)
+
+
+def masks(me, length, start, end):
+    shape = (length, 2 * length)
+    key = lax.broadcasted_iota(jnp.int32, shape, 0)
+    row = lax.broadcasted_iota(jnp.int32, shape, 1)
+    noisy = row < length
+    at = jnp.where(noisy, row, row - length)
+    key_block = key >> 4
+    row_block = at >> 4
+    pos = key + me * length
+    same = jnp.logical_and(pos >= start, pos < end)
+    clean = jnp.logical_and(same, key_block < row_block + jnp.where(noisy, 0, 1))
+    own = jnp.logical_and(same, key_block == row_block)[:, :length]
+    return clean, own
+
+
+class Sum:
+    def __init__(self, at, src, res, gx, part, gz, own, xs, xr, zs, zr, cs, cr, fs, fr, ls):
+        self.m = at.n // 2
+        self.lo = lax.rem(at.me, 2)
+        self.hi = lax.div(at.me, 2)
+        self.head = at.head
+        self.pair = (at.me + 1 - 2 * self.lo, at.head)
+        self.src, self.res, self.gx, self.part, self.gz = src, res, gx, part, gz
+        self.xs, self.xr, self.zs, self.zr = xs, xr, zs, zr
+        self.cs, self.cr, self.fs, self.fr, self.ls = cs, cr, fs, fr, ls
+        self.own = own
+
+    def piece(self, half, k):
+        size = self.gx.shape[1]
+        return half, pl.ds(pl.multiple_of(k * size, 16), size)
+
+    def at_z(self, k):
+        return (2 * k + self.lo, self.head)
+
+    def x(self, k):
+        return remote(self.src.at[self.piece(1 - self.lo, k)], self.gx.at[k], self.xs.at[k], self.xr.at[k], self.pair)
+
+    def z(self, k):
+        return remote(self.part.at[k], self.gz.at[self.hi], self.zs.at[k], self.zr.at[self.hi], self.at_z(k))
+
+    def z_in(self, k):
+        return remote(self.part.at[k], self.gz.at[k], self.zs.at[k], self.zr.at[k], self.at_z(k))
+
+    def c(self, k):
+        there = self.res.at[self.lo, self.hi]
+        return remote(self.own, there, self.cs.at[k], self.cr.at[self.hi], self.at_z(k))
+
+    def c_in(self, k):
+        part = self.res.at[self.lo, k]
+        return remote(part, part, self.cs.at[k], self.cr.at[k], self.at_z(k))
+
+    def f(self, k):
+        part = self.res.at[self.lo, k]
+        return remote(part, part, self.fs.at[k], self.fr.at[k], self.pair)
+
+    def f_own(self):
+        there = self.res.at[self.lo, self.hi]
+        return remote(self.own, there, self.fs.at[self.hi], self.fr.at[self.hi], self.pair)
+
+    def keep(self):
+        return pltpu.make_async_copy(self.own, self.res.at[self.lo, self.hi], self.ls)
+
+    def others(self):
+        return [lax.rem(self.hi + d, self.m) for d in range(1, self.m)]
+
+    def begin(self):
+        each(self.m, lambda k: self.x(k).start())
+
+    def pass_on(self, k):
+        self.x(k).wait_recv()
+        self.part[k] = (self.src[self.piece(self.lo, k)].astype(F32) + self.gx[k].astype(F32)).astype(BF16)
+
+        @pl.when(k != self.hi)
+        def _():
+            self.z(k).start()
+
+    def reduce(self):
+        total = self.part[self.hi].astype(F32)
+        for k in self.others():
+            self.z_in(k).wait_recv()
+            total += self.gz[k].astype(F32)
+        self.own[...] = total.astype(BF16)
+        self.keep().start()
+        for k in self.others():
+            self.c(k).start()
+        self.f_own().start()
+
+    def forward(self, d):
+        k = lax.rem(self.hi + d, self.m)
+        self.c_in(k).wait_recv()
+        self.f(k).start()
+
+    def finish(self):
+        each(self.m, lambda k: self.x(k).wait_send())
+        for k in self.others():
+            self.z(k).wait_send()
+            self.c(k).wait_send()
+            self.f(k).wait()
+        self.f_own().wait()
+        self.keep().wait()
+
+
+def layer(n, names, *refs):
+    r = types.SimpleNamespace(**dict(zip(names, refs)))
+    at = Place(n)
+    slots, rows, feat = r.x_in.shape
+    length = rows // 2
+    half = 2 * feat
+    hl = feat // HEAD_DIM
+    m = n // 2
+    core, y, me = at.core, at.y, at.me
+    mine = pl.ds(length * core, length)
+    other = pl.ds(length * (1 - core), length)
+    early, late = slice(0, length), slice(length, rows)
+    heads = [slice(h * HEAD_DIM, (h + 1) * HEAD_DIM) for h in range(hl)]
+    fulls = (r.xg, r.cg, r.ag)
+    owns = (r.x_in, r.c_in, r.own_att)
+    lands = (r.land.at[0], r.land.at[1], r.land.at[0])
+    quarter = D // m
+    sum1 = Sum(
+        at, r.gl, r.res1, r.gx1, r.act.at[:m, :quarter], r.gz1, r.own1, *[getattr(r, "u%d" % i) for i in range(9)]
+    )
+    src2 = r.act.at[m : m + 2, :feat]
+    sum2 = Sum(at, src2, r.res2, r.gx2, r.pt2, r.gz2, r.own2, *[getattr(r, "v%d" % i) for i in range(9)])
+    sum3 = Sum(at, r.src3, r.res3, r.gx3, r.pt3, r.gz3, r.own3, *[getattr(r, "w%d" % i) for i in range(9)])
+
+    def sib_copy(k, s):
+        return remote(owns[k].at[s], lands[k].at[s], r.ss.at[k, s], r.sr.at[k, s], at.sib)
+
+    def build(k, s):
+        a, b = owns[k][s], lands[k][s]
+
+        @pl.when(core == 0)
+        def _():
+            fulls[k][s, y] = jnp.concatenate([a, b], axis=1)
+
+        @pl.when(core == 1)
+        def _():
+            fulls[k][s, y] = jnp.concatenate([b, a], axis=1)
+
+    def y_copy(k, s):
+        part = fulls[k].at[s, y, mine]
+        return remote(part, part, r.ys.at[k, s], r.yr.at[k, s], at.yp)
+
+    def f_copy(k, s):
+        part = fulls[k].at[s, 1 - y, mine]
+        return remote(part, part, r.fs.at[k, s], r.fr.at[k, s], at.sib)
+
+    def kv_copy(s, i):
+        return remote(r.kvo.at[s], r.kvb.at[at.spot(s, me, me)], r.ks.at[s, i], r.kr.at[s, me], (i, at.head))
+
+    def kv_in(s, j):
+        return remote(r.kvo.at[s], r.kvb.at[at.spot(s, j, j)], r.ks.at[s, j], r.kr.at[s, j], (j, at.head))
+
+    def dkv_copy(s, j):
+        return remote(
+            r.kvb.at[at.spot(s, j, j)], r.dla.at[at.spot(s, j, me)], r.ds.at[s, j], r.dr.at[s, me], (j, at.head)
+        )
+
+    def dkv_in(s, i):
+        here = r.dla.at[at.spot(s, me, i)]
+        return remote(here, here, r.ds.at[s, i], r.dr.at[s, i], (i, at.head))
+
+    def readers(s, step):
+        for d in range(1, n):
+            i = me + d
+
+            @pl.when(jnp.logical_and(i < n, at.lowest(s, i) <= me))
+            def _():
+                step(i)
+
+    def e_core(s):
+        return remote(r.ep.at[s, other], r.er.at[s], r.e1s.at[s], r.e1r.at[s], at.sib)
+
+    def e_y(s):
+        return remote(r.er.at[s], r.ey.at[s], r.e2s.at[s], r.e2r.at[s], at.yp)
+
+    def e_back(s):
+        return remote(r.ey.at[s], r.eb.at[s], r.e3s.at[s], r.e3r.at[s], at.sib)
+
+    def held(first, s, k):
+        return (s, pl.ds(first, length), pl.ds(pl.multiple_of(k * half, 128), half))
+
+    def f_core(s):
+        return remote(r.ag.at[s, :, other], r.fc.at[s], r.f1s.at[s], r.f1r.at[s], at.sib)
+
+    def f_y(s):
+        return remote(r.upre.at[held(0, s, 1 - y)], r.fy.at[s], r.f2s.at[s], r.f2r.at[s], at.yp)
+
+    def f_back(s):
+        return remote(r.osd.at[s], r.out.at[s, core], r.f3s.at[s], r.f3r.at[s], at.sib)
+
+    def b_core(s):
+        return remote(r.n2.at[s, other], r.er.at[s], r.a1s.at[s], r.a1r.at[s], at.sib)
+
+    def s_core(s):
+        return remote(r.st.at[s, 1 - core], r.sl.at[s], r.b1s.at[s], r.b1r.at[s], at.sib)
+
+    def b_y(s):
+        return remote(r.upre.at[held(length, s, 1 - y)], r.bey.at[s], r.a2s.at[s], r.a2r.at[s], at.yp)
+
+    def s_y(s):
+        return remote(r.sh.at[s], r.sy.at[s], r.b2s.at[s], r.b2r.at[s], at.yp)
+
+    def b_back(s):
+        return remote(r.isd.at[s], r.ig.at[s, core], r.a3s.at[s], r.a3r.at[s], at.sib)
+
+    at.greet([at.sib, at.yp, at.diag], True)
+    each(slots, lambda s: sib_copy(0, s).start())
+    r.gland[at.head] = r.gb_in[...]
+    g_copies = [
+        remote(r.gb_in, r.gland.at[at.head], r.gs.at[k], r.gr.at[k], d)
+        for k, d in enumerate((at.sib, at.yp, at.diag))
+    ]
+    for copy in g_copies:
+        copy.start()
+
+    def first_y(s):
+        sib_copy(0, s).wait_recv()
+        build(0, s)
+        y_copy(0, s).start()
+
+    each(slots, first_y)
+
+    def wo_block(who):
+        return r.wog.at[pl.ds(pl.multiple_of(feat * who, 16), feat)]
+
+    wo_sib = remote(r.wo_in, wo_block(at.head), r.ws.at[0], r.wr.at[0], at.sib)
+    wo_y = remote(r.wo_in, wo_block(at.head), r.ws.at[1], r.wr.at[1], at.yp)
+    wo_f = remote(wo_block(at.yp[1]), wo_block(at.yp[1]), r.ws.at[2], r.wr.at[2], at.sib)
+    wo_y.start()
+    wo_sib.start()
+    each(slots, lambda s: sib_copy(1, s).start())
+    r.wog[pl.ds(pl.multiple_of(feat * at.head, 16), feat)] = r.wo_in[...]
+    for copy in g_copies:
+        copy.wait()
+    r.gbf[...] = jnp.concatenate([r.gland[i] for i in range(4)], axis=1)
+    r.mrow[...] = jnp.zeros_like(r.mrow)
+    r.lrow[...] = jnp.ones_like(r.lrow)
+    r.og[...] = jnp.zeros_like(r.og)
+    r.qq[...] = jnp.zeros_like(r.qq)
+    r.qkv[...] = jnp.zeros_like(r.qkv)
+    r.gsum[...] = jnp.zeros_like(r.gsum)
+    r.gtwo[...] = jnp.zeros_like(r.gtwo)
+    r.drow[...] = jnp.zeros_like(r.drow)
+
+    def project(s):
+        x = whole_rows(r.xg, s).astype(F32)
+        mean, inv = row_stats(x)
+        normed = ((x - mean) * inv * r.gbf[0:1] + r.gbf[1:2]).astype(BF16)
+        r.n1[s] = normed
+        pt = dot(r.w_t[...], normed, 1, 1)
+        qk = turn(pt[:half], r.cos[...], r.sin[...])
+        r.qt[s] = (qk[:feat] * HEAD_DIM**-0.5).astype(BF16)
+        kv = jnp.concatenate([qk[feat:], pt[half:]], axis=0).astype(BF16)
+        r.kvn[s] = kv[:, :length]
+        r.kvo[s] = kv[:, length:]
+        readers(s, lambda i: kv_copy(s, i).start())
+
+    def arrive(t):
+        @pl.when(t < slots)
+        def _():
+            y_copy(0, t).wait_recv()
+            f_copy(0, t).start()
+
+        @pl.when(t >= 1)
+        def _():
+            f_copy(0, t - 1).wait_recv()
+            project(t - 1)
+
+    each(slots + 1, arrive)
+
+    def cot_on(s):
+        sib_copy(1, s).wait_recv()
+        build(1, s)
+        y_copy(1, s).start()
+
+    each(2, cot_on)
+
+    def attend(s):
+        start, end = r.bounds[s, 0:1], r.bounds[s, 1:2]
+        clean, noisy = masks(me, length, start, end)
+        kc, kn = r.kvo[s], r.kvn[s]
+        q = [r.qt[s, hd] for hd in heads]
+        sc = [dot(kc[hd], q[h], 0, 0) for h, hd in enumerate(heads)]
+        sn = [dot(kn[hd], q[h][:, :length], 0, 0) for h, hd in enumerate(heads)]
+        sc = [jnp.where(clean, v, masked_score) for v in sc]
+        sn = [jnp.where(noisy, v, masked_score) for v in sn]
+        top = []
+        for h in range(hl):
+            tc = jnp.max(sc[h], axis=0, keepdims=True)
+            tn = jnp.max(sn[h], axis=0, keepdims=True)
+            top.append(jnp.concatenate([jnp.maximum(tc[:, :length], tn), tc[:, length:]], axis=1))
+        pc = [jnp.exp(sc[h] - top[h]) for h in range(hl)]
+        pn = [jnp.exp(sn[h] - top[h][:, :length]) for h in range(hl)]
+        oc = [dot(kc[feat:][hd], pc[h].astype(BF16), 1, 0) for h, hd in enumerate(heads)]
+        on = [dot(kn[feat:][hd], pn[h].astype(BF16), 1, 0) for h, hd in enumerate(heads)]
+        for h, hd in enumerate(heads):
+            tc = jnp.sum(pc[h], axis=0, keepdims=True)
+            tn = jnp.sum(pn[h], axis=0, keepdims=True)
+            r.mrow[h : h + 1] = top[h]
+            r.lrow[h : h + 1] = jnp.concatenate([tc[:, :length] + tn, tc[:, length:]], axis=1)
+            r.acc[hd, early] = oc[h][:, :length] + on[h]
+            r.acc[hd, late] = oc[h][:, length:]
+
+        def one(j, carry):
+            kv_in(s, j).wait_recv()
+            kv = r.kvb[at.spot(s, j, j)]
+            q = [r.qt[s, hd] for hd in heads]
+            old = [r.mrow[h : h + 1] for h in range(hl)]
+            total = [r.lrow[h : h + 1] for h in range(hl)]
+            pos = lax.broadcasted_iota(jnp.int32, (length, rows), 0) + j * length
+            allowed = pos >= start
+            sc = [dot(kv[hd], q[h], 0, 0) for h, hd in enumerate(heads)]
+            sc = [jnp.where(allowed, v, masked_score) for v in sc]
+            new = [jnp.maximum(old[h], jnp.max(sc[h], axis=0, keepdims=True)) for h in range(hl)]
+            p = [jnp.exp(sc[h] - new[h]) for h in range(hl)]
+            add = [dot(kv[feat:][hd], p[h].astype(BF16), 1, 0) for h, hd in enumerate(heads)]
+            scale = [jnp.exp(old[h] - new[h]) for h in range(hl)]
+            for h, hd in enumerate(heads):
+                r.mrow[h : h + 1] = new[h]
+                r.lrow[h : h + 1] = total[h] * scale[h] + jnp.sum(p[h], axis=0, keepdims=True)
+                r.acc[hd] = r.acc[hd] * scale[h] + add[h]
+            return carry
+
+        lax.fori_loop(at.lowest(s, me), me, one, 0)
+        for h, hd in enumerate(heads):
+            r.att[s, hd] = r.acc[hd] / r.lrow[h : h + 1]
+        r.lse[s] = r.mrow[...] + jnp.log(r.lrow[...])
+        r.own_att[s] = r.att[s].T.astype(BF16)
+        sib_copy(2, s).start()
+
+    def forward(s):
+        x = whole_rows(r.xg, s).astype(F32)
+        branch = dot(r.ag[s, 0], r.wog[:half], 1, 0) + dot(r.ag[s, 1], r.wog[half:], 1, 0)
+        h = x + branch
+        for yy in range(2):
+            for cc in range(2):
+
+                @pl.when(jnp.logical_and(y == yy, core == cc))
+                def _():
+                    r.hp[s] = h[cc * length : (cc + 1) * length, yy * half : (yy + 1) * half]
+
+        mean, inv = row_stats(h)
+        r.iv[s] = inv
+        normed = ((h - mean) * inv * r.gbf[2:3] + r.gbf[3:4]).astype(BF16)
+        r.n2[s] = normed
+        up = dot(normed, r.wu[...], 1, 0)
+        cube = 0.7978845608028654 * (up + 0.044715 * up * up * up)
+        t = jnp.tanh(cube)
+        r.act[s] = (0.5 * up * (1.0 + t)).astype(BF16)
+        slope = 0.5 * (1.0 + t) + 0.5 * up * (1.0 - t * t) * (
+            0.7978845608028654 * (1.0 + 3 * 0.044715 * up * up)
+        )
+        da = dot(whole_rows(r.cg, s), r.wd[...], 1, 1)
+        pre = (da * slope).astype(BF16)
+        r.upre[s] = pre
+        r.ep[s] = dot(pre, r.wu[...], 1, 1).astype(BF16)
+        e_core(s).start()
+
+    def stage(t, offset, step):
+        s = t - offset
+
+        @pl.when(jnp.logical_and(s >= 0, s < slots))
+        def _():
+            step(s)
+
+    def att_on(s):
+        sib_copy(2, s).wait_recv()
+        build(2, s)
+        y_copy(2, s).start()
+
+    def att_back(s):
+        y_copy(2, s).wait_recv()
+        f_copy(2, s).start()
+
+    def cot_back(s):
+        y_copy(1, s).wait_recv()
+        f_copy(1, s).start()
+
+    def feed(s):
+        @pl.when(s == 0)
+        def _():
+            wo_y.wait_recv()
+            wo_f.start()
+            wo_sib.wait_recv()
+            wo_f.wait_recv()
+
+        f_copy(1, s).wait_recv()
+        f_copy(2, s).wait_recv()
+        forward(s)
+
+    def e_on(s):
+        e_core(s).wait_recv()
+        r.er[s] = (r.ep[s, mine].astype(F32) + r.er[s].astype(F32)).astype(BF16)
+        e_y(s).start()
+
+    def e_total(s):
+        e_y(s).wait_recv()
+        r.ey[s] = (r.er[s].astype(F32) + r.ey[s].astype(F32)).astype(BF16)
+        e_y(s).wait_send()
+        e_back(s).start()
+
+    def loop_one(t):
+        stage(t, 1, att_on)
+
+        @pl.when(jnp.logical_and(t >= 1, t < slots - 1))
+        def _():
+            cot_on(t + 1)
+
+        stage(t, 2, cot_back)
+        stage(t, 2, att_back)
+
+        @pl.when(t == slots)
+        def _():
+            each(slots - 2, e_on)
+
+        @pl.when(t == slots + 1)
+        def _():
+            e_on(slots - 2)
+
+        stage(t, 0, attend)
+        stage(t, 2, feed)
+
+    each(slots + 2, loop_one)
+
+    wide = slots * rows
+
+    def up_tile(i):
+        cols = pl.ds(pl.multiple_of(i * 256, 256), 256)
+        left = r.n2[...].reshape(wide, D)
+        part = dot(left, r.upre[:, :, cols].reshape(wide, 256), 0, 0).astype(BF16)
+        r.gl[0, :, cols] = part
+
+    def down_tile(i):
+        cols = pl.ds(pl.multiple_of(lax.rem(i, 3) * 128, 128), 128)
+        out_cols = pl.ds(pl.multiple_of(i * 128, 128), 128)
+        left = r.act[...].reshape(wide, D)
+        part = dot(left, r.cg[:, lax.div(i, 3), :, cols].reshape(wide, 128), 0, 0).astype(BF16)
+        r.gl[1, :, out_cols] = part
+
+    e_on(slots - 1)
+    each(D // 256, up_tile)
+    each(D // 128, down_tile)
+    sum1.begin()
+    e_total(0)
+    e_total(1)
+
+    def two_back(s):
+        e_back(s).wait_recv()
+        e_back(s).wait_send()
+        e_core(s).wait_send()
+
+        @pl.when(core == 0)
+        def _():
+            r.ep[s, early] = r.ey[s]
+            r.ep[s, late] = r.eb[s]
+
+        @pl.when(core == 1)
+        def _():
+            r.ep[s, early] = r.eb[s]
+            r.ep[s, late] = r.ey[s]
+
+        e = r.ep[s].astype(F32)
+        xh = (r.n2[s].astype(F32) - r.gbf[3:4]) * r.ginv[0:1]
+        r.gtwo[2:3] += jnp.sum(e * xh, axis=0, keepdims=True)
+        r.gtwo[3:4] += jnp.sum(e, axis=0, keepdims=True)
+        g = e * r.gbf[2:3]
+        first = jnp.sum(g, axis=1, keepdims=True) / D
+        second = jnp.sum(g * xh, axis=1, keepdims=True) / D
+        resid = whole_rows(r.cg, s).astype(F32) + r.iv[s] * (g - first - xh * second)
+        r.ep[s] = resid.astype(BF16)
+
+    r.ginv[...] = 1.0 / r.gbf[2:3] + jnp.zeros_like(r.ginv)
+
+    def head_grads(s, kv, lanes, allowed):
+        q = [r.qt[s, hd, lanes] for hd in heads]
+        d_out = [r.do[hd, lanes] for hd in heads]
+        sc = [dot(kv[hd], q[h], 0, 0) for h, hd in enumerate(heads)]
+        dp = [dot(kv[feat:][hd], d_out[h], 0, 0) for h, hd in enumerate(heads)]
+        p = [
+            jnp.exp(jnp.where(allowed, sc[h], masked_score) - r.lse[s, h : h + 1, lanes])
+            for h in range(hl)
+        ]
+        ds = [(p[h] * (dp[h] - r.drow[h : h + 1, lanes])).astype(BF16) for h in range(hl)]
+        dv = [dot(d_out[h], p[h].astype(BF16), 1, 1) for h in range(hl)]
+        dk = [dot(q[h], ds[h], 1, 1) for h in range(hl)]
+        dq_add = [dot(kv[hd], ds[h], 1, 0) for h, hd in enumerate(heads)]
+        return [jnp.concatenate(v, axis=0) for v in (dq_add, dk, dv)]
+
+    def attend_back(s):
+        low_rows = r.ep[s]
+        d_out = dot(r.wo_in[...], low_rows, 1, 1).astype(BF16)
+        r.do[...] = d_out
+        a = r.att[s]
+        r.og[...] += dot(a.astype(BF16), low_rows, 1, 0)
+        prod = d_out.astype(F32) * a
+        for h, hd in enumerate(heads):
+            r.drow[h : h + 1] = jnp.sum(prod[hd], axis=0, keepdims=True)
+        start, end = r.bounds[s, 0:1], r.bounds[s, 1:2]
+        clean, noisy = masks(me, length, start, end)
+        dqa, dk, dv = head_grads(s, r.kvo[s], slice(0, rows), clean)
+        dqn, dkn, dvn = head_grads(s, r.kvn[s], early, noisy)
+        r.acc[...] = dqa
+        r.acc[:, early] += dqn
+        r.dkv[s, :feat] = dk
+        r.dkv[s, feat:] = dv
+        r.qp[s, half:, early] = dvn.astype(BF16)
+        r.qp[s, feat:half, early] = turn(dkn, r.cos[:, :length], -r.sin[:, :length]).astype(BF16)
+
+        def one(j, carry):
+            spot = at.spot(s, j, j)
+            kv = r.kvb[spot]
+            pos = lax.broadcasted_iota(jnp.int32, (length, rows), 0) + j * length
+            dqa, dk, dv = head_grads(s, kv, slice(0, rows), pos >= start)
+            r.acc[...] += dqa
+            r.kvb[spot, :feat] = dk.astype(BF16)
+            r.kvb[spot, feat:] = dv.astype(BF16)
+            dkv_copy(s, j).start()
+            return carry
+
+        lax.fori_loop(at.lowest(s, me), me, one, 0)
+        r.qp[s, :feat] = (turn(r.acc[...], r.cos[...], -r.sin[...]) * HEAD_DIM**-0.5).astype(BF16)
+        r.qq[...] += dot(r.qp[s, :feat], r.n1[s], 1, 0)
+
+    def f_start(s):
+        y_copy(2, s).wait_send()
+        f_copy(2, s).wait_send()
+        ff = dot(r.act[s], r.wd[...], 1, 0)
+        r.ag[s, 0] = ff[:, :half].astype(BF16)
+        r.ag[s, 1] = ff[:, half:].astype(BF16)
+        f_core(s).start()
+
+    def f_on(s):
+        f_core(s).wait_recv()
+        for k in range(2):
+            r.upre[held(0, s, k)] = (r.ag[s, k, mine].astype(F32) + r.fc[s, k].astype(F32)).astype(BF16)
+        f_y(s).start()
+
+    def f_end(s):
+        f_y(s).wait_recv()
+        total = r.hp[s] + (r.upre[held(0, s, y)].astype(F32) + r.fy[s].astype(F32))
+        lo = total[:, :feat].astype(BF16)
+        hi = total[:, feat:].astype(BF16)
+
+        @pl.when(core == 0)
+        def _():
+            r.out[s, 0] = lo
+            r.osd[s] = hi
+
+        @pl.when(core == 1)
+        def _():
+            r.out[s, 1] = hi
+            r.osd[s] = lo
+
+        f_back(s).start()
+
+    def loop_two(t):
+        def run(s):
+            two_back(s)
+            attend_back(s)
+
+        stage(t, 1, f_on)
+        stage(t, -2, e_total)
+        stage(t, 0, run)
+
+        @pl.when(jnp.logical_or(t == 3, t == 5))
+        def _():
+            sum1.pass_on(lax.div(t - 3, 2))
+
+    each(slots, f_start)
+    each(slots, loop_two)
+    src2[0] = r.og[...].astype(BF16)
+    src2[1] = r.qq[...].astype(BF16)
+    sum2.begin()
+    f_on(slots - 1)
+    sum1.pass_on(2)
+    sum1.pass_on(3)
+
+    def project_back(s):
+        def add(i):
+            dkv_in(s, i).wait_recv()
+            r.dkv[s] += r.dla[at.spot(s, me, i)].astype(F32)
+
+        readers(s, add)
+        total = r.dkv[s]
+        r.qp[s, feat:half, late] = turn(total[:feat], r.cos[:, late], -r.sin[:, late]).astype(BF16)
+        r.qp[s, half:, late] = total[feat:].astype(BF16)
+        pre = r.qp[s]
+        r.qkv[...] += dot(pre[feat:], r.n1[s], 1, 0)
+        e = dot(pre, r.w_t[...], 0, 0)
+        x = whole_rows(r.xg, s).astype(F32)
+        mean, inv = row_stats(x)
+        xh = (x - mean) * inv
+        r.gsum[0:1] += jnp.sum(e * xh, axis=0, keepdims=True)
+        r.gsum[1:2] += jnp.sum(e, axis=0, keepdims=True)
+        r.n2[s] = e.astype(BF16)
+        g = e * r.gbf[0:1]
+        one_sum = jnp.sum(g, axis=1, keepdims=True)
+        two_sum = jnp.sum(g * xh, axis=1, keepdims=True)
+        lane = lax.broadcasted_iota(jnp.int32, (rows, 128), 1)
+        packed = jnp.where(lane == 0, one_sum, jnp.where(lane == 1, two_sum, 0.0)).T
+        r.st[s, 0] = packed[:8, :length]
+        r.st[s, 1] = packed[:8, length:]
+        b_core(s).start()
+        s_core(s).start()
+
+    def b_on(s):
+        b_core(s).wait_recv()
+        s_core(s).wait_recv()
+        both = r.n2[s, mine].astype(F32) + r.er[s].astype(F32)
+        r.upre[s, late] = both.astype(BF16)
+        r.sh[s] = r.st[s, core] + r.sl[s]
+        b_y(s).start()
+        s_y(s).start()
+
+    def b_end(s):
+        b_y(s).wait_recv()
+        s_y(s).wait_recv()
+        e = r.upre[held(length, s, y)].astype(F32) + r.bey[s].astype(F32)
+        sums = r.sh[s] + r.sy[s]
+        cols = jnp.concatenate([sums, jnp.zeros((120, length), F32)], axis=0).T
+        first, second = cols[:, 0:1] / D, cols[:, 1:2] / D
+        x = jnp.concatenate([r.xg[s, 0, mine], r.xg[s, 1, mine]], axis=1).astype(F32)
+        mean, inv = row_stats(x)
+        xh = (r.xg[s, y, mine].astype(F32) - mean) * inv
+        gain = jnp.where(y == 0, r.gbf[0:1, :half], r.gbf[0:1, half:])
+        resid = r.ep[s, mine].astype(F32)
+        resid = jnp.where(y == 0, resid[:, :half], resid[:, half:])
+        grad = resid + inv * (e * gain - first - xh * second)
+        lo, hi = grad[:, :feat], grad[:, feat:]
+
+        @pl.when(core == 0)
+        def _():
+            r.ig[s, 0] = lo
+            r.isd[s] = hi
+
+        @pl.when(core == 1)
+        def _():
+            r.ig[s, 1] = hi
+            r.isd[s] = lo
+
+        b_back(s).start()
+
+    def loop_three(t):
+        stage(t, 0, f_end)
+        stage(t, 1, b_on)
+        stage(t, 0, project_back)
+
+        pl.when(t == 2)(sum1.reduce)
+
+        @pl.when(jnp.logical_or(t == 3, t == 4))
+        def _():
+            sum2.pass_on(2 * t - 6)
+            sum2.pass_on(2 * t - 5)
+
+    each(slots, loop_three)
+    grads = r.qkv[...].astype(BF16)
+    r.src3[0] = grads[:feat]
+    r.src3[1] = grads[feat:]
+    sum3.begin()
+    b_on(slots - 1)
+    h_copies = [
+        remote(r.gsum, r.gh.at[k], r.hs.at[k], r.hr.at[k], d)
+        for k, d in enumerate((at.sib, at.yp, at.diag))
+    ]
+    for copy in h_copies:
+        copy.start()
+    sum2.reduce()
+
+    def share(i):
+        return remote(r.gf, r.gq.at[me], r.qs.at[i], r.qr.at[me], (i, at.head))
+
+    def share_in(i):
+        return remote(r.gf, r.gq.at[i], r.qs.at[i], r.qr.at[i], (i, at.head))
+
+    def gains_on():
+        for copy in h_copies:
+            copy.wait()
+        total = r.gsum[...] + r.gh[0] + r.gh[1] + r.gh[2] + r.gtwo[...]
+        for h in range(4):
+
+            @pl.when(at.head == h)
+            def _():
+                r.gf[...] = total[:, h * feat : (h + 1) * feat]
+
+        r.gq[me] = r.gf[...]
+        for d in range(1, n):
+            share(lax.rem(me + d, n)).start()
+
+    def loop_four(t):
+        stage(t, 0, b_end)
+        pl.when(t == 0)(gains_on)
+
+        @pl.when(jnp.logical_or(t == 1, t >= 4))
+        def _():
+            sum1.forward(jnp.where(t == 1, 1, t - 2))
+
+        @pl.when(jnp.logical_or(t == 2, t == 3))
+        def _():
+            sum3.pass_on(2 * t - 4)
+            sum3.pass_on(2 * t - 3)
+
+    each(slots, loop_four)
+    sum3.reduce()
+    for d in range(1, n):
+        share_in(lax.rem(me + d, n)).wait_recv()
+    r.gains[...] = jnp.sum(r.gq[...], axis=0)
+    for d in range(1, m):
+        sum2.forward(d)
+    for d in range(1, m):
+        sum3.forward(d)
+
+    def finish(s):
+        for k in range(3):
+            sib_copy(k, s).wait_send()
+        for k in range(2):
+            y_copy(k, s).wait_send()
+            f_copy(k, s).wait_send()
+        readers(s, lambda i: kv_copy(s, i).wait_send())
+        f_core(s).wait_send()
+        f_y(s).wait_send()
+        f_back(s).wait()
+        b_core(s).wait_send()
+        s_core(s).wait_send()
+        b_y(s).wait_send()
+        s_y(s).wait_send()
+        b_back(s).wait()
+
+        def sent(j, carry):
+            dkv_copy(s, j).wait_send()
+            return carry
+
+        lax.fori_loop(at.lowest(s, me), me, sent, 0)
+
+    each(slots, finish)
+    wo_sib.wait_send()
+    wo_y.wait_send()
+    wo_f.wait_send()
+    for part in (sum1, sum2, sum3):
+        part.finish()
+    for d in range(1, n):
+        share(lax.rem(me + d, n)).wait_send()
+
+
+def body(
+    inputs,
+    doc_lengths,
+    attn_gain,
+    attn_bias,
+    w_qkv,
+    w_out,
+    ffn_gain,
+    ffn_bias,
+    w_up,
+    w_down,
+    cotangent,
+):
+    n = lax.axis_size("seq")
+    slots, _, length, feat = inputs.shape
+    rows, half, m = 2 * length, 2 * feat, n // 2
+    held = slots * n * half * length * 2
+    if held > ROWS_LIMIT or m != 4:
+        return gathered_body(
+            inputs, doc_lengths, attn_gain, attn_bias, w_qkv, w_out, ffn_gain, ffn_bias, w_up, w_down, cotangent
+        )
+    me = lax.axis_index("seq")
+    long = jnp.argmax(doc_lengths[:, 0]).astype(jnp.int32)
+    ids = jnp.arange(slots, dtype=jnp.int32)
+
+    def swap(v):
+        pick = lax.dynamic_index_in_dim(v, long, 0, keepdims=True)
+        where = ids.reshape((slots,) + (1,) * (v.ndim - 1))
+        return jnp.where(where == 0, pick, jnp.where(where == long, v[:1], v))
+
+    ends = jnp.cumsum(swap(doc_lengths), axis=1)
+    positions = me * length + jnp.arange(length, dtype=jnp.int32)
+    past = ends[:, :, None] <= positions[None, None, :]
+    first_key = jnp.max(jnp.where(past, ends[:, :, None], 0), axis=1)
+    last_key = jnp.min(jnp.where(past, 2**30, ends[:, :, None]), axis=1)
+    pair = jnp.stack([jnp.tile(first_key, (1, 2)), jnp.tile(last_key, (1, 2))], axis=1)
+    bounds = jnp.pad(pair, ((0, 0), (0, 6), (0, 0)))
+    half_dim = HEAD_DIM // 2
+    freqs = rotary_base ** (-jnp.arange(half_dim, dtype=F32) / half_dim)
+    angles = freqs[:, None] * positions.astype(F32)[None, :]
+    cos = jnp.tile(jnp.cos(angles), (1, 2))
+    sin = jnp.tile(jnp.sin(angles), (1, 2))
+    w_t = w_qkv.reshape(D, 3 * feat).T
+    gains = jnp.concatenate(
+        [jnp.stack([attn_gain, attn_bias, ffn_gain, ffn_bias]), jnp.zeros((4, feat), F32)], axis=0
+    )
+    operands = dict(
+        x_in=swap(inputs).reshape(slots, rows, feat), c_in=swap(cotangent).reshape(slots, rows, feat),
+        gb_in=gains, w_t=w_t, wo_in=w_out, wu=w_up, wd=w_down, cos=cos, sin=sin, bounds=bounds,
+    )
+    small = (m, feat // m, D)
+    quarter = (m, D // m, D)
+    outs = dict(
+        out=((slots, 2, length, feat), BF16), ig=((slots, 2, length, feat), F32), res1=((2, *quarter), BF16),
+        res2=((2, *small), BF16), res3=((2, *small), BF16), gains=((8, feat), F32),
+    )
+    blocks = n + (slots - 1) * (n // 2 + max(1, n // 8))
+    full, wide = (slots, 2, rows, half), (slots, rows, D)
+    part, stat = (slots, length, D), (slots, 8, length)
+    halves, own_half = (slots, 2, length, half), (slots, length, half)
+    buffers = dict(
+        land=((2, slots, rows, feat), BF16), own_att=((slots, rows, feat), BF16), gland=((4, 8, feat), F32),
+        gbf=((8, D), F32), ginv=((8, D), F32), xg=(full, BF16), cg=(full, BF16), ag=(full, BF16),
+        wog=((D, D), BF16), n1=(wide, BF16), qt=((slots, feat, rows), BF16),
+        kvn=((slots, half, length), BF16), kvo=((slots, half, length), BF16), kvb=((blocks, half, length), BF16),
+        att=((slots, feat, rows), F32), lse=((slots, 8, rows), F32), acc=((feat, rows), F32),
+        mrow=((8, rows), F32), lrow=((8, rows), F32), hp=(own_half, F32), iv=((slots, rows, 1), F32),
+        n2=(wide, BF16), act=(wide, BF16), upre=(wide, BF16), ep=(wide, BF16), er=(part, BF16), ey=(part, BF16),
+        eb=(part, BF16), fc=(halves, BF16), fy=(own_half, BF16),
+        osd=((slots, length, feat), BF16), gl=((2, D, D), BF16), gx1=(quarter, BF16), gz1=(quarter, BF16),
+        own1=(quarter[1:], BF16), do=((feat, rows), BF16), drow=((8, rows), F32),
+        dkv=((slots, half, length), F32), dla=((blocks, half, length), BF16), qp=((slots, 3 * feat, rows), BF16),
+        og=((feat, D), F32), qq=((feat, D), F32), qkv=((half, D), F32), gsum=((8, D), F32), gtwo=((8, D), F32),
+        st=((slots, 2, 8, length), F32), sl=(stat, F32), sh=(stat, F32), sy=(stat, F32),
+        bey=(own_half, BF16), isd=((slots, length, feat), F32), src3=((2, feat, D), BF16),
+        gx2=(small, BF16), pt2=(small, BF16), gz2=(small, BF16), own2=(small[1:], BF16),
+        gx3=(small, BF16), pt3=(small, BF16), gz3=(small, BF16), own3=(small[1:], BF16),
+        gh=((3, 8, D), F32), gq=((n, 8, feat), F32), gf=((8, feat), F32),
+    )
+    sems = {k: (3, slots) for k in ("ss", "sr", "ys", "yr", "fs", "fr")}
+    sems |= {k: (3,) for k in ("gs", "gr", "ws", "wr", "hs", "hr")}
+    sems |= {k: (slots, n) for k in ("ks", "kr", "ds", "dr")}
+    sems |= {k + i + e: (slots,) for k in "efab" for i in "123" for e in "sr" if k + i != "b3"}
+    sems |= {"qs": (n,), "qr": (n,)}
+    sems |= {"%s%d" % (k, i): (m,) for k in "uvw" for i in range(8)}
+    sem = pltpu.SemaphoreType.DMA
+    scratch = {k: VMEM(*v) for k, v in buffers.items()}
+    scratch |= {k: sem(v) for k, v in sems.items()}
+    scratch |= {k + "8": sem for k in "uvw"}
+    vmem = pl.BlockSpec(memory_space=VMEM)
+    names = [*operands, *outs, *scratch]
+    got = pl.pallas_call(
+        functools.partial(layer, n, names),
+        out_shape=[jax.ShapeDtypeStruct(*v) for v in outs.values()],
+        in_specs=[vmem] * len(operands),
+        out_specs=[pl.BlockSpec(memory_space=pl.ANY) if k.startswith("res") else vmem for k in outs],
+        scratch_shapes=list(scratch.values()),
+        compiler_params=pltpu.CompilerParams(
+            collective_id=0, has_side_effects=True, vmem_limit_bytes=VMEM_LIMIT
+        ),
+        name="layer",
+    )(*operands.values())
+    outputs, input_grad, res1, res2, res3, gain_grads = got
+    up_grad, down_grad = res1.reshape(2, D, D).astype(F32)
+    out_grad, q_grad = res2.reshape(2, feat, D).astype(F32)
+    qkv_grad = jnp.concatenate([q_grad[None], res3.reshape(2, feat, D).astype(F32)], axis=0)
+    return (
+        swap(outputs),
+        swap(input_grad),
+        jnp.transpose(qkv_grad, (2, 0, 1)),
+        out_grad,
+        up_grad,
+        down_grad,
+        gain_grads[0],
+        gain_grads[1],
+        gain_grads[2],
+        gain_grads[3],
+    )
+
+
 def solution(mesh):
     in_specs = (
         P(None, None, "seq", "head"),

time: 1020 us -> 245 us (0.24)
  waiting for transfers between devices: 591 us -> 0 us
  Pallas kernels: 0 us -> 218 us
  matrix products: 134 us -> 0 us
  other arithmetic: 86.3 us -> 7.03 us
  starting transfers between devices: 69.7 us -> 0 us
  blocking collectives: 68.4 us -> 0 us
  local copies, waits for them, and re-layouts: 52.2 us -> 16.8 us
  between operations: 14.7 us -> 2.78 us
    psum x1 -> x0, waiting for transfers between devices: 237 us -> none  [body(): lax.psum((qkv_grad, out_grad, up_grad, down_grad, attn_gain_grad, attn_bi...]
    pallas_call x0 -> x1, Pallas kernels: none -> 218 us  [body(): pl.pallas_call(functools.partial(layer, n, names), out_shape=[jax.ShapeDt...]
    all_gather x6 -> x0, waiting for transfers between devices: 158 us -> none  [the longest x2 48.4 us: normalize(): gathered = lax.all_gather(scaled, 'head', axis=3, tiled=True)]
    dot_general x60 -> x0, matrix products: 134 us -> none  [the longest x8 24.7 us: piece_grads(): jnp.einsum('schlk,schld->skhd', weights_now, grad_wide, precision=lax.Pre...]
    reduce_scatter x4 -> x0, waiting for transfers between devices: 128 us -> none  [the longest x2 71 us: norm_backward(): lax.psum_scatter(partial_value, 'head', scatter_dimension=3, tiled=True)]
    psum x5 -> x0, blocking collectives: 68.4 us -> none  [the longest x4 46.4 us: row_pair(): return lax.psum((first_sum, second_sum), 'head')]
    ppermute x32 -> x0, starting transfers between devices: 68 us -> none  [the longest x16 52.6 us: passed_along(): return lax.ppermute(block, axis, route)]
    ppermute x32 -> x0, waiting for transfers between devices: 66.3 us -> none  [the longest x16 66.3 us: from_behind(): lax.ppermute(x, axis, [(i, (i + by) % devices) for i in range(devices)])]
  transfers between devices with their start and end apart: 43 -> 0, of which waited for: 27 -> 0; matrix products, arithmetic and copies ran while one was open for 17% -> 0% of each run, Pallas kernels for 0% -> 0%
where the time goes in v3:
time: 245 us
  Pallas kernels  218 us (89%)
  local copies, waits for them, and re-layouts  16.8 us (7%)
  other arithmetic  7.03 us (3%)
  between operations  2.78 us (1%)
    pallas_call x1, Pallas kernels, body(): pl.pallas_call(functools.partial(layer, n, names), out_shape=[jax.ShapeDt...  218 us
    unnamed x18, local copies, waits for them, and re-layouts  5.75 us

profile of v3, /device:TPU:0, one launch (start us, length us, event | category | flops | bytes accessed | tf_op | source)
XLA Modules:
  0.0 244.8 jit_solution(14943097871975248407)
XLA Ops:
  0.6 0.0 copy-start.3
  0.7 0.9 slice_reduce_fusion
  1.5 0.7 iota_reduce_fusion
  4.1 0.7 iota_compare_fusion
  4.8 0.8 fusion.2
  5.6 0.8 select_select_fusion.4
  6.3 0.2 reduce_window_sum.11
  6.5 0.1 fusion
  6.6 1.3 concatenate.6.refs_2_
  8.0 0.1 multiply_sine_fusion
  8.1 0.6 copy.47
  8.8 0.6 copy.48
  9.4 0.0 copy-start.4
  9.4 0.6 pad.4.refs_9_
  10.0 1.1 dynamic-slice_bitcast_fusion.2
  11.1 0.1 copy.38
  11.2 0.1 copy.39
  11.3 0.1 copy.36
  11.4 0.1 copy.35
  11.6 0.0 copy-done.3
  11.6 0.3 copy.37
  11.9 0.0 copy-done.4
  11.9 0.3 copy.40
  12.2 1.5 select_select_fusion.2
  13.6 218.2 %layer.1 = (bf16[6,2,128,192]{3,2,1,0:T(8,128)(2,1)}, f32[6,2,128,192]{3,2,1,0:T(8,128)}, bf16[2,4,192,768]{3,2,1,0:T(8,128)(2,1)}, bf16[2,4,48,768]{3,2,1,0:T(8...) custom-call(bf16[6,256,192]{2,1,0:T(8,128)(2,1)} %bitcast.53, bf16[6,256,192]{2,1,0:T(8,128)(2,1)} %bitcast.52, ...), custom_call_target="tpu_custom_call" | custom-call | tf_op jit(solution)/shard_map/layer/pallas_call | solution.py:1255
  231.8 1.4 fusion.6
  233.2 1.0 dynamic-slice_bitcast_fusion.1
  234.2 0.0 copy-start.1
  234.2 1.4 select_select_fusion.1
  235.6 1.1 copy.41
  236.7 0.0 copy-done.1
  236.8 0.2 select_select_fusion
  237.0 0.0 copy-start.2
  237.0 1.5 copy.42
  238.5 0.0 copy-done.2
  238.5 0.0 copy-start.5
  238.5 0.9 fusion.5
  239.4 0.4 copy-done.5
  239.8 0.1 bitcast_convert_fusion
  239.9 0.0 copy-start
  239.9 1.3 maximum_bitcast_fusion
  241.2 1.0 copy-done
  242.2 2.6 %fusion.4 = (f32[1,4,192,768]{3,2,1,0:T(8,128)}, f32[1,4,192,768]{3,2,1,0:T(8,128)}) fusion(bf16[2,4,192,768]{3,2,1,0:T(8,128)(2,1)S(1)} %copy-done), kind=kLoop, calls=%fused_computation.34 | loop fusion | bytes 9437184 | tf_op jit(solution)/shard_map/unstack | solution.py:1267
  (9 shorter events, 0.1 us)
Async XLA Ops:
  0.6 10.9 %copy-start.3 = (bf16[6,2,128,192]{2,3,1,0:T(8,128)(2,1)S(1)}, bf16[6,2,128,192]{2,3,1,0:T(8,128)(2,1)}, u32[]{:S(2)}) copy-start(bf16[6,2,128,192]{2,3,1,0:T(8,128)(2,1)} %param.11) | copy-start | bytes 1769476
  9.4 2.5 %copy-start.4 = (bf16[6,2,128,192]{2,3,1,0:T(8,128)(2,1)S(1)}, bf16[6,2,128,192]{2,3,1,0:T(8,128)(2,1)}, u32[]{:S(2)}) copy-start(bf16[6,2,128,192]{2,3,1,0:T(8,128)(2,1)} %param.21) | copy-start | bytes 1769476
  234.2 2.5 %copy-start.1 = (f32[6,2,128,192]{3,2,1,0:T(8,128)S(1)}, f32[6,2,128,192]{3,2,1,0:T(8,128)}, u32[]{:S(2)}) copy-start(f32[6,2,128,192]{3,2,1,0:T(8,128)} %get-tuple-element.19) | copy-start | bytes 3538948
  237.0 1.5 copy-start.2
  238.5 1.3 copy-start.5
  239.9 2.3 copy-start

commit v4 on v3

--- a/solution.py
+++ b/solution.py
@@ -432,7 +432,7 @@
 
 
 class Sum:
-    def __init__(self, at, src, res, gx, part, gz, own, xs, xr, zs, zr, cs, cr, fs, fr, ls):
+    def __init__(self, at, src, res, gx, part, gz, own, xs, xr, zs, zr, cs, cr, fs, fr, ls, ds):
         self.m = at.n // 2
         self.lo = lax.rem(at.me, 2)
         self.hi = lax.div(at.me, 2)
@@ -440,7 +440,8 @@
         self.pair = (at.me + 1 - 2 * self.lo, at.head)
         self.src, self.res, self.gx, self.part, self.gz = src, res, gx, part, gz
         self.xs, self.xr, self.zs, self.zr = xs, xr, zs, zr
-        self.cs, self.cr, self.fs, self.fr, self.ls = cs, cr, fs, fr, ls
+        self.cs, self.cr, self.fs, self.fr, self.ls, self.ds = cs, cr, fs, fr, ls, ds
+        self.pieces = ds.shape[0]
         self.own = own
 
     def piece(self, half, k):
@@ -459,21 +460,28 @@
     def z_in(self, k):
         return remote(self.part.at[k], self.gz.at[k], self.zs.at[k], self.zr.at[k], self.at_z(k))
 
-    def c(self, k):
-        there = self.res.at[self.lo, self.hi]
-        return remote(self.own, there, self.cs.at[k], self.cr.at[self.hi], self.at_z(k))
-
-    def c_in(self, k):
-        part = self.res.at[self.lo, k]
-        return remote(part, part, self.cs.at[k], self.cr.at[k], self.at_z(k))
-
-    def f(self, k):
-        part = self.res.at[self.lo, k]
-        return remote(part, part, self.fs.at[k], self.fr.at[k], self.pair)
-
-    def f_own(self):
-        there = self.res.at[self.lo, self.hi]
-        return remote(self.own, there, self.fs.at[self.hi], self.fr.at[self.hi], self.pair)
+    def piece_of(self, k, p):
+        size = self.gx.shape[1] // self.pieces
+        return pl.ds(p * size, size)
+
+    def c_own(self, p, step):
+        rows = self.piece_of(self.hi, p)
+        there = self.res.at[self.lo, self.hi, rows]
+        sent = self.cs.at[self.hi, p] if step > 0 else self.ds.at[p]
+        return remote(self.own.at[rows], there, sent, self.cr.at[self.hi, p], self.at_z(self.hi + step))
+
+    def c_on(self, k, p, step):
+        part = self.res.at[self.lo, k, self.piece_of(k, p)]
+        return remote(part, part, self.cs.at[k, p], self.cr.at[k, p], self.at_z(self.hi + step))
+
+    def f(self, k, p):
+        part = self.res.at[self.lo, k, self.piece_of(k, p)]
+        return remote(part, part, self.fs.at[k, p], self.fr.at[k, p], self.pair)
+
+    def f_own(self, p):
+        rows = self.piece_of(self.hi, p)
+        there = self.res.at[self.lo, self.hi, rows]
+        return remote(self.own.at[rows], there, self.fs.at[self.hi, p], self.fr.at[self.hi, p], self.pair)
 
     def keep(self):
         return pltpu.make_async_copy(self.own, self.res.at[self.lo, self.hi], self.ls)
@@ -481,16 +489,24 @@
     def others(self):
         return [lax.rem(self.hi + d, self.m) for d in range(1, self.m)]
 
+    def turn_of(self, i):
+        return lax.rem(self.hi + 1 + i, self.m)
+
     def begin(self):
-        each(self.m, lambda k: self.x(k).start())
-
-    def pass_on(self, k):
+        each(self.m, lambda i: self.x(self.turn_of(i)).start())
+
+    def pass_on(self, i):
+        k = self.turn_of(i)
         self.x(k).wait_recv()
         self.part[k] = (self.src[self.piece(self.lo, k)].astype(F32) + self.gx[k].astype(F32)).astype(BF16)
 
         @pl.when(k != self.hi)
         def _():
             self.z(k).start()
+
+    def ends(self, step, run):
+        there = self.hi + step
+        pl.when(jnp.logical_and(there >= 0, there < self.m))(run)
 
     def reduce(self):
         total = self.part[self.hi].astype(F32)
@@ -499,22 +515,40 @@
             total += self.gz[k].astype(F32)
         self.own[...] = total.astype(BF16)
         self.keep().start()
-        for k in self.others():
-            self.c(k).start()
-        self.f_own().start()
+        for p in range(self.pieces):
+            self.ends(1, lambda: self.c_own(p, 1).start())
+            self.ends(-1, lambda: self.c_own(p, -1).start())
+            self.f_own(p).start()
 
     def forward(self, d):
-        k = lax.rem(self.hi + d, self.m)
-        self.c_in(k).wait_recv()
-        self.f(k).start()
+        for p in range(self.pieces):
+            for step in (1, -1):
+
+                def run():
+                    k = self.hi - step * d
+                    self.c_on(k, p, step).wait_recv()
+                    self.ends(step, lambda: self.c_on(k, p, step).start())
+                    self.f(k, p).start()
+
+                self.ends(-step * d, run)
 
     def finish(self):
         each(self.m, lambda k: self.x(k).wait_send())
         for k in self.others():
             self.z(k).wait_send()
-            self.c(k).wait_send()
-            self.f(k).wait()
-        self.f_own().wait()
+        for p in range(self.pieces):
+            for step in (1, -1):
+                self.ends(step, lambda: self.c_own(p, step).wait_send())
+                for d in range(1, self.m):
+
+                    def run():
+                        k = self.hi - step * d
+                        self.ends(step, lambda: self.c_on(k, p, step).wait_send())
+                        self.f(k, p).wait_send()
+
+                    self.ends(-step * d, run)
+            self.f_own(p).wait_send()
+            each(self.m, lambda k: self.f(k, p).wait_recv())
         self.keep().wait()
 
 
@@ -536,11 +570,11 @@
     lands = (r.land.at[0], r.land.at[1], r.land.at[0])
     quarter = D // m
     sum1 = Sum(
-        at, r.gl, r.res1, r.gx1, r.act.at[:m, :quarter], r.gz1, r.own1, *[getattr(r, "u%d" % i) for i in range(9)]
+        at, r.gl, r.res1, r.gx1, r.act.at[:m, :quarter], r.gz1, r.own1, *[getattr(r, "u%d" % i) for i in range(10)]
     )
     src2 = r.act.at[m : m + 2, :feat]
-    sum2 = Sum(at, src2, r.res2, r.gx2, r.pt2, r.gz2, r.own2, *[getattr(r, "v%d" % i) for i in range(9)])
-    sum3 = Sum(at, r.src3, r.res3, r.gx3, r.pt3, r.gz3, r.own3, *[getattr(r, "w%d" % i) for i in range(9)])
+    sum2 = Sum(at, src2, r.res2, r.gx2, r.pt2, r.gz2, r.own2, *[getattr(r, "v%d" % i) for i in range(10)])
+    sum3 = Sum(at, r.src3, r.res3, r.gx3, r.pt3, r.gz3, r.own3, *[getattr(r, "w%d" % i) for i in range(10)])
 
     def sib_copy(k, s):
         return remote(owns[k].at[s], lands[k].at[s], r.ss.at[k, s], r.sr.at[k, s], at.sib)
@@ -1245,7 +1279,10 @@
     sems |= {k: (slots, n) for k in ("ks", "kr", "ds", "dr")}
     sems |= {k + i + e: (slots,) for k in "efab" for i in "123" for e in "sr" if k + i != "b3"}
     sems |= {"qs": (n,), "qr": (n,)}
-    sems |= {"%s%d" % (k, i): (m,) for k in "uvw" for i in range(8)}
+    pieces = {"u": 2, "v": 1, "w": 1}
+    sems |= {"%s%d" % (k, i): (m,) for k in "uvw" for i in range(4)}
+    sems |= {"%s%d" % (k, i): (m, pieces[k]) for k in "uvw" for i in range(4, 8)}
+    sems |= {k + "9": (pieces[k],) for k in "uvw"}
     sem = pltpu.SemaphoreType.DMA
     scratch = {k: VMEM(*v) for k, v in buffers.items()}
     scratch |= {k: sem(v) for k, v in sems.items()}

time: 245 us -> 224 us (0.914)
  Pallas kernels: 218 us -> 197 us
    pallas_call x1, Pallas kernels: 218 us -> 197 us  [body(): pl.pallas_call(functools.partial(layer, n, names), out_shape=[jax.ShapeDt...]
where the time goes in v4:
time: 224 us
  Pallas kernels  197 us (88%)
  local copies, waits for them, and re-layouts  16.8 us (8%)
  other arithmetic  7.03 us (3%)
  between operations  2.78 us (1%)
    pallas_call x1, Pallas kernels, body(): pl.pallas_call(functools.partial(layer, n, names), out_shape=[jax.ShapeDt...  197 us
    unnamed x18, local copies, waits for them, and re-layouts  5.75 us

profile of v4, /device:TPU:0, one launch (start us, length us, event | category | flops | bytes accessed | tf_op | source)
XLA Modules:
  0.0 224.0 jit_solution(17846408179020038722)
XLA Ops:
  0.6 0.0 copy-start.3
  0.7 0.9 slice_reduce_fusion
  1.5 0.7 iota_reduce_fusion
  4.1 0.7 iota_compare_fusion
  4.8 0.8 fusion.2
  5.6 0.8 select_select_fusion.4
  6.3 0.2 reduce_window_sum.11
  6.5 0.1 fusion
  6.6 1.3 concatenate.6.refs_2_
  8.0 0.1 multiply_sine_fusion
  8.1 0.6 copy.47
  8.8 0.6 copy.48
  9.4 0.0 copy-start.4
  9.4 0.6 pad.4.refs_9_
  10.0 1.1 dynamic-slice_bitcast_fusion.2
  11.1 0.1 copy.38
  11.2 0.1 copy.39
  11.3 0.1 copy.36
  11.4 0.1 copy.35
  11.6 0.0 copy-done.3
  11.6 0.3 copy.37
  11.9 0.0 copy-done.4
  11.9 0.3 copy.40
  12.2 1.5 select_select_fusion.2
  13.6 197.4 %layer.1 = (bf16[6,2,128,192]{3,2,1,0:T(8,128)(2,1)}, f32[6,2,128,192]{3,2,1,0:T(8,128)}, bf16[2,4,192,768]{3,2,1,0:T(8,128)(2,1)}, bf16[2,4,48,768]{3,2,1,0:T(8...) custom-call(bf16[6,256,192]{2,1,0:T(8,128)(2,1)} %bitcast.53, bf16[6,256,192]{2,1,0:T(8,128)(2,1)} %bitcast.52, ...), custom_call_target="tpu_custom_call" | custom-call | tf_op jit(solution)/shard_map/layer/pallas_call | solution.py:1292
  211.0 1.4 fusion.6
  212.4 1.0 dynamic-slice_bitcast_fusion.1
  213.4 0.0 copy-start.1
  213.4 1.4 select_select_fusion.1
  214.8 1.1 copy.41
  215.9 0.0 copy-done.1
  216.0 0.2 select_select_fusion
  216.2 0.0 copy-start.2
  216.2 1.5 copy.42
  217.7 0.0 copy-done.2
  217.7 0.0 copy-start.5
  217.7 0.9 fusion.5
  218.6 0.4 copy-done.5
  219.0 0.1 bitcast_convert_fusion
  219.1 0.0 copy-start
  219.1 1.3 maximum_bitcast_fusion
  220.4 1.0 copy-done
  221.4 2.6 %fusion.4 = (f32[1,4,192,768]{3,2,1,0:T(8,128)}, f32[1,4,192,768]{3,2,1,0:T(8,128)}) fusion(bf16[2,4,192,768]{3,2,1,0:T(8,128)(2,1)S(1)} %copy-done), kind=kLoop, calls=%fused_computation.34 | loop fusion | bytes 9437184 | tf_op jit(solution)/shard_map/unstack | solution.py:1304
  (9 shorter events, 0.1 us)
Async XLA Ops:
  0.6 10.9 %copy-start.3 = (bf16[6,2,128,192]{2,3,1,0:T(8,128)(2,1)S(1)}, bf16[6,2,128,192]{2,3,1,0:T(8,128)(2,1)}, u32[]{:S(2)}) copy-start(bf16[6,2,128,192]{2,3,1,0:T(8,128)(2,1)} %param.11) | copy-start | bytes 1769476
  9.4 2.5 %copy-start.4 = (bf16[6,2,128,192]{2,3,1,0:T(8,128)(2,1)S(1)}, bf16[6,2,128,192]{2,3,1,0:T(8,128)(2,1)}, u32[]{:S(2)}) copy-start(bf16[6,2,128,192]{2,3,1,0:T(8,128)(2,1)} %param.21) | copy-start | bytes 1769476
  213.4 2.5 %copy-start.1 = (f32[6,2,128,192]{3,2,1,0:T(8,128)S(1)}, f32[6,2,128,192]{3,2,1,0:T(8,128)}, u32[]{:S(2)}) copy-start(f32[6,2,128,192]{3,2,1,0:T(8,128)} %get-tuple-element.19) | copy-start | bytes 3538948
  216.2 1.5 copy-start.2
  217.7 1.3 copy-start.5
  219.1 2.3 %copy-start = (bf16[2,4,192,768]{3,2,1,0:T(8,128)(2,1)S(1)}, bf16[2,4,192,768]{3,2,1,0:T(8,128)(2,1)}, u32[]{:S(2)}) copy-start(bf16[2,4,192,768]{3,2,1,0:T(8,128)(2,1)} %get-tuple-element.22) | copy-start | bytes 7077892

commit v5 on v4

--- a/solution.py
+++ b/solution.py
@@ -23,6 +23,7 @@
 BF16 = jnp.bfloat16
 ROWS_LIMIT = 16 << 20
 VMEM_LIMIT = 63 << 20
+LONG_SLOT = 3
 
 
 def passed_along(block, axis, distance):
@@ -365,13 +366,14 @@
     def lowest(self, slot, i):
         near = i - self.band
         short = jnp.where(i >= self.half, jnp.minimum(near, self.half), near)
-        return jnp.where(slot == 0, 0, jnp.maximum(short, 0))
+        return jnp.where(slot == LONG_SLOT, 0, jnp.maximum(short, 0))
 
     def spot(self, slot, block, other):
         window = self.half + self.band
         near = self.half + lax.rem(other, self.band)
         late = jnp.where(block >= self.half, other - self.half, near)
-        return jnp.where(slot == 0, other, self.n + (slot - 1) * window + late)
+        order = slot - jnp.where(slot > LONG_SLOT, 1, 0)
+        return jnp.where(slot == LONG_SLOT, other, self.n + order * window + late)
 
     def spots(self, slots):
         return self.n + (slots - 1) * (self.half + self.band)
@@ -573,8 +575,8 @@
         at, r.gl, r.res1, r.gx1, r.act.at[:m, :quarter], r.gz1, r.own1, *[getattr(r, "u%d" % i) for i in range(10)]
     )
     src2 = r.act.at[m : m + 2, :feat]
-    sum2 = Sum(at, src2, r.res2, r.gx2, r.pt2, r.gz2, r.own2, *[getattr(r, "v%d" % i) for i in range(10)])
-    sum3 = Sum(at, r.src3, r.res3, r.gx3, r.pt3, r.gz3, r.own3, *[getattr(r, "w%d" % i) for i in range(10)])
+    sum2 = Sum(at, src2, r.res2.at[:2], r.gx2, r.pt2, r.gz2, r.own2, *[getattr(r, "v%d" % i) for i in range(10)])
+    sum3 = Sum(at, r.src3, r.res2.at[2:], r.gx3, r.pt3, r.gz3, r.own3, *[getattr(r, "w%d" % i) for i in range(10)])
 
     def sib_copy(k, s):
         return remote(owns[k].at[s], lands[k].at[s], r.ss.at[k, s], r.sr.at[k, s], at.sib)
@@ -659,6 +661,9 @@
 
     at.greet([at.sib, at.yp, at.diag], True)
     each(slots, lambda s: sib_copy(0, s).start())
+    r.gb_in[...] = jnp.zeros_like(r.gb_in)
+    for i, vector in enumerate((r.ga, r.ba, r.gf_in, r.bf_in)):
+        r.gb_in[i : i + 1] = vector[...]
     r.gland[at.head] = r.gb_in[...]
     g_copies = [
         remote(r.gb_in, r.gland.at[at.head], r.gs.at[k], r.gr.at[k], d)
@@ -687,6 +692,23 @@
     for copy in g_copies:
         copy.wait()
     r.gbf[...] = jnp.concatenate([r.gland[i] for i in range(4)], axis=1)
+    r.cos[...] = jnp.concatenate([r.cos_in[...]] * 2, axis=1)
+    r.sin[...] = jnp.concatenate([r.sin_in[...]] * 2, axis=1)
+    long, most = 0, r.docs[0, 0]
+    for i in range(1, slots):
+        long = jnp.where(r.docs[i, 0] > most, i, long)
+        most = jnp.maximum(r.docs[i, 0], most)
+    lane = lax.broadcasted_iota(jnp.int32, (8, rows), 1)
+    pos = jnp.where(lane < length, lane, lane - length) + me * length
+    for s in range(slots):
+        row = long if s == LONG_SLOT else jnp.where(long == s, LONG_SLOT, s)
+        end = 0
+        first_key, last_key = jnp.zeros_like(pos), jnp.full_like(pos, 2**30)
+        for j in range(r.docs.shape[1]):
+            end = end + r.docs[row, j]
+            first_key = jnp.where(pos >= end, end, first_key)
+            last_key = jnp.where(pos < end, jnp.minimum(last_key, end), last_key)
+        r.bounds[s] = jnp.where(lax.broadcasted_iota(jnp.int32, (8, rows), 0) == 0, first_key, last_key)
     r.mrow[...] = jnp.zeros_like(r.mrow)
     r.lrow[...] = jnp.ones_like(r.lrow)
     r.og[...] = jnp.zeros_like(r.og)
@@ -992,8 +1014,8 @@
     def f_end(s):
         f_y(s).wait_recv()
         total = r.hp[s] + (r.upre[held(0, s, y)].astype(F32) + r.fy[s].astype(F32))
-        lo = total[:, :feat].astype(BF16)
-        hi = total[:, feat:].astype(BF16)
+        turned = total.T.astype(BF16)
+        lo, hi = turned[:feat], turned[feat:]
 
         @pl.when(core == 0)
         def _():
@@ -1080,7 +1102,8 @@
         resid = r.ep[s, mine].astype(F32)
         resid = jnp.where(y == 0, resid[:, :half], resid[:, half:])
         grad = resid + inv * (e * gain - first - xh * second)
-        lo, hi = grad[:, :feat], grad[:, feat:]
+        turned = grad.T
+        lo, hi = turned[:feat], turned[feat:]
 
         @pl.when(core == 0)
         def _():
@@ -1223,33 +1246,24 @@
     def swap(v):
         pick = lax.dynamic_index_in_dim(v, long, 0, keepdims=True)
         where = ids.reshape((slots,) + (1,) * (v.ndim - 1))
-        return jnp.where(where == 0, pick, jnp.where(where == long, v[:1], v))
-
-    ends = jnp.cumsum(swap(doc_lengths), axis=1)
+        kept = v[LONG_SLOT : LONG_SLOT + 1]
+        return jnp.where(where == LONG_SLOT, pick, jnp.where(where == long, kept, v))
+
     positions = me * length + jnp.arange(length, dtype=jnp.int32)
-    past = ends[:, :, None] <= positions[None, None, :]
-    first_key = jnp.max(jnp.where(past, ends[:, :, None], 0), axis=1)
-    last_key = jnp.min(jnp.where(past, 2**30, ends[:, :, None]), axis=1)
-    pair = jnp.stack([jnp.tile(first_key, (1, 2)), jnp.tile(last_key, (1, 2))], axis=1)
-    bounds = jnp.pad(pair, ((0, 0), (0, 6), (0, 0)))
     half_dim = HEAD_DIM // 2
     freqs = rotary_base ** (-jnp.arange(half_dim, dtype=F32) / half_dim)
     angles = freqs[:, None] * positions.astype(F32)[None, :]
-    cos = jnp.tile(jnp.cos(angles), (1, 2))
-    sin = jnp.tile(jnp.sin(angles), (1, 2))
     w_t = w_qkv.reshape(D, 3 * feat).T
-    gains = jnp.concatenate(
-        [jnp.stack([attn_gain, attn_bias, ffn_gain, ffn_bias]), jnp.zeros((4, feat), F32)], axis=0
-    )
     operands = dict(
         x_in=swap(inputs).reshape(slots, rows, feat), c_in=swap(cotangent).reshape(slots, rows, feat),
-        gb_in=gains, w_t=w_t, wo_in=w_out, wu=w_up, wd=w_down, cos=cos, sin=sin, bounds=bounds,
+        ga=attn_gain[None], ba=attn_bias[None], gf_in=ffn_gain[None], bf_in=ffn_bias[None],
+        w_t=w_t, wo_in=w_out, wu=w_up, wd=w_down, cos_in=jnp.cos(angles), sin_in=jnp.sin(angles), docs=doc_lengths,
     )
     small = (m, feat // m, D)
     quarter = (m, D // m, D)
     outs = dict(
-        out=((slots, 2, length, feat), BF16), ig=((slots, 2, length, feat), F32), res1=((2, *quarter), BF16),
-        res2=((2, *small), BF16), res3=((2, *small), BF16), gains=((8, feat), F32),
+        out=((slots, 2, feat, length), BF16), ig=((slots, 2, feat, length), F32), res1=((2, *quarter), BF16),
+        res2=((4, *small), BF16), gains=((8, feat), F32),
     )
     blocks = n + (slots - 1) * (n // 2 + max(1, n // 8))
     full, wide = (slots, 2, rows, half), (slots, rows, D)
@@ -1264,15 +1278,16 @@
         mrow=((8, rows), F32), lrow=((8, rows), F32), hp=(own_half, F32), iv=((slots, rows, 1), F32),
         n2=(wide, BF16), act=(wide, BF16), upre=(wide, BF16), ep=(wide, BF16), er=(part, BF16), ey=(part, BF16),
         eb=(part, BF16), fc=(halves, BF16), fy=(own_half, BF16),
-        osd=((slots, length, feat), BF16), gl=((2, D, D), BF16), gx1=(quarter, BF16), gz1=(quarter, BF16),
+        osd=((slots, feat, length), BF16), gl=((2, D, D), BF16), gx1=(quarter, BF16), gz1=(quarter, BF16),
         own1=(quarter[1:], BF16), do=((feat, rows), BF16), drow=((8, rows), F32),
         dkv=((slots, half, length), F32), dla=((blocks, half, length), BF16), qp=((slots, 3 * feat, rows), BF16),
         og=((feat, D), F32), qq=((feat, D), F32), qkv=((half, D), F32), gsum=((8, D), F32), gtwo=((8, D), F32),
         st=((slots, 2, 8, length), F32), sl=(stat, F32), sh=(stat, F32), sy=(stat, F32),
-        bey=(own_half, BF16), isd=((slots, length, feat), F32), src3=((2, feat, D), BF16),
+        bey=(own_half, BF16), isd=((slots, feat, length), F32), src3=((2, feat, D), BF16),
         gx2=(small, BF16), pt2=(small, BF16), gz2=(small, BF16), own2=(small[1:], BF16),
         gx3=(small, BF16), pt3=(small, BF16), gz3=(small, BF16), own3=(small[1:], BF16),
-        gh=((3, 8, D), F32), gq=((n, 8, feat), F32), gf=((8, feat), F32),
+        gb_in=((8, feat), F32), cos=((half_dim, rows), F32), sin=((half_dim, rows), F32),
+        bounds=((slots, 8, rows), jnp.int32), gh=((3, 8, D), F32), gq=((n, 8, feat), F32), gf=((8, feat), F32),
     )
     sems = {k: (3, slots) for k in ("ss", "sr", "ys", "yr", "fs", "fr")}
     sems |= {k: (3,) for k in ("gs", "gr", "ws", "wr", "hs", "hr")}
@@ -1292,7 +1307,7 @@
     got = pl.pallas_call(
         functools.partial(layer, n, names),
         out_shape=[jax.ShapeDtypeStruct(*v) for v in outs.values()],
-        in_specs=[vmem] * len(operands),
+        in_specs=[pl.BlockSpec(memory_space=pltpu.SMEM) if k == "docs" else vmem for k in operands],
         out_specs=[pl.BlockSpec(memory_space=pl.ANY) if k.startswith("res") else vmem for k in outs],
         scratch_shapes=list(scratch.values()),
         compiler_params=pltpu.CompilerParams(
@@ -1300,13 +1315,14 @@
         ),
         name="layer",
     )(*operands.values())
-    outputs, input_grad, res1, res2, res3, gain_grads = got
+    outputs, input_grad, res1, res2, gain_grads = got
     up_grad, down_grad = res1.reshape(2, D, D).astype(F32)
-    out_grad, q_grad = res2.reshape(2, feat, D).astype(F32)
-    qkv_grad = jnp.concatenate([q_grad[None], res3.reshape(2, feat, D).astype(F32)], axis=0)
+    small_grads = res2.reshape(4, feat, D)
+    out_grad = small_grads[0].astype(F32)
+    qkv_grad = small_grads[1:].astype(F32)
     return (
-        swap(outputs),
-        swap(input_grad),
+        jnp.swapaxes(swap(outputs), 2, 3),
+        jnp.swapaxes(swap(input_grad), 2, 3),
         jnp.transpose(qkv_grad, (2, 0, 1)),
         out_grad,
         up_grad,

time: 224 us -> 212 us (0.946)
  local copies, waits for them, and re-layouts: 16.8 us -> 9.77 us
  Pallas kernels: 197 us -> 191 us
    pallas_call x1, Pallas kernels: 197 us -> 191 us  [body(): pl.pallas_call(functools.partial(layer, n, names), out_shape=[jax.ShapeDt...]
    unnamed x18 -> x10, local copies, waits for them, and re-layouts: 5.75 us -> 0.5 us
    select_n x4 -> x1, other arithmetic: 3.87 us -> 1.31 us  [swap(): jnp.where(where == LONG_SLOT, pick, jnp.where(where == long, kept, v))]
    select_n x0 -> x2, local copies, waits for them, and re-layouts: none -> 2.32 us  [swap(): jnp.where(where == LONG_SLOT, pick, jnp.where(where == long, kept, v))]
where the time goes in v5:
time: 212 us
  Pallas kernels  191 us (90%)
  local copies, waits for them, and re-layouts  9.77 us (5%)
  other arithmetic  7.82 us (4%)
  between operations  2.67 us (1%)
    pallas_call x1, Pallas kernels, body(): pl.pallas_call(functools.partial(layer, n, names), out_shape=[jax.ShapeDt...  191 us
    another operation x1, local copies, waits for them, and re-layouts, body(): up_grad, down_grad = res1.reshape(2, D, D).astype(F32)  4.33 us

profile of v5, /device:TPU:0, one launch (start us, length us, event | category | flops | bytes accessed | tf_op | source)
XLA Modules:
  0.0 211.7 jit_solution(16215594348107730147)
XLA Ops:
  0.6 0.0 copy-start.2
  0.7 0.9 slice_reduce_fusion
  1.5 0.7 iota_reduce_fusion
  4.1 1.1 dynamic-slice_bitcast_fusion.2
  5.2 0.7 iota_compare_fusion
  5.8 0.0 copy-done.2
  5.9 1.3 select_select_fusion
  7.2 1.2 copy.21
  8.3 1.2 copy.22
  9.5 0.8 multiply_sine_fusion
  10.3 191.4 %layer.1 = (bf16[6,2,192,128]{3,2,1,0:T(8,128)(2,1)}, f32[6,2,192,128]{3,2,1,0:T(8,128)}, bf16[2,4,192,768]{3,2,1,0:T(8,128)(2,1)}, bf16[4,4,48,768]{3,2,1,0:T(8,128)(2,1)}, f32[8,192]{1,0:T(8,128)}) custom-call(bf16[6,256,192]{2,1,0:T(8,128)(2,1)} %bitcast.43, bf16[6,256,192]{2,1,0:T(8,128)(2,1)} %bitcast.44, f32[1,192]{1,0:T(1,128)} %bitcast.48, ...), custom_call_target="tpu_custom_call" | custom-call | tf_op jit(solution)/shard_map/layer/pallas_call | solution.py:1307
  201.7 0.0 copy-start.1
  201.7 4.3 %fusion = (f32[1,4,192,768]{3,2,1,0:T(8,128)}, f32[1,4,192,768]{3,2,1,0:T(8,128)}) fusion(bf16[2,4,192,768]{3,2,1,0:T(8,128)(2,1)} %get-tuple-element.20), kind=kLoop, calls=%fused_computation.22 | loop fusion | bytes 9437184 | tf_op jit(solution)/shard_map/unstack | solution.py:1319
  206.1 0.0 copy-done.1
  206.1 0.1 slice.42
  206.1 0.0 copy-start
  206.1 1.4 convert_bitcast_fusion
  207.5 0.2 copy-done
  207.7 1.2 select_bitcast_fusion
  208.9 0.0 copy-start.3
  209.0 0.0 copy-start.4
  209.0 0.9 bitcast_convert_fusion
  209.8 0.3 copy-done.3
  210.2 0.9 select_bitcast_fusion.1
  211.1 0.0 copy-done.4
  211.1 0.6 fusion.1
  (5 shorter events, 0.1 us)
Async XLA Ops:
  0.6 5.2 %copy-start.2 = (bf16[6,2,128,192]{2,3,1,0:T(8,128)(2,1)S(1)}, bf16[6,2,128,192]{2,3,1,0:T(8,128)(2,1)}, u32[]{:S(2)}) copy-start(bf16[6,2,128,192]{2,3,1,0:T(8,128)(2,1)} %param.21) | copy-start | bytes 1769476
  201.7 4.3 %copy-start.1 = (bf16[4,4,48,768]{3,2,1,0:T(8,128)(2,1)S(1)}, bf16[4,4,48,768]{3,2,1,0:T(8,128)(2,1)}, u32[]{:S(2)}) copy-start(bf16[4,4,48,768]{3,2,1,0:T(8,128)(2,1)} %get-tuple-element.19) | copy-start | bytes 3538948
  206.1 1.6 copy-start
  208.9 1.2 copy-start.3
  209.0 2.2 %copy-start.4 = (f32[8,192]{1,0:T(8,128)S(1)}, f32[8,192]{1,0:T(8,128)}, u32[]{:S(2)}) copy-start(f32[8,192]{1,0:T(8,128)} %get-tuple-element.21) | copy-start | bytes 18436

commit v6 on v5

--- a/solution.py
+++ b/solution.py
@@ -914,9 +914,18 @@
         r.gl[1, :, out_cols] = part
 
     e_on(slots - 1)
-    each(D // 256, up_tile)
-    each(D // 128, down_tile)
-    sum1.begin()
+    @pl.when(sum1.lo == 0)
+    def _():
+        each(D // 128, down_tile)
+        sum1.begin()
+        each(D // 256, up_tile)
+
+    @pl.when(sum1.lo == 1)
+    def _():
+        each(D // 256, up_tile)
+        sum1.begin()
+        each(D // 128, down_tile)
+
     e_total(0)
     e_total(1)
 
@@ -1255,7 +1264,7 @@
     angles = freqs[:, None] * positions.astype(F32)[None, :]
     w_t = w_qkv.reshape(D, 3 * feat).T
     operands = dict(
-        x_in=swap(inputs).reshape(slots, rows, feat), c_in=swap(cotangent).reshape(slots, rows, feat),
+        x_in=swap(inputs.reshape(slots, rows, feat)), c_in=swap(cotangent.reshape(slots, rows, feat)),
         ga=attn_gain[None], ba=attn_bias[None], gf_in=ffn_gain[None], bf_in=ffn_bias[None],
         w_t=w_t, wo_in=w_out, wu=w_up, wd=w_down, cos_in=jnp.cos(angles), sin_in=jnp.sin(angles), docs=doc_lengths,
     )

time: 212 us -> 210 us (level)
    select_n x2 -> x0, local copies, waits for them, and re-layouts: 2.32 us -> none  [swap(): jnp.where(where == LONG_SLOT, pick, jnp.where(where == long, kept, v))]
where the time goes in v6:
time: 210 us
  Pallas kernels  191 us (91%)
  local copies, waits for them, and re-layouts  8.27 us (4%)
  other arithmetic  8 us (4%)
  between operations  2.73 us (1%)
    pallas_call x1, Pallas kernels, body(): pl.pallas_call(functools.partial(layer, n, names), out_shape=[jax.ShapeDt...  191 us
    another operation x1, local copies, waits for them, and re-layouts, body(): up_grad, down_grad = res1.reshape(2, D, D).astype(F32)  4.33 us

profile of v6, /device:TPU:0, one launch (start us, length us, event | category | flops | bytes accessed | tf_op | source)
XLA Modules:
  0.0 209.9 jit_solution(7713199391244629755)
XLA Ops:
  0.6 0.0 copy-start.3
  0.7 0.9 slice_reduce_fusion
  1.5 0.7 iota_reduce_fusion
  4.1 1.3 copy.23
  5.5 0.0 slice-start
  5.5 0.0 copy-done.3
  5.5 0.0 slice-start.1
  5.5 0.3 copy.26
  5.8 0.7 iota_compare_fusion
  6.5 0.0 slice-done
  6.5 0.1 copy.29
  6.6 0.0 slice-done.1
  6.6 0.1 copy.30
  6.7 1.5 select_select_fusion
  8.2 0.8 multiply_sine_fusion
  9.0 190.9 %layer.1 = (bf16[6,2,192,128]{3,2,1,0:T(8,128)(2,1)}, f32[6,2,192,128]{3,2,1,0:T(8,128)}, bf16[2,4,192,768]{3,2,1,0:T(8,128)(2,1)}, bf16[4,4,48,768]{3,2,1,0:T(8,128)(2,1)}, f32[8,192]{1,0:T(8,128)}) custom-call(bf16[6,256,192]{2,1,0:T(8,128)(2,1)} %get-tuple-element.35.refs_0_, bf16[6,256,192]{2,1,0:T(8,128)(2,1)} %get-tuple-element.34.refs_1_, ...), custom_call_target="tpu_custom_call" | custom-call | tf_op jit(solution)/shard_map/layer/pallas_call | solution.py:1316
  199.9 0.0 copy-start.1
  199.9 4.3 %fusion = (f32[1,4,192,768]{3,2,1,0:T(8,128)}, f32[1,4,192,768]{3,2,1,0:T(8,128)}) fusion(bf16[2,4,192,768]{3,2,1,0:T(8,128)(2,1)} %get-tuple-element.20), kind=kLoop, calls=%fused_computation.20 | loop fusion | bytes 9437184 | tf_op jit(solution)/shard_map/unstack | solution.py:1328
  204.3 0.0 copy-done.1
  204.3 0.1 slice.44
  204.3 0.0 copy-start
  204.3 1.4 convert_bitcast_fusion
  205.7 0.2 copy-done
  205.9 1.2 select_bitcast_fusion
  207.1 0.0 copy-start.2
  207.2 0.0 copy-start.4
  207.2 0.9 bitcast_convert_fusion
  208.0 0.3 copy-done.2
  208.4 0.9 select_bitcast_fusion.1
  209.3 0.0 copy-done.4
  209.3 0.6 fusion.1
  (6 shorter events, 0.1 us)
Async XLA Ops:
  0.6 4.8 %copy-start.3 = (bf16[6,2,128,192]{2,3,1,0:T(8,128)(2,1)S(1)}, bf16[6,2,128,192]{2,3,1,0:T(8,128)(2,1)}, u32[]{:S(2)}) copy-start(bf16[6,2,128,192]{2,3,1,0:T(8,128)(2,1)} %param.21) | copy-start | bytes 1769476
  5.5 1.0 slice-start
  5.5 1.1 slice-start.1
  199.9 4.3 %copy-start.1 = (bf16[4,4,48,768]{3,2,1,0:T(8,128)(2,1)S(1)}, bf16[4,4,48,768]{3,2,1,0:T(8,128)(2,1)}, u32[]{:S(2)}) copy-start(bf16[4,4,48,768]{3,2,1,0:T(8,128)(2,1)} %get-tuple-element.19) | copy-start | bytes 3538948
  204.3 1.6 copy-start
  207.1 1.2 copy-start.2
  207.2 2.2 %copy-start.4 = (f32[8,192]{1,0:T(8,128)S(1)}, f32[8,192]{1,0:T(8,128)}, u32[]{:S(2)}) copy-start(f32[8,192]{1,0:T(8,128)} %get-tuple-element.21) | copy-start | bytes 18436

commit v7 on v6

--- a/solution.py
+++ b/solution.py
@@ -887,7 +887,8 @@
 
         @pl.when(t == slots)
         def _():
-            each(slots - 2, e_on)
+            e_on(LONG_SLOT)
+            each(LONG_SLOT, e_on)
 
         @pl.when(t == slots + 1)
         def _():
@@ -913,6 +914,9 @@
         part = dot(left, r.cg[:, lax.div(i, 3), :, cols].reshape(wide, 128), 0, 0).astype(BF16)
         r.gl[1, :, out_cols] = part
 
+    def long_first(t):
+        return jnp.where(t == 0, LONG_SLOT, jnp.where(t <= LONG_SLOT, t - 1, t))
+
     e_on(slots - 1)
     @pl.when(sum1.lo == 0)
     def _():
@@ -926,8 +930,8 @@
         sum1.begin()
         each(D // 128, down_tile)
 
-    e_total(0)
-    e_total(1)
+    e_total(long_first(0))
+    e_total(long_first(1))
 
     def two_back(s):
         e_back(s).wait_recv()
@@ -1043,9 +1047,9 @@
             two_back(s)
             attend_back(s)
 
-        stage(t, 1, f_on)
-        stage(t, -2, e_total)
-        stage(t, 0, run)
+        stage(t, 1, lambda s: f_on(long_first(s)))
+        stage(t, -2, lambda s: e_total(long_first(s)))
+        stage(t, 0, lambda s: run(long_first(s)))
 
         @pl.when(jnp.logical_or(t == 3, t == 5))
         def _():
@@ -1244,7 +1248,7 @@
     slots, _, length, feat = inputs.shape
     rows, half, m = 2 * length, 2 * feat, n // 2
     held = slots * n * half * length * 2
-    if held > ROWS_LIMIT or m != 4:
+    if held > ROWS_LIMIT or n != 8:
         return gathered_body(
             inputs, doc_lengths, attn_gain, attn_bias, w_qkv, w_out, ffn_gain, ffn_bias, w_up, w_down, cotangent
         )
@@ -1303,7 +1307,7 @@
     sems |= {k: (slots, n) for k in ("ks", "kr", "ds", "dr")}
     sems |= {k + i + e: (slots,) for k in "efab" for i in "123" for e in "sr" if k + i != "b3"}
     sems |= {"qs": (n,), "qr": (n,)}
-    pieces = {"u": 2, "v": 1, "w": 1}
+    pieces = {"u": 4, "v": 1, "w": 1}
     sems |= {"%s%d" % (k, i): (m,) for k in "uvw" for i in range(4)}
     sems |= {"%s%d" % (k, i): (m, pieces[k]) for k in "uvw" for i in range(4, 8)}
     sems |= {k + "9": (pieces[k],) for k in "uvw"}

time: 210 us -> 210 us (level)
  no operation moved by 1% of the time
where the time goes in v7:
time: 210 us
  Pallas kernels  191 us (91%)
  local copies, waits for them, and re-layouts  8.27 us (4%)
  other arithmetic  8 us (4%)
  between operations  2.73 us (1%)
    pallas_call x1, Pallas kernels, body(): pl.pallas_call(functools.partial(layer, n, names), out_shape=[jax.ShapeDt...  191 us
    another operation x1, local copies, waits for them, and re-layouts, body(): up_grad, down_grad = res1.reshape(2, D, D).astype(F32)  4.33 us

profile of v7, /device:TPU:0, one launch (start us, length us, event | category | flops | bytes accessed | tf_op | source)
XLA Modules:
  0.0 209.8 jit_solution(3930971394627990268)
XLA Ops:
  0.6 0.0 copy-start.3
  0.7 0.9 slice_reduce_fusion
  1.5 0.7 iota_reduce_fusion
  4.1 1.3 copy.23
  5.5 0.0 slice-start
  5.5 0.0 copy-done.3
  5.5 0.0 slice-start.1
  5.5 0.3 copy.26
  5.8 0.7 iota_compare_fusion
  6.5 0.0 slice-done
  6.5 0.1 copy.29
  6.6 0.0 slice-done.1
  6.6 0.1 copy.30
  6.7 1.5 select_select_fusion
  8.2 0.8 multiply_sine_fusion
  9.0 190.9 %layer.1 = (bf16[6,2,192,128]{3,2,1,0:T(8,128)(2,1)}, f32[6,2,192,128]{3,2,1,0:T(8,128)}, bf16[2,4,192,768]{3,2,1,0:T(8,128)(2,1)}, bf16[4,4,48,768]{3,2,1,0:T(8,128)(2,1)}, f32[8,192]{1,0:T(8,128)}) custom-call(bf16[6,256,192]{2,1,0:T(8,128)(2,1)} %get-tuple-element.35.refs_0_, bf16[6,256,192]{2,1,0:T(8,128)(2,1)} %get-tuple-element.34.refs_1_, ...), custom_call_target="tpu_custom_call" | custom-call | tf_op jit(solution)/shard_map/layer/pallas_call | solution.py:1320
  199.9 0.0 copy-start.1
  199.9 4.3 %fusion = (f32[1,4,192,768]{3,2,1,0:T(8,128)}, f32[1,4,192,768]{3,2,1,0:T(8,128)}) fusion(bf16[2,4,192,768]{3,2,1,0:T(8,128)(2,1)} %get-tuple-element.20), kind=kLoop, calls=%fused_computation.20 | loop fusion | bytes 9437184 | tf_op jit(solution)/shard_map/unstack | solution.py:1332
  204.2 0.0 copy-done.1
  204.2 0.1 slice.44
  204.3 0.0 copy-start
  204.3 1.4 convert_bitcast_fusion
  205.7 0.2 copy-done
  205.9 1.2 select_bitcast_fusion
  207.1 0.0 copy-start.2
  207.1 0.0 copy-start.4
  207.1 0.9 bitcast_convert_fusion
  208.0 0.3 copy-done.2
  208.3 0.9 select_bitcast_fusion.1
  209.3 0.0 copy-done.4
  209.3 0.6 fusion.1
  (6 shorter events, 0.1 us)
Async XLA Ops:
  0.6 4.8 %copy-start.3 = (bf16[6,2,128,192]{2,3,1,0:T(8,128)(2,1)S(1)}, bf16[6,2,128,192]{2,3,1,0:T(8,128)(2,1)}, u32[]{:S(2)}) copy-start(bf16[6,2,128,192]{2,3,1,0:T(8,128)(2,1)} %param.21) | copy-start | bytes 1769476
  5.5 1.0 slice-start
  5.5 1.1 slice-start.1
  199.9 4.3 %copy-start.1 = (bf16[4,4,48,768]{3,2,1,0:T(8,128)(2,1)S(1)}, bf16[4,4,48,768]{3,2,1,0:T(8,128)(2,1)}, u32[]{:S(2)}) copy-start(bf16[4,4,48,768]{3,2,1,0:T(8,128)(2,1)} %get-tuple-element.19) | copy-start | bytes 3538948
  204.3 1.6 copy-start
  207.1 1.2 copy-start.2
  207.1 2.2 %copy-start.4 = (f32[8,192]{1,0:T(8,128)S(1)}, f32[8,192]{1,0:T(8,128)}, u32[]{:S(2)}) copy-start(f32[8,192]{1,0:T(8,128)} %get-tuple-element.21) | copy-start | bytes 18436
